TPU v7x, 32 devices: a whole 2x2x4 slice. The times are simulated.
32 devices in a mesh: groups: 1, tensor: 32 (over z, y, x, core).
Axes of the slice: x: 2, y: 2, z: 4, core: 2. Of those that a mesh axis runs over, the one named last changes fastest.
Arguments:
- hidden: bfloat16 [24, 8192], P('groups', 'tensor'), may hold values from -10 to 10
- w_qkv: bfloat16 [8192, 5120], P('tensor'), may hold values from -0.0625 to 0.0625
- key_cache: bfloat16 [24, 8192, 512], P('groups', 'tensor'), may hold values from -6 to 6
- value_cache: bfloat16 [24, 8192, 512], P('groups', 'tensor'), may hold values from -24 to 24
- lengths: int32 [24], P('groups'), may hold values from 1024 to 8192
- w_out: bfloat16 [4096, 8192], P(None, 'tensor'), may hold values from -0.25 to 0.25
- w_gate: bfloat16 [8192, 14336], P(None, 'tensor'), may hold values from -0.0625 to 0.0625
- w_up: bfloat16 [8192, 14336], P(None, 'tensor'), may hold values from -0.0625 to 0.0625
- w_down: bfloat16 [14336, 8192], P('tensor'), may hold values from -0.09375 to 0.09375
Outputs:
- output: bfloat16 [24, 8192], P('groups', 'tensor')
All inputs are finite; a program needn't handle non-finite values.
Results may differ from a plain program's by a relative error of at most 0.009.
Values may be sent and summed in bfloat16 or wider, within the bound.
No kernel may reach another device: no remote copies, remote signals or barrier semaphores. Data moves between devices by JAX's collectives and lax.ppermute only.
A program may use at most 128 MiB of HBM per device.

v0:
```python
import jax
import jax.numpy as jnp
import numpy as np
from jax import lax
from jax.sharding import PartitionSpec as P

D = 8192
FF = 14336
H = 32
KVH = 4
HD = 128


EPSILON = 1e-05
ROPE_BASE = 500000.0


def partner_2(value, axis, apart):
    mask = 2**apart
    pairs = [(source, source ^ mask) for source in range(lax.axis_size(axis))]
    return lax.ppermute(value, axis, pairs)


def paley_table():
    prime = 13
    residues = [value * value % prime for value in range(1, prime)]
    conference = np.zeros((prime + 1, prime + 1))
    conference[0, 1:] = 1.0
    conference[1:, 0] = 1.0
    for row_number in range(prime):
        for col_number in range(prime):
            offset = (col_number - row_number) % prime
            if offset != 0:
                conference[row_number + 1, col_number + 1] = 1.0 if offset in residues else -1.0
    first_block = np.array([[1.0, -1.0], [-1.0, -1.0]])
    second_block = np.array([[1.0, 1.0], [1.0, -1.0]])
    return np.kron(conference, first_block) + np.kron(np.eye(prime + 1), second_block)


def sylvester_table(order):
    result = np.ones((1, 1))
    while result.shape[0] < order:
        result = np.kron(np.array([[1.0, 1.0], [1.0, -1.0]]), result)
    return result


def rotary(values, positions):
    half_width = values.shape[-1] // 2
    frequency = ROPE_BASE ** (-2.0 * jnp.arange(half_width, dtype=jnp.float32) / values.shape[-1])
    angles = positions.astype(jnp.float32)[:, None, None] * frequency[None, None, :]
    cosine = jnp.cos(angles)
    sine = jnp.sin(angles)
    front = values[..., :half_width]
    back = values[..., half_width:]
    return jnp.concatenate([front * cosine - back * sine, back * cosine + front * sine], axis=-1)


def per_device(hidden, w_qkv, key_cache, value_cache, lengths, w_out, w_gate, w_up, w_down):
    row_count = hidden.shape[0]
    devices = lax.axis_size("tensor")
    device_index = lax.axis_index("tensor")
    query_width = H * HD
    kv_width = KVH * HD
    group_size = H // KVH
    score_scale = HD ** (-0.5)
    hidden_wide = hidden.astype(jnp.float32)
    squares = jnp.sum(hidden_wide * hidden_wide, axis=1)
    partial_sums = jnp.dot(hidden, w_qkv, preferred_element_type=jnp.float32)
    squares_all, projected = lax.psum((squares, partial_sums), "tensor")
    inverse = lax.rsqrt(squares_all / D + EPSILON)
    qkv = (projected * inverse[:, None]).astype(jnp.bfloat16)
    queries = rotary(
        qkv[:, :query_width].astype(jnp.float32).reshape(row_count, H, HD), lengths
    ).astype(jnp.bfloat16)
    keys_new = rotary(
        qkv[:, query_width : query_width + kv_width]
        .astype(jnp.float32)
        .reshape(row_count, KVH, HD),
        lengths,
    ).astype(jnp.bfloat16)
    values_new = qkv[:, query_width + kv_width :].reshape(row_count, KVH, HD)
    grouped = queries.reshape(row_count, KVH, group_size, HD)
    local_length = key_cache.shape[1]
    positions = device_index * local_length + jnp.arange(local_length)
    live_mask = positions[None, :] < lengths[:, None]
    keys_local = key_cache.reshape(row_count, local_length, KVH, HD)
    values_local = value_cache.reshape(row_count, local_length, KVH, HD)
    scores = (
        jnp.einsum("rkgd,rckd->rkgc", grouped, keys_local, preferred_element_type=jnp.float32)
        * score_scale
    )
    weights = jnp.where(live_mask[:, None, None, :], jnp.exp(scores), jnp.float32(0.0))
    totals_local = jnp.sum(weights, axis=3)
    summed_local = jnp.einsum(
        "rkgc,rckd->rkgd",
        weights.astype(jnp.bfloat16),
        values_local,
        preferred_element_type=jnp.float32,
    )
    totals, summed = lax.psum((totals_local, summed_local), "tensor")
    own_scores = (
        jnp.einsum("rkgd,rkd->rkg", grouped, keys_new, preferred_element_type=jnp.float32)
        * score_scale
    )
    own_weights = jnp.exp(own_scores)
    totals = totals + own_weights
    summed = summed + own_weights[..., None] * values_new.astype(jnp.float32)[:, :, None, :]
    attention = (summed / totals[..., None]).reshape(row_count, query_width).astype(jnp.bfloat16)
    residual = (hidden_wide + jnp.dot(attention, w_out, preferred_element_type=jnp.float32)).astype(
        jnp.bfloat16
    )
    residual_full = lax.all_gather(residual, "tensor", axis=1, tiled=True)
    residual_wide = residual_full.astype(jnp.float32)
    normed = (
        residual_wide
        * lax.rsqrt(jnp.mean(residual_wide * residual_wide, axis=1, keepdims=True) + EPSILON)
    ).astype(jnp.bfloat16)
    gate = jnp.dot(normed, w_gate, preferred_element_type=jnp.float32)
    upward = jnp.dot(normed, w_up, preferred_element_type=jnp.float32)
    activation = jax.nn.silu(gate) * upward
    local_width = activation.shape[1]
    local_table = jnp.asarray(
        np.kron(sylvester_table(local_width // 28), paley_table()), dtype=jnp.float32
    )
    mixed = jnp.dot(activation, local_table, precision=lax.Precision.HIGHEST)
    for bit_number in range(devices.bit_length() - 1):
        partner = partner_2(mixed, "tensor", bit_number)
        upper_half = device_index // 2**bit_number % 2
        mixed = jnp.where(upper_half == 1, partner - mixed, mixed + partner)
    rotated = (mixed * FF ** (-0.5)).astype(jnp.bfloat16)
    down_share = lax.psum_scatter(
        lax.dot_general(
            w_down, rotated, (((0,), (1,)), ((), ())), preferred_element_type=jnp.float32
        ),
        "tensor",
        scatter_dimension=0,
        tiled=True,
    )
    return (residual.astype(jnp.float32) + down_share.T).astype(jnp.bfloat16)


def solution(mesh):
    in_specs = (
        P("groups", "tensor"),
        P("tensor", None),
        P("groups", "tensor", None),
        P("groups", "tensor", None),
        P("groups"),
        P(None, "tensor"),
        P(None, "tensor"),
        P(None, "tensor"),
        P("tensor", None),
    )
    out_specs = P("groups", "tensor")
    return jax.shard_map(
        per_device, mesh=mesh, in_specs=in_specs, out_specs=out_specs, check_vma=False
    )
```

profile of v0, /device:TPU:0, one launch (start us, length us, event | category | flops | bytes accessed | tf_op | source)
XLA Modules:
  0.0 539.0 jit_solution(6456057145155909253)
XLA Ops:
  6.5 0.0 copy-start
  6.5 0.0 all-reduce.3.cloned.1.call-start
  6.5 1.7 copy-done
  8.3 2.0 fusion.37
  10.2 0.0 all-reduce.3.cloned.1.call-update
  10.3 0.0 all-reduce.5.cloned.1.call-start
  10.3 0.8 fusion.28
  11.1 42.1 %psum.29 = f32[24]{0:T(128)S(1)} all-reduce(f32[24]{0:T(128)S(1)} %fusion.28), channel_id=1, replica_groups=mesh['groups'=1,'tensor'=32] {'tensor'}, use_global_device_ids=true, to_apply=%region_2.0 | all-reduce | flops 24 | bytes 192 | tf_op jit(solution)/shard_map/psum | solution.py:69
  53.2 0.7 broadcast_compare_fusion
  54.0 0.7 convert_element_type.54
  54.6 0.1 multiply_cosine_fusion
  54.7 87.3 %all-reduce.3.cloned.1.call-done = f32[24,5120]{1,0:T(8,128)} async-done(((f32[24,5120]{1,0:T(8,128)}), f32[24,5120]{1,0:T(8,128)}) %all-reduce.3.cloned.1.call-update) | async-done | bytes 491536 | tf_op jit(solution)/shard_map/psum | solution.py:69
  142.0 1.1 multiply_convert_fusion
  143.2 0.1 copy.17
  143.3 0.1 subtract_convert_fusion.1
  143.4 0.2 fusion.19
  143.6 0.1 maximum_bitcast_fusion
  143.7 0.3 fusion.26
  144.0 0.0 copy-start.2
  144.0 4.7 fusion.36
  148.7 40.8 %psum.31 = f32[24,4,8]{2,1,0:T(4,128)S(1)} all-reduce(f32[24,4,8]{2,1,0:T(4,128)S(1)} %get-tuple-element.15), channel_id=1, replica_groups=mesh['groups'=1,'tensor'=32] {'tensor'}, use_global_device_ids=true, to_apply=%region_5.6 | all-reduce | flops 768 | bytes 6144 | tf_op jit(solution)/shard_map/psum | solution.py:100
  189.5 4.5 fusion
  194.0 0.0 all-reduce.5.cloned.1.call-update
  194.0 0.0 reduce-scatter.2.cloned.1.call-start
  194.1 127.4 %all-reduce.5.cloned.1.call-done = f32[24,4,8,128]{3,2,1,0:T(8,128)} async-done(((f32[24,4,8,128]{3,2,1,0:T(8,128)}), f32[24,4,8,128]{3,2,1,0:T(8,128)}) %all-reduce.5.cloned.1.call-update) | async-done | bytes 393232 | tf_op jit(solution)/shard_map/psum | solution.py:100
  321.5 1.3 divide_convert_fusion
  322.8 0.0 copy-done.2
  322.8 2.0 fusion.15
  324.8 40.7 %all_gather.3 = bf16[24,8192]{1,0:T(8,128)(2,1)S(1)} all-gather(bf16[24,256]{1,0:T(8,128)(2,1)S(1)} %fusion.15), channel_id=1, replica_groups=mesh['groups'=1,'tensor'=32] {'tensor'}, dimensions={1}, use_global_device_ids=true | all-gather | bytes 405504 | tf_op jit(solution)/shard_map/all_gather | solution.py:112
  365.5 0.2 fusion.16
  365.7 0.0 copy-start.1
  365.7 5.2 fusion.24
  370.9 5.1 convolution_multiply_fusion
  376.1 0.0 copy-done.1
  376.1 0.6 fusion.38
  376.6 0.4 collective-permute-start
  377.0 0.9 collective-permute-done
  377.9 0.1 collective-permute-start.1
  378.0 4.0 collective-permute-done.1
  382.1 0.1 collective-permute-start.2
  382.2 4.0 collective-permute-done.2
  386.2 0.1 collective-permute-start.3
  386.4 4.0 collective-permute-done.3
  390.4 0.1 collective-permute-start.4
  390.5 5.2 collective-permute-done.4
  395.7 5.0 convolution_bitcast_fusion
  400.7 0.0 reduce-scatter.2.cloned.1.call-update
  400.7 130.4 %reduce-scatter.2.cloned.1.call-done = f32[256,24]{0,1:T(8,128)} async-done(((f32[8192,24]{0,1:T(8,128)}), f32[256,24]{0,1:T(8,128)}) %reduce-scatter.2.cloned.1.call-update) | async-done | bytes 24592 | tf_op jit(solution)/shard_map/reduce_scatter | solution.py:131
  531.1 1.3 fusion.29
  (13 shorter events, 0.2 us)
Async XLA Ops:
  6.5 1.7 copy-start
  6.5 135.5 %all-reduce.3.cloned.1.call-start = ((), (), s32[]{:S(2)}) async-start(), calls=%async_computation.1 | async-start | bytes 983040 | tf_op jit(solution)/shard_map/psum | solution.py:69
  10.3 311.3 %all-reduce.5.cloned.1.call-start = ((), (), s32[]{:S(2)}) async-start(), calls=%async_computation.2 | async-start | bytes 786432 | tf_op jit(solution)/shard_map/psum | solution.py:100
  144.0 178.8 %copy-start.2 = (bf16[24,256]{1,0:T(8,128)(2,1)S(1)}, bf16[24,256]{1,0:T(8,128)(2,1)}, u32[]{:S(2)}) copy-start(bf16[24,256]{1,0:T(8,128)(2,1)} %param.10) | copy-start | bytes 36868
  194.0 337.1 %reduce-scatter.2.cloned.1.call-start = ((), (), s32[]{:S(2)}) async-start(), calls=%async_computation.3 | async-start | bytes 811008 | tf_op jit(solution)/shard_map/reduce_scatter | solution.py:131
  365.7 10.3 %copy-start.1 = (f32[448,448]{1,0:T(8,128)S(1)}, f32[448,448]{1,0:T(8,128)}, u32[]{:S(2)}) copy-start(f32[448,448]{1,0:T(8,128)} %constant.113.clone) | copy-start | bytes 2408452
  376.6 1.3 collective-permute-start
  377.9 4.2 collective-permute-start.1
  382.1 4.2 collective-permute-start.2
  386.2 4.2 collective-permute-start.3
  390.4 5.3 collective-permute-start.4
Sparse Core Ops, SparseCore 0:
  12.6 129.3 all-reduce.2
  194.1 127.3 all-reduce.4
  400.9 130.1 reduce-scatter.1
where the time goes:
time: 540 us; the launch traced here: 539 us
  waiting for transfers between devices  363 us (67%)
  blocking collectives  124 us (23%)
  matrix products  29.3 us (5%)
  between operations  13.4 us (2%)
  other arithmetic  6.79 us (1%)
    reduce_scatter x1, waiting for transfers between devices, per_device(): lax.psum_scatter(lax.dot_general(w_down, rotated, (((0,), (1,)), ((), ())...  130 us
    psum x1, waiting for transfers between devices, per_device(): totals, summed = lax.psum((totals_local, summed_local), 'tensor')  127 us
    psum x1, waiting for transfers between devices, per_device(): squares_all, projected = lax.psum((squares, partial_sums), 'tensor')  87.3 us
    psum x1, blocking collectives, per_device(): squares_all, projected = lax.psum((squares, partial_sums), 'tensor')  42.1 us
    psum x1, blocking collectives, per_device(): totals, summed = lax.psum((totals_local, summed_local), 'tensor')  40.8 us
    all_gather x1, blocking collectives, per_device(): residual_full = lax.all_gather(residual, 'tensor', axis=1, tiled=True)  40.7 us
    ppermute x5, waiting for transfers between devices, partner_2(): return lax.ppermute(value, axis, pairs)  18.2 us
  transfers between devices with their start and end apart: 8, of which 8 were waited for; matrix products, arithmetic and copies ran while one was open for 0% of the time, Pallas kernels for 0%

commit v1 on v0

v1 whole, which is shorter than its diff:
```python
import jax
import jax.numpy as jnp
import numpy as np
from jax import lax
from jax.sharding import PartitionSpec as P

D = 8192
FF = 14336
H = 32
KVH = 4
HD = 128


EPSILON = 1e-05
ROPE_BASE = 500000.0


def scattered_sum(pieces):
    received = lax.all_to_all(pieces, "tensor", 0, 0, tiled=True)
    return jnp.sum(received.astype(jnp.float32), axis=0)


def gathered(piece):
    copies = jnp.broadcast_to(piece[None], (lax.axis_size("tensor"), *piece.shape))
    return lax.all_to_all(copies, "tensor", 0, 0, tiled=True)


def paley_table():
    prime = 13
    residues = [value * value % prime for value in range(1, prime)]
    conference = np.zeros((prime + 1, prime + 1))
    conference[0, 1:] = 1.0
    conference[1:, 0] = 1.0
    for row_number in range(prime):
        for col_number in range(prime):
            offset = (col_number - row_number) % prime
            if offset != 0:
                conference[row_number + 1, col_number + 1] = 1.0 if offset in residues else -1.0
    first_block = np.array([[1.0, -1.0], [-1.0, -1.0]])
    second_block = np.array([[1.0, 1.0], [1.0, -1.0]])
    return np.kron(conference, first_block) + np.kron(np.eye(prime + 1), second_block)


def sylvester_table(order):
    result = np.ones((1, 1))
    while result.shape[0] < order:
        result = np.kron(np.array([[1.0, 1.0], [1.0, -1.0]]), result)
    return result


def rotary(values, positions):
    half_width = values.shape[-1] // 2
    frequency = ROPE_BASE ** (-2.0 * jnp.arange(half_width, dtype=jnp.float32) / values.shape[-1])
    angles = positions.astype(jnp.float32)[:, None] * frequency[None, :]
    cosine = jnp.cos(angles)
    sine = jnp.sin(angles)
    front = values[..., :half_width]
    back = values[..., half_width:]
    return jnp.concatenate([front * cosine - back * sine, back * cosine + front * sine], axis=-1)


def per_device(hidden, w_qkv, key_cache, value_cache, lengths, w_out, w_gate, w_up, w_down):
    row_count = hidden.shape[0]
    devices = lax.axis_size("tensor")
    device_index = lax.axis_index("tensor")
    query_width = H * HD
    kv_width = KVH * HD
    group_size = H // KVH
    score_scale = HD ** (-0.5)
    hidden_wide = hidden.astype(jnp.float32)
    squares = jnp.sum(hidden_wide * hidden_wide, axis=1)
    partial_sums = jnp.dot(hidden, w_qkv, preferred_element_type=jnp.float32)
    blocks = H + 2 * KVH
    rows_used = (blocks + 1) * row_count
    rows_sent = -(-rows_used // (8 * devices)) * 8
    stacked = jnp.concatenate(
        [
            partial_sums.reshape(row_count, blocks, HD).transpose(1, 0, 2).reshape(-1, HD),
            jnp.broadcast_to(squares[:, None], (row_count, HD)),
            jnp.zeros((rows_sent * devices - rows_used, HD), jnp.float32),
        ]
    ).astype(jnp.bfloat16)
    projected = gathered(scattered_sum(stacked.reshape(devices, rows_sent, HD)).astype(jnp.bfloat16))
    projected = projected.reshape(-1, HD)[:rows_used].astype(jnp.float32)
    projected = projected.reshape(blocks + 1, row_count, HD)
    inverse = lax.rsqrt(projected[blocks] / D + EPSILON)
    qkv = (projected[:blocks] * inverse).astype(jnp.bfloat16)
    turned = rotary(qkv[: H + KVH].astype(jnp.float32), lengths).astype(jnp.bfloat16)
    grouped = turned[:H].reshape(KVH, group_size, row_count, HD)
    keys_new = turned[H:]
    values_new = qkv[H + KVH :]
    local_length = key_cache.shape[1]
    positions = device_index * local_length + jnp.arange(local_length)
    live_mask = positions[None, :] < lengths[:, None]
    keys_local = key_cache.reshape(row_count, local_length, KVH, HD)
    values_local = value_cache.reshape(row_count, local_length, KVH, HD)
    scores = (
        jnp.einsum("kgrd,rckd->rkgc", grouped, keys_local, preferred_element_type=jnp.float32)
        * score_scale
    )
    weights = jnp.where(live_mask[:, None, None, :], jnp.exp(scores), jnp.float32(0.0))
    totals = jnp.sum(weights, axis=3)
    summed = jnp.einsum(
        "rkgc,rckd->rkgd",
        weights.astype(jnp.bfloat16),
        values_local,
        preferred_element_type=jnp.float32,
    )
    own_scores = (
        jnp.einsum("kgrd,krd->rkg", grouped, keys_new, preferred_element_type=jnp.float32)
        * score_scale
    )
    own_weights = jnp.where(device_index == 0, jnp.exp(own_scores), jnp.float32(0.0))
    totals = totals + own_weights
    summed = summed + own_weights[..., None] * values_new.astype(jnp.float32).transpose(1, 0, 2)[:, :, None, :]
    held = H * row_count // devices
    numerators = summed.transpose(1, 2, 0, 3).reshape(devices, held, HD)
    totals = totals.transpose(1, 2, 0).reshape(devices, 1, held)
    totals = jnp.pad(totals, ((0, 0), (0, 0), (0, HD - held)))
    parts = scattered_sum(jnp.concatenate([numerators, totals], axis=1).astype(jnp.bfloat16))
    piece = (parts[:held] / parts[held, :held][:, None]).astype(jnp.bfloat16)
    attention = gathered(piece).reshape(H, row_count, HD).transpose(1, 0, 2).reshape(row_count, query_width)
    residual = (hidden_wide + jnp.dot(attention, w_out, preferred_element_type=jnp.float32)).astype(
        jnp.bfloat16
    )
    residual_full = gathered(residual).transpose(1, 0, 2).reshape(row_count, D)
    residual_wide = residual_full.astype(jnp.float32)
    normed = (
        residual_wide
        * lax.rsqrt(jnp.mean(residual_wide * residual_wide, axis=1, keepdims=True) + EPSILON)
    ).astype(jnp.bfloat16)
    gate = jnp.dot(normed, w_gate, preferred_element_type=jnp.float32)
    upward = jnp.dot(normed, w_up, preferred_element_type=jnp.float32)
    activation = jax.nn.silu(gate) * upward
    local_width = activation.shape[1]
    local_table = jnp.asarray(
        np.kron(sylvester_table(local_width // 28), paley_table()), dtype=jnp.float32
    )
    mixed = jnp.dot(activation, local_table, precision=lax.Precision.HIGHEST)
    share = mixed.astype(jnp.bfloat16).reshape(devices, -1)
    share = lax.all_to_all(share, "tensor", 0, 0, tiled=True)
    share = jnp.dot(jnp.asarray(sylvester_table(devices), dtype=jnp.bfloat16), share, preferred_element_type=jnp.float32)
    share = lax.all_to_all((share * FF ** (-0.5)).astype(jnp.bfloat16), "tensor", 0, 0, tiled=True)
    rotated = share.reshape(row_count, local_width)
    down = jnp.dot(rotated, w_down, preferred_element_type=jnp.float32).astype(jnp.bfloat16)
    down_share = scattered_sum(down.reshape(row_count, devices, -1).transpose(1, 0, 2))
    return (residual.astype(jnp.float32) + down_share).astype(jnp.bfloat16)


def solution(mesh):
    in_specs = (
        P("groups", "tensor"),
        P("tensor", None),
        P("groups", "tensor", None),
        P("groups", "tensor", None),
        P("groups"),
        P(None, "tensor"),
        P(None, "tensor"),
        P(None, "tensor"),
        P("tensor", None),
    )
    out_specs = P("groups", "tensor")
    return jax.shard_map(
        per_device, mesh=mesh, in_specs=in_specs, out_specs=out_specs, check_vma=False
    )
```

time: 540 us -> 133 us (0.25)
  waiting for transfers between devices: 363 us -> 19.6 us
  blocking collectives: 124 us -> 73.1 us
  between operations: 13.4 us -> 0.36 us
  matrix products: 29.3 us -> 19.1 us
  starting transfers between devices: 0.74 us -> 9.88 us
    psum x2 -> x0, waiting for transfers between devices: 215 us -> none  [the longest x1 127 us: per_device(): totals, summed = lax.psum((totals_local, summed_local), 'tensor')]
    reduce_scatter x1 -> x0, waiting for transfers between devices: 130 us -> none  [per_device(): lax.psum_scatter(lax.dot_general(w_down, rotated, (((0,), (1,)), ((), ())...]
    psum x2 -> x0, blocking collectives: 82.9 us -> none  [the longest x1 42.1 us: per_device(): squares_all, projected = lax.psum((squares, partial_sums), 'tensor')]
    all_to_all x0 -> x6, blocking collectives: none -> 73.1 us  [the longest x2 27.6 us: scattered_sum(): received = lax.all_to_all(pieces, 'tensor', 0, 0, tiled=True)]
    all_gather x1 -> x0, blocking collectives: 40.7 us -> none  [per_device(): residual_full = lax.all_gather(residual, 'tensor', axis=1, tiled=True)]
    all_to_all x0 -> x2, waiting for transfers between devices: none -> 19.6 us  [the longest x1 9.93 us: scattered_sum(): received = lax.all_to_all(pieces, 'tensor', 0, 0, tiled=True)]
    ppermute x5 -> x0, waiting for transfers between devices: 18.2 us -> none  [partner_2(): return lax.ppermute(value, axis, pairs)]
    all_to_all x0 -> x2, starting transfers between devices: none -> 9.88 us  [the longest x1 7.3 us: scattered_sum(): received = lax.all_to_all(pieces, 'tensor', 0, 0, tiled=True)]
  transfers between devices with their start and end apart: 8 -> 2, of which waited for: 8 -> 2; matrix products, arithmetic and copies ran while one was open for 0% -> 1% of each run, Pallas kernels for 0% -> 0%
where the time goes in v1:
time: 133 us; the launch traced here: 132 us
  blocking collectives  73.1 us (55%)
  waiting for transfers between devices  19.6 us (15%)
  matrix products  19.1 us (14%)
  starting transfers between devices  9.88 us (7%)
  other arithmetic  6.85 us (5%)
  local copies, waits for them, and re-layouts  3.31 us (2%)
    all_to_all x2, blocking collectives, scattered_sum(): received = lax.all_to_all(pieces, 'tensor', 0, 0, tiled=True)  27.6 us
    all_to_all x2, blocking collectives, gathered(): return lax.all_to_all(copies, 'tensor', 0, 0, tiled=True)  26.8 us
    all_to_all x1, waiting for transfers between devices, scattered_sum(): received = lax.all_to_all(pieces, 'tensor', 0, 0, tiled=True)  9.93 us
    all_to_all x1, waiting for transfers between devices, gathered(): return lax.all_to_all(copies, 'tensor', 0, 0, tiled=True)  9.72 us
    all_to_all x1, blocking collectives, per_device(): share = lax.all_to_all(share, 'tensor', 0, 0, tiled=True)  9.69 us
    all_to_all x1, blocking collectives, per_device(): lax.all_to_all((share * FF ** (-0.5)).astype(jnp.bfloat16), 'tensor', 0,...  8.95 us
    all_to_all x1, starting transfers between devices, scattered_sum(): received = lax.all_to_all(pieces, 'tensor', 0, 0, tiled=True)  7.3 us
    dot_general x1, matrix products, per_device(): jnp.einsum('kgrd,rckd->rkgc', grouped, keys_local, preferred_element_type...  4.62 us
  transfers between devices with their start and end apart: 2, of which 2 were waited for; matrix products, arithmetic and copies ran while one was open for 1% of the time, Pallas kernels for 0%

profile of v1, /device:TPU:0, one launch (start us, length us, event | category | flops | bytes accessed | tf_op | source)
XLA Modules:
  0.0 132.2 jit_solution(9649525811117234613)
XLA Ops:
  0.0 1.0 fusion.44
  1.0 0.1 pad.12.clone
  1.1 0.1 pad.11.clone
  1.1 0.6 copy-done
  1.8 1.2 fusion.24
  2.9 0.1 copy.130
  3.0 1.0 maximum_maximum_fusion
  4.0 7.3 %all-to-all-start = ((bf16[32,32,128]{2,1,0:T(8,128)(2,1)}), bf16[32,32,128]{2,1,0:T(8,128)(2,1)S(1)}, u32[]{:S(2)}, u32[]{:S(2)}) async-start(bf16[32,32,128]{2,1,0:T(8,128)(2,1)} %bitcast.2), calls=%async_computation | async-start | bytes 524288 | tf_op jit(solution)/shard_map/all_to_all | solution.py:19
  11.3 0.7 convert_element_type.83
  12.0 9.9 %all-to-all-done = bf16[32,32,128]{2,1,0:T(8,128)(2,1)S(1)} async-done(((bf16[32,32,128]{2,1,0:T(8,128)(2,1)}), bf16[32,32,128]{2,1,0:T(8,128)(2,1)S(1)}, u32[]{:S(2)}, u32[]{:S(2)}) %all-to-all-start) | async-done | bytes 262176 | tf_op jit(solution)/shard_map/all_to_all | solution.py:19
  21.9 0.1 reduce_sum.60
  22.0 0.7 broadcast_in_dim.29
  22.7 2.6 %all-to-all-start.1 = ((bf16[32,32,128]{2,1,0:T(8,128)(2,1)}), bf16[32,32,128]{2,1,0:T(8,128)(2,1)S(1)}, u32[]{:S(2)}, u32[]{:S(2)}) async-start(bf16[32,32,128]{2,1,0:T(8,128)(2,1)} %broadcast_in_dim.29), calls=%async_computation.1 | async-start | bytes 524288 | tf_op jit(solution)/shard_map/all_to_all | solution.py:25
  25.3 0.7 broadcast_compare_fusion
  26.0 0.1 multiply_cosine_fusion
  26.2 9.7 %all-to-all-done.1 = bf16[32,32,128]{2,1,0:T(8,128)(2,1)S(1)} async-done(((bf16[32,32,128]{2,1,0:T(8,128)(2,1)}), bf16[32,32,128]{2,1,0:T(8,128)(2,1)S(1)}, u32[]{:S(2)}, u32[]{:S(2)}) %all-to-all-start.1) | async-done | bytes 262176 | tf_op jit(solution)/shard_map/all_to_all | solution.py:25
  36.1 0.2 add_convert_fusion
  36.3 0.1 fusion.45
  36.4 0.1 fusion.35
  36.5 0.2 fusion.38
  36.8 0.1 copy.74
  36.8 4.6 %fusion.58 = (f32[24,4,8]{2,1,0:T(4,128)S(1)}, bf16[24,4,8,256]{3,2,1,0:T(8,128)(2,1)S(1)}) fusion(bf16[32,24,128]{2,1,0:T(8,128)(2,1)S(1)} %fusion.35, pred[24,256]{1,0:T(8,128)(4,1)S(1)} %broadcast_compare_fusion, bf16[24,256,512]{2,1,0:T(8,128)(2,1)} %param.13), kind=kOutput, calls=%fused_computation.80 | convolution fusion | flops 51117312 | bytes 6890496 | tf_op jit(solution)/shard_map/kgrd,rckd->rkgc/dot_general | solution.py:98
  41.5 0.0 copy-start.3
  41.5 0.1 copy.65
  41.6 0.1 copy.63
  41.7 0.0 slice-start
  41.7 0.0 slice-start.2
  41.7 3.9 %fusion.25 = bf16[32,24,128]{2,0,1:T(8,128)(2,1)S(1)} fusion(bf16[24,4,8,256]{3,2,1,0:T(8,128)(2,1)S(1)} %get-tuple-element.12, f32[4,24,128]{2,0,1:T(4,128)S(1)} %copy.64, f32[4,8,24]{1,0,2:T(4,128)S(1)} %copy.63, bf16[24,256,512]{2,1,0:T(8,128)(2,1)} %param.14), kind=kOutput, calls=%fused_computation.15 | convolution fusion | flops 50626560 | bytes 6933504 | tf_op jit(solution)/shard_map/rkgc,rckd->rkgd/dot_general | solution.py:103
  45.6 0.1 copy.66
  45.7 0.0 slice-start.1
  45.7 12.7 %all_to_all.52 = bf16[32,25,128]{2,1,0:T(8,128)(2,1)S(1)} all-to-all(bf16[32,25,128]{2,1,0:T(8,128)(2,1)S(1)} %fusion.34), channel_id=1, replica_groups=mesh['groups'=1,'tensor'=32] {'tensor'}, dimensions={0} | all-to-all | bytes 409600 | tf_op jit(solution)/shard_map/all_to_all | solution.py:19
  58.5 0.1 convert_reduce_fusion.1
  58.5 0.1 fusion.52
  58.6 11.1 %all_to_all.53 = bf16[32,24,128]{2,1,0:T(8,128)(2,1)S(1)} all-to-all(bf16[32,24,128]{2,1,0:T(8,128)(2,1)S(1)} %broadcast_in_dim.32), channel_id=1, replica_groups=mesh['groups'=1,'tensor'=32] {'tensor'}, dimensions={0} | all-to-all | bytes 393216 | tf_op jit(solution)/shard_map/all_to_all | solution.py:25
  69.7 0.4 fusion.30
  70.1 0.0 slice-start.3
  70.2 15.7 %all_to_all.54 = bf16[32,24,256]{2,1,0:T(8,128)(2,1)S(1)} all-to-all(bf16[32,24,256]{2,1,0:T(8,128)(2,1)S(1)} %broadcast_in_dim.33), channel_id=1, replica_groups=mesh['groups'=1,'tensor'=32] {'tensor'}, dimensions={0} | all-to-all | bytes 786432 | tf_op jit(solution)/shard_map/all_to_all | solution.py:25
  85.9 0.2 fusion.31
  86.1 0.1 convert_bitcast_fusion
  86.2 0.1 copy.82
  86.3 0.0 copy-start.2
  86.3 2.0 %fusion.56 = f32[24,448]{1,0:T(8,128)S(1)} fusion(bf16[8192,448]{0,1:T(8,128)(2,1)S(1)} %bitcast.120, f32[24,8192]{1,0:T(8,128)S(1)} %bitcast.123, f32[24]{0:T(128)S(1)} %add_rsqrt_fusion), kind=kOutput, calls=%fused_computation.79 | convolution fusion | flops 176553984 | bytes 8169568 | tf_op jit(solution)/shard_map/dot_general | solution.py:132
  88.3 0.0 slice-done.3
  88.3 0.0 copy-start.4
  88.4 2.0 %convolution_multiply_fusion.1 = f32[24,448]{1,0:T(8,128)S(1)} fusion(bf16[8192,448]{0,1:T(8,128)(2,1)S(1)} %bitcast.122, f32[24,448]{1,0:T(8,128)S(1)} %fusion.56, f32[24,8192]{1,0:T(8,128)S(1)} %bitcast.124, f32[24]{0:T(128)S(1)} %add_rsqrt_fusion), kind=kOutput, calls=%fused_computation.17 | convolution fusion | flops 176607744 | bytes 8212576 | tf_op jit(solution)/shard_map/dot_general | solution.py:133
  90.4 0.0 copy-done.2
  90.4 0.6 convolution_convert_fusion.2
  91.0 0.1 all_to_all.43
  91.1 0.5 broadcast.127
  91.6 0.8 reduce.4
  92.4 0.1 reshape.173
  92.5 9.7 %all_to_all.55 = bf16[32,2,168]{2,1,0:T(2,128)(2,1)S(1)} all-to-all(bf16[32,2,168]{2,1,0:T(2,128)(2,1)S(1)} %reshape.173), channel_id=1, replica_groups=mesh['groups'=1,'tensor'=32] {'tensor'}, dimensions={0} | all-to-all | bytes 43008 | tf_op jit(solution)/shard_map/all_to_all | solution.py:141
  102.2 0.1 reshape.174
  102.3 0.1 fusion.29
  102.4 0.7 reduce.5
  103.1 0.1 reshape.175
  103.2 8.9 %all_to_all.56 = bf16[32,2,168]{2,1,0:T(2,128)(2,1)S(1)} all-to-all(bf16[32,2,168]{2,1,0:T(2,128)(2,1)S(1)} %reshape.175), channel_id=1, replica_groups=mesh['groups'=1,'tensor'=32] {'tensor'}, dimensions={0} | all-to-all | bytes 43008 | tf_op jit(solution)/shard_map/all_to_all | solution.py:143
  112.1 0.1 reshape.176
  112.2 0.1 reduce.3
  112.4 0.1 reshape.166
  112.5 4.2 %convolution_convert_fusion = bf16[24,8192]{1,0:T(8,128)(2,1)S(1)} fusion(bf16[24,448]{1,0:T(8,128)(2,1)S(1)} %reshape.166, bf16[448,8192]{1,0:T(8,128)(2,1)} %param.19), kind=kOutput, calls=%fused_computation | convolution fusion | flops 176357376 | bytes 7754752 | tf_op jit(solution)/shard_map/dot_general | solution.py:145
  116.7 14.9 %all_to_all.57 = bf16[32,24,256]{2,1,0:T(8,128)(2,1)S(1)} all-to-all(bf16[32,24,256]{2,1,0:T(8,128)(2,1)S(1)} %bitcast.127), channel_id=1, replica_groups=mesh['groups'=1,'tensor'=32] {'tensor'}, dimensions={0} | all-to-all | bytes 786432 | tf_op jit(solution)/shard_map/all_to_all | solution.py:19
  131.6 0.1 convert_reduce_fusion
  131.6 0.6 add_convert_fusion.1
  (28 shorter events, 0.4 us)
Async XLA Ops:
  0.0 1.8 %copy-start = (bf16[256,5120]{1,0:T(8,128)(2,1)S(1)}, bf16[256,5120]{1,0:T(8,128)(2,1)}, u32[]{:S(2)}) copy-start(bf16[256,5120]{1,0:T(8,128)(2,1)} %param.12) | copy-start | bytes 7864324
  4.0 17.9 %all-to-all-start = ((bf16[32,32,128]{2,1,0:T(8,128)(2,1)}), bf16[32,32,128]{2,1,0:T(8,128)(2,1)S(1)}, u32[]{:S(2)}, u32[]{:S(2)}) async-start(bf16[32,32,128]{2,1,0:T(8,128)(2,1)} %bitcast.2), calls=%async_computation | async-start | bytes 524288 | tf_op jit(solution)/shard_map/all_to_all | solution.py:19
  22.7 13.2 %all-to-all-start.1 = ((bf16[32,32,128]{2,1,0:T(8,128)(2,1)}), bf16[32,32,128]{2,1,0:T(8,128)(2,1)S(1)}, u32[]{:S(2)}, u32[]{:S(2)}) async-start(bf16[32,32,128]{2,1,0:T(8,128)(2,1)} %broadcast_in_dim.29), calls=%async_computation.1 | async-start | bytes 524288 | tf_op jit(solution)/shard_map/all_to_all | solution.py:25
  41.5 28.3 %copy-start.3 = (bf16[24,256]{1,0:T(8,128)(2,1)S(1)}, bf16[24,256]{1,0:T(8,128)(2,1)}, u32[]{:S(2)}) copy-start(bf16[24,256]{1,0:T(8,128)(2,1)} %param.11) | copy-start | bytes 36868
  41.7 28.1 %copy-start.1 = (bf16[4096,256]{1,0:T(8,128)(2,1)S(1)}, bf16[4096,256]{1,0:T(8,128)(2,1)}, u32[]{:S(2)}) copy-start(bf16[4096,256]{1,0:T(8,128)(2,1)} %param.16) | copy-start | bytes 6291460
  41.7 44.6 %slice-start = ((s8[7340032]{0:T(1024)(128)(4,1)}), s8[4194304]{0:T(1024)(128)(4,1)S(1)}, s32[]{:S(2)}) async-start(s8[7340032]{0:T(1024)(128)(4,1)} %bitcast.119), calls=%async_computation.8 | async-start | bytes 8388608
  41.7 46.6 %slice-start.2 = ((s8[7340032]{0:T(1024)(128)(4,1)}), s8[4194304]{0:T(1024)(128)(4,1)S(1)}, s32[]{:S(2)}) async-start(s8[7340032]{0:T(1024)(128)(4,1)} %bitcast.121), calls=%async_computation.10 | async-start | bytes 8388608
  45.7 40.5 %slice-start.1 = ((s8[7340032]{0:T(1024)(128)(4,1)}), s8[3145728]{0:T(1024)(128)(4,1)S(1)}, s32[]{:S(2)}) async-start(s8[7340032]{0:T(1024)(128)(4,1)} %bitcast.119), calls=%async_computation.9 | async-start | bytes 6291456
  70.1 18.2 %slice-start.3 = ((s8[7340032]{0:T(1024)(128)(4,1)}), s8[3145728]{0:T(1024)(128)(4,1)S(1)}, s32[]{:S(2)}) async-start(s8[7340032]{0:T(1024)(128)(4,1)} %bitcast.121), calls=%async_computation.11 | async-start | bytes 6291456
  86.3 4.1 %copy-start.2 = (f32[448,448]{1,0:T(8,128)S(1)}, f32[448,448]{1,0:T(8,128)}, u32[]{:S(2)}) copy-start(f32[448,448]{1,0:T(8,128)} %constant.42.clone) | copy-start | bytes 2408452
  88.3 13.9 %copy-start.4 = (bf16[32,32]{1,0:T(8,128)(2,1)S(1)}, bf16[32,32]{1,0:T(8,128)(2,1)}, u32[]{:S(2)}) copy-start(bf16[32,32]{1,0:T(8,128)(2,1)} %constant.43.clone) | copy-start | bytes 6148

commit v2 on v1

--- a/solution.py
+++ b/solution.py
@@ -15,14 +15,59 @@
 ROPE_BASE = 500000.0
 
 
+def across(value, apart):
+    pairs = [(source, source ^ apart) for source in range(lax.axis_size("tensor"))]
+    return lax.ppermute(value, "tensor", pairs)
+
+
+def same_core():
+    devices = lax.axis_size("tensor")
+    return [list(range(core, devices, 2)) for core in range(2)]
+
+
 def scattered_sum(pieces):
-    received = lax.all_to_all(pieces, "tensor", 0, 0, tiled=True)
+    second = lax.axis_index("tensor") % 2 == 1
+    halves = pieces.reshape(-1, 2, *pieces.shape[1:])
+    kept = jnp.where(second, halves[:, 1], halves[:, 0])
+    sent = jnp.where(second, halves[:, 0], halves[:, 1]).astype(jnp.bfloat16)
+    joined = kept.astype(jnp.float32) + across(sent, 1).astype(jnp.float32)
+    received = lax.all_to_all(
+        joined.astype(jnp.bfloat16), "tensor", 0, 0, tiled=True, axis_index_groups=same_core()
+    )
     return jnp.sum(received.astype(jnp.float32), axis=0)
 
 
 def gathered(piece):
-    copies = jnp.broadcast_to(piece[None], (lax.axis_size("tensor"), *piece.shape))
-    return lax.all_to_all(copies, "tensor", 0, 0, tiled=True)
+    second = lax.axis_index("tensor") % 2 == 1
+    copies = jnp.broadcast_to(piece[None], (lax.axis_size("tensor") // 2, *piece.shape))
+    mine = lax.all_to_all(copies, "tensor", 0, 0, tiled=True, axis_index_groups=same_core())
+    theirs = across(mine, 1)
+    both = jnp.stack([jnp.where(second, theirs, mine), jnp.where(second, mine, theirs)], axis=1)
+    return both.reshape(-1, *piece.shape)
+
+
+def signed_pair(value, apart):
+    upper = lax.axis_index("tensor") // apart % 2 == 1
+    partner = across(value, apart).astype(jnp.float32)
+    own = value.astype(jnp.float32)
+    return jnp.where(upper, partner - own, own + partner)
+
+
+def signed_sum(value):
+    devices = lax.axis_size("tensor")
+    middle = devices // 4
+    groups = [
+        [top * devices // 2 + 2 * inner + core for inner in range(middle)]
+        for top in range(2)
+        for core in range(2)
+    ]
+    value = signed_pair(value, 1)
+    value = signed_pair(value.astype(jnp.bfloat16), devices // 2).astype(jnp.bfloat16)
+    copies = jnp.broadcast_to(value[None], (middle, *value.shape))
+    received = lax.all_to_all(copies, "tensor", 0, 0, tiled=True, axis_index_groups=groups)
+    table = jnp.asarray(sylvester_table(middle), dtype=jnp.float32)
+    signs = table[lax.axis_index("tensor") // 2 % middle]
+    return jnp.sum(received.astype(jnp.float32) * signs[:, None, None], axis=0)
 
 
 def paley_table():
@@ -137,11 +182,7 @@
         np.kron(sylvester_table(local_width // 28), paley_table()), dtype=jnp.float32
     )
     mixed = jnp.dot(activation, local_table, precision=lax.Precision.HIGHEST)
-    share = mixed.astype(jnp.bfloat16).reshape(devices, -1)
-    share = lax.all_to_all(share, "tensor", 0, 0, tiled=True)
-    share = jnp.dot(jnp.asarray(sylvester_table(devices), dtype=jnp.bfloat16), share, preferred_element_type=jnp.float32)
-    share = lax.all_to_all((share * FF ** (-0.5)).astype(jnp.bfloat16), "tensor", 0, 0, tiled=True)
-    rotated = share.reshape(row_count, local_width)
+    rotated = (signed_sum(mixed) * FF ** (-0.5)).astype(jnp.bfloat16)
     down = jnp.dot(rotated, w_down, preferred_element_type=jnp.float32).astype(jnp.bfloat16)
     down_share = scattered_sum(down.reshape(row_count, devices, -1).transpose(1, 0, 2))
     return (residual.astype(jnp.float32) + down_share).astype(jnp.bfloat16)

time: 133 us -> 123 us (0.925)
  blocking collectives: 73.1 us -> 44.7 us
  waiting for transfers between devices: 19.6 us -> 32.1 us
  starting transfers between devices: 9.88 us -> 17.2 us
    all_to_all x6 -> x4, blocking collectives: 73.1 us -> 44.7 us  [the longest x2 22.4 us: scattered_sum(): lax.all_to_all(joined.astype(jnp.bfloat16), 'tensor', 0, 0, tiled=True, a...]
    ppermute x0 -> x8, waiting for transfers between devices: none -> 11.8 us  [across(): return lax.ppermute(value, 'tensor', pairs)]
    all_to_all x2 -> x3, starting transfers between devices: 9.88 us -> 15.1 us  [the longest x1 8.22 us: scattered_sum(): lax.all_to_all(joined.astype(jnp.bfloat16), 'tensor', 0, 0, tiled=True, a...]
    ppermute x0 -> x8, starting transfers between devices: none -> 2.03 us  [across(): return lax.ppermute(value, 'tensor', pairs)]
    all_to_all x3 -> x0, other arithmetic: 1.58 us -> none  [the longest x2 0.8 us: per_device(): lax.all_to_all((share * FF ** (-0.5)).astype(jnp.bfloat16), 'tensor', 0,...]
    all_to_all x2 -> x3, waiting for transfers between devices: 19.6 us -> 20.3 us  [the longest x1 7.78 us: scattered_sum(): lax.all_to_all(joined.astype(jnp.bfloat16), 'tensor', 0, 0, tiled=True, a...]
  transfers between devices with their start and end apart: 2 -> 11, of which waited for: 2 -> 11; matrix products, arithmetic and copies ran while one was open for 1% -> 2% of each run, Pallas kernels for 0% -> 0%
where the time goes in v2:
time: 123 us; the launch traced here: 122 us
  blocking collectives  44.7 us (36%)
  waiting for transfers between devices  32.1 us (26%)
  matrix products  19 us (15%)
  starting transfers between devices  17.2 us (14%)
  other arithmetic  5.56 us (5%)
  local copies, waits for them, and re-layouts  3.47 us (3%)
    all_to_all x2, blocking collectives, scattered_sum(): lax.all_to_all(joined.astype(jnp.bfloat16), 'tensor', 0, 0, tiled=True, a...  22.4 us
    all_to_all x2, blocking collectives, gathered(): lax.all_to_all(copies, 'tensor', 0, 0, tiled=True, axis_index_groups=same...  22.3 us
    ppermute x8, waiting for transfers between devices, across(): return lax.ppermute(value, 'tensor', pairs)  11.8 us
    all_to_all x1, starting transfers between devices, scattered_sum(): lax.all_to_all(joined.astype(jnp.bfloat16), 'tensor', 0, 0, tiled=True, a...  8.22 us
    all_to_all x1, waiting for transfers between devices, scattered_sum(): lax.all_to_all(joined.astype(jnp.bfloat16), 'tensor', 0, 0, tiled=True, a...  7.78 us
    all_to_all x1, waiting for transfers between devices, gathered(): lax.all_to_all(copies, 'tensor', 0, 0, tiled=True, axis_index_groups=same...  6.95 us
    all_to_all x1, waiting for transfers between devices, signed_sum(): lax.all_to_all(copies, 'tensor', 0, 0, tiled=True, axis_index_groups=groups)  5.56 us
    dot_general x1, matrix products, per_device(): jnp.einsum('kgrd,rckd->rkgc', grouped, keys_local, preferred_element_type...  4.62 us
  transfers between devices with their start and end apart: 11, of which 11 were waited for; matrix products, arithmetic and copies ran while one was open for 2% of the time, Pallas kernels for 0%

profile of v2, /device:TPU:0, one launch (start us, length us, event | category | flops | bytes accessed | tf_op | source)
XLA Modules:
  0.0 122.5 jit_solution(5380464950823410915)
XLA Ops:
  0.0 1.0 fusion.43
  1.0 0.1 pad.16.clone
  1.1 0.1 pad.15.clone
  1.1 0.6 copy-done
  1.8 1.2 fusion.24
  2.9 0.1 copy.172
  3.0 0.3 maximum_maximum_fusion
  3.3 0.5 collective-permute-start
  3.9 1.0 collective-permute-done
  4.8 0.7 fusion.28
  5.6 8.2 %all-to-all-start = ((bf16[16,32,128]{2,1,0:T(8,128)(2,1)}), bf16[16,32,128]{2,1,0:T(8,128)(2,1)S(1)}, u32[]{:S(2)}, u32[]{:S(2)}) async-start(bf16[16,32,128]{2,1,0:T(8,128)(2,1)} %fusion.28), calls=%async_computation | async-start | bytes 262144 | tf_op jit(solution)/shard_map/all_to_all | solution.py:34
  13.8 7.8 %all-to-all-done = bf16[16,32,128]{2,1,0:T(8,128)(2,1)S(1)} async-done(((bf16[16,32,128]{2,1,0:T(8,128)(2,1)}), bf16[16,32,128]{2,1,0:T(8,128)(2,1)S(1)}, u32[]{:S(2)}, u32[]{:S(2)}) %all-to-all-start) | async-done | bytes 131104 | tf_op jit(solution)/shard_map/all_to_all | solution.py:34
  21.6 0.7 broadcast_in_dim.31
  22.3 3.5 %all-to-all-start.1 = ((bf16[16,32,128]{2,1,0:T(8,128)(2,1)}), bf16[16,32,128]{2,1,0:T(8,128)(2,1)S(1)}, u32[]{:S(2)}, u32[]{:S(2)}) async-start(bf16[16,32,128]{2,1,0:T(8,128)(2,1)} %broadcast_in_dim.31), calls=%async_computation.1 | async-start | bytes 262144 | tf_op jit(solution)/shard_map/all_to_all | solution.py:43
  25.8 0.7 convert_element_type.137
  26.5 0.1 multiply_cosine_fusion
  26.6 7.0 %all-to-all-done.1 = bf16[16,32,128]{2,1,0:T(8,128)(2,1)S(1)} async-done(((bf16[16,32,128]{2,1,0:T(8,128)(2,1)}), bf16[16,32,128]{2,1,0:T(8,128)(2,1)S(1)}, u32[]{:S(2)}, u32[]{:S(2)}) %all-to-all-start.1) | async-done | bytes 131104 | tf_op jit(solution)/shard_map/all_to_all | solution.py:43
  33.6 0.7 broadcast_compare_fusion
  34.3 0.6 collective-permute-done.1
  35.2 0.2 add_convert_fusion
  35.4 0.1 fusion.44
  35.5 0.1 fusion.30
  35.6 0.2 fusion.33
  35.9 0.1 copy.121
  35.9 4.6 %fusion.57 = (f32[24,4,8]{2,1,0:T(4,128)S(1)}, bf16[24,4,8,256]{3,2,1,0:T(8,128)(2,1)S(1)}) fusion(bf16[32,24,128]{2,1,0:T(8,128)(2,1)S(1)} %fusion.30, pred[24,256]{1,0:T(8,128)(4,1)S(1)} %broadcast_compare_fusion, bf16[24,256,512]{2,1,0:T(8,128)(2,1)} %param.13), kind=kOutput, calls=%fused_computation.101 | convolution fusion | flops 51117312 | bytes 6890496 | tf_op jit(solution)/shard_map/kgrd,rckd->rkgc/dot_general | solution.py:143
  40.6 0.1 copy.111
  40.7 0.1 copy.109
  40.8 0.0 slice-start
  40.8 3.9 %fusion.21 = bf16[4,8,24,128]{3,1,0,2:T(8,128)(2,1)S(1)} fusion(bf16[24,4,8,256]{3,2,1,0:T(8,128)(2,1)S(1)} %get-tuple-element.18, f32[4,24,128]{2,0,1:T(4,128)S(1)} %copy.110, f32[4,8,24]{1,0,2:T(4,128)S(1)} %copy.109, bf16[24,256,512]{2,1,0:T(8,128)(2,1)} %param.14), kind=kOutput, calls=%fused_computation.13 | convolution fusion | flops 50626560 | bytes 6933504 | tf_op jit(solution)/shard_map/rkgc,rckd->rkgd/dot_general | solution.py:148
  44.7 0.2 collective-permute-start.2
  44.9 1.2 collective-permute-done.2
  46.2 0.0 slice-start.1
  46.2 10.9 %all_to_all.35 = bf16[16,25,128]{2,1,0:T(8,128)(2,1)S(1)} all-to-all(bf16[16,25,128]{2,1,0:T(8,128)(2,1)S(1)} %copy.114), channel_id=1, replica_groups={{0,2,4,6,8,10,12,14,16,18,20,22,24,26,28,30},{1,3,5,7,9,11,13,15,17,19,..., dimensions={0} | all-to-all | bytes 204800 | tf_op jit(solution)/shard_map/all_to_all | solution.py:34
  57.1 0.1 fusion.50
  57.2 10.6 %all_to_all.36 = bf16[16,24,128]{2,1,0:T(8,128)(2,1)S(1)} all-to-all(bf16[16,24,128]{2,1,0:T(8,128)(2,1)S(1)} %broadcast_in_dim.34), channel_id=1, replica_groups={{0,2,4,6,8,10,12,14,16,18,20,22,24,26,28,30},{1,3,5,7,9,11,13,15,17,19,..., dimensions={0} | all-to-all | bytes 196608 | tf_op jit(solution)/shard_map/all_to_all | solution.py:43
  67.8 1.3 %collective-permute-done.3 = bf16[16,24,128]{2,1,0:T(8,128)(2,1)S(1)} collective-permute-done((bf16[16,24,128]{2,1,0:T(8,128)(2,1)S(1)}, bf16[16,24,128]{2,1,0:T(8,128)(2,1)S(1)}, u32[]{:S(2)}, u32[]{:S(2)}) %collective-permute-start.3) | collective-permute-done | bytes 98336 | tf_op jit(solution)/shard_map/ppermute | solution.py:20
  69.2 0.0 slice-start.2
  69.2 0.4 fusion.25
  69.6 11.8 %all_to_all.37 = bf16[16,24,256]{2,1,0:T(8,128)(2,1)S(1)} all-to-all(bf16[16,24,256]{2,1,0:T(8,128)(2,1)S(1)} %broadcast_in_dim.35), channel_id=1, replica_groups={{0,2,4,6,8,10,12,14,16,18,20,22,24,26,28,30},{1,3,5,7,9,11,13,15,17,19,..., dimensions={0} | all-to-all | bytes 393216 | tf_op jit(solution)/shard_map/all_to_all | solution.py:43
  81.4 1.4 %collective-permute-done.4 = bf16[16,24,256]{2,1,0:T(8,128)(2,1)S(1)} collective-permute-done((bf16[16,24,256]{2,1,0:T(8,128)(2,1)S(1)}, bf16[16,24,256]{2,1,0:T(8,128)(2,1)S(1)}, u32[]{:S(2)}, u32[]{:S(2)}) %collective-permute-start.4) | collective-permute-done | bytes 196640 | tf_op jit(solution)/shard_map/ppermute | solution.py:20
  82.9 0.2 multiply_reduce_fusion
  83.1 0.1 maximum_convert_fusion
  83.2 0.1 copy.128
  83.3 0.0 slice-start.3
  83.3 2.0 %fusion.55 = f32[24,448]{1,0:T(8,128)S(1)} fusion(bf16[8192,448]{0,1:T(8,128)(2,1)S(1)} %bitcast.158, f32[24,8192]{1,0:T(8,128)S(1)} %bitcast.161, f32[24]{0:T(128)S(1)} %add_rsqrt_fusion), kind=kOutput, calls=%fused_computation.100 | convolution fusion | flops 176553984 | bytes 8169568 | tf_op jit(solution)/shard_map/dot_general | solution.py:177
  85.3 0.0 slice-done.3
  85.3 2.0 %convolution_multiply_fusion = f32[24,448]{1,0:T(8,128)S(1)} fusion(bf16[8192,448]{0,1:T(8,128)(2,1)S(1)} %bitcast.160, f32[24,448]{1,0:T(8,128)S(1)} %fusion.55, f32[24,8192]{1,0:T(8,128)S(1)} %bitcast.162, f32[24]{0:T(128)S(1)} %add_rsqrt_fusion), kind=kOutput, calls=%fused_computation.15 | convolution fusion | flops 176607744 | bytes 8212576 | tf_op jit(solution)/shard_map/dot_general | solution.py:178
  87.4 0.0 copy-done.2
  87.4 0.6 fusion.58
  87.9 0.2 collective-permute-start.5
  88.1 1.1 collective-permute-done.5
  89.2 1.1 collective-permute-start.6
  90.3 3.7 %collective-permute-done.6 = bf16[24,448]{1,0:T(8,128)(2,1)S(1)} collective-permute-done((bf16[24,448]{1,0:T(8,128)(2,1)S(1)}, bf16[24,448]{1,0:T(8,128)(2,1)S(1)}, u32[]{:S(2)}, u32[]{:S(2)}) %collective-permute-start.6) | collective-permute-done | bytes 21536 | tf_op jit(solution)/shard_map/ppermute | solution.py:20
  94.0 0.7 broadcast_in_dim.36
  94.7 3.4 %all-to-all-start.5 = ((bf16[8,24,448]{2,1,0:T(8,128)(2,1)}), bf16[8,24,448]{2,1,0:T(8,128)(2,1)S(1)}, u32[]{:S(2)}, u32[]{:S(2)}) async-start(bf16[8,24,448]{2,1,0:T(8,128)(2,1)} %broadcast_in_dim.36), calls=%async_computation.5 | async-start | bytes 393216 | tf_op jit(solution)/shard_map/all_to_all | solution.py:67
  98.1 0.7 dynamic-slice_bitcast_fusion
  98.8 5.6 %all-to-all-done.5 = bf16[8,24,448]{2,1,0:T(8,128)(2,1)S(1)} async-done(((bf16[8,24,448]{2,1,0:T(8,128)(2,1)}), bf16[8,24,448]{2,1,0:T(8,128)(2,1)S(1)}, u32[]{:S(2)}, u32[]{:S(2)}) %all-to-all-start.5) | async-done | bytes 172064 | tf_op jit(solution)/shard_map/all_to_all | solution.py:67
  104.4 0.1 multiply_reduce_fusion.1
  104.5 4.2 %convolution_convert_fusion = bf16[24,8192]{1,0:T(8,128)(2,1)S(1)} fusion(bf16[448,8192]{1,0:T(8,128)(2,1)} %param.19, f32[24,448]{1,0:T(8,128)S(1)} %multiply_reduce_fusion.1), kind=kOutput, calls=%fused_computation | convolution fusion | flops 176378880 | bytes 7776256 | tf_op jit(solution)/shard_map/dot_general | solution.py:186
  108.8 0.1 collective-permute-start.7
  108.8 1.4 %collective-permute-done.7 = bf16[16,24,256]{2,1,0:T(8,128)(2,1)S(1)} collective-permute-done((bf16[16,24,256]{2,1,0:T(8,128)(2,1)S(1)}, bf16[16,24,256]{2,1,0:T(8,128)(2,1)S(1)}, u32[]{:S(2)}, u32[]{:S(2)}) %collective-permute-start.7) | collective-permute-done | bytes 196640 | tf_op jit(solution)/shard_map/ppermute | solution.py:20
  110.3 0.1 fusion.26
  110.3 11.5 %all_to_all.38 = bf16[16,24,256]{2,1,0:T(8,128)(2,1)S(1)} all-to-all(bf16[16,24,256]{2,1,0:T(8,128)(2,1)S(1)} %fusion.26), channel_id=1, replica_groups={{0,2,4,6,8,10,12,14,16,18,20,22,24,26,28,30},{1,3,5,7,9,11,13,15,17,19,..., dimensions={0} | all-to-all | bytes 393216 | tf_op jit(solution)/shard_map/all_to_all | solution.py:34
  121.9 0.6 add_convert_fusion.1
  (48 shorter events, 0.7 us)
Async XLA Ops:
  0.0 1.8 %copy-start = (bf16[256,5120]{1,0:T(8,128)(2,1)S(1)}, bf16[256,5120]{1,0:T(8,128)(2,1)}, u32[]{:S(2)}) copy-start(bf16[256,5120]{1,0:T(8,128)(2,1)} %param.12) | copy-start | bytes 7864324
  3.3 1.5 %collective-permute-start = (bf16[16,32,128]{2,1,0:T(8,128)(2,1)S(1)}, bf16[16,32,128]{2,1,0:T(8,128)(2,1)S(1)}, u32[]{:S(2)}, u32[]{:S(2)}) collective-permute-start(bf16[16,32,128]{2,1,0:T(8,128)(2,1)S(1)} %fusion.38), channel_id=1, source_target_pairs={{0,1},{1,0},{2,3},{3,2},{4,5},{5,4},{6,7},{7,6},{8,9},{9,8},{10,11... | collective-permute-start | bytes 393224 | tf_op jit(solution)/shard_map/ppermute | solution.py:20
  5.6 16.0 %all-to-all-start = ((bf16[16,32,128]{2,1,0:T(8,128)(2,1)}), bf16[16,32,128]{2,1,0:T(8,128)(2,1)S(1)}, u32[]{:S(2)}, u32[]{:S(2)}) async-start(bf16[16,32,128]{2,1,0:T(8,128)(2,1)} %fusion.28), calls=%async_computation | async-start | bytes 262144 | tf_op jit(solution)/shard_map/all_to_all | solution.py:34
  22.3 11.3 %all-to-all-start.1 = ((bf16[16,32,128]{2,1,0:T(8,128)(2,1)}), bf16[16,32,128]{2,1,0:T(8,128)(2,1)S(1)}, u32[]{:S(2)}, u32[]{:S(2)}) async-start(bf16[16,32,128]{2,1,0:T(8,128)(2,1)} %broadcast_in_dim.31), calls=%async_computation.1 | async-start | bytes 262144 | tf_op jit(solution)/shard_map/all_to_all | solution.py:43
  33.6 1.3 %collective-permute-start.1 = (bf16[16,32,128]{2,1,0:T(8,128)(2,1)S(1)}, bf16[16,32,128]{2,1,0:T(8,128)(2,1)S(1)}, u32[]{:S(2)}, u32[]{:S(2)}) collective-permute-start(bf16[16,32,128]{2,1,0:T(8,128)(2,1)S(1)} %all-to-all-done.1), channel_id=1, source_target_pairs={{0,1},{1,0},{2,3},{3,2},{4,5},{5,4},{6,7},{7,6},{8,9},{9,8},{10,11... | collective-permute-start | bytes 393224 | tf_op jit(solution)/shard_map/ppermute | solution.py:20
  40.6 28.6 %copy-start.3 = (bf16[24,256]{1,0:T(8,128)(2,1)S(1)}, bf16[24,256]{1,0:T(8,128)(2,1)}, u32[]{:S(2)}) copy-start(bf16[24,256]{1,0:T(8,128)(2,1)} %param.11) | copy-start | bytes 36868
  40.8 28.4 %copy-start.1 = (bf16[4096,256]{1,0:T(8,128)(2,1)S(1)}, bf16[4096,256]{1,0:T(8,128)(2,1)}, u32[]{:S(2)}) copy-start(bf16[4096,256]{1,0:T(8,128)(2,1)} %param.16) | copy-start | bytes 6291460
  40.8 42.4 %slice-start = ((s8[7340032]{0:T(1024)(128)(4,1)}), s8[4194304]{0:T(1024)(128)(4,1)S(1)}, s32[]{:S(2)}) async-start(s8[7340032]{0:T(1024)(128)(4,1)} %bitcast.157), calls=%async_computation.7 | async-start | bytes 8388608
  44.7 1.4 %collective-permute-start.2 = (bf16[16,25,128]{2,0,1:T(8,128)(2,1)S(1)}, bf16[16,25,128]{2,0,1:T(8,128)(2,1)S(1)}, u32[]{:S(2)}, u32[]{:S(2)}) collective-permute-start(bf16[16,25,128]{2,0,1:T(8,128)(2,1)S(1)} %select_bitcast_fusion.5), channel_id=1, source_target_pairs={{0,1},{1,0},{2,3},{3,2},{4,5},{5,4},{6,7},{7,6},{8,9},{9,8},{10,11... | collective-permute-start | bytes 307208 | tf_op jit(solution)/shard_map/ppermute | solution.py:20
  46.2 37.1 %slice-start.1 = ((s8[7340032]{0:T(1024)(128)(4,1)}), s8[3145728]{0:T(1024)(128)(4,1)S(1)}, s32[]{:S(2)}) async-start(s8[7340032]{0:T(1024)(128)(4,1)} %bitcast.157), calls=%async_computation.8 | async-start | bytes 6291456
  67.8 1.3 %collective-permute-start.3 = (bf16[16,24,128]{2,1,0:T(8,128)(2,1)S(1)}, bf16[16,24,128]{2,1,0:T(8,128)(2,1)S(1)}, u32[]{:S(2)}, u32[]{:S(2)}) collective-permute-start(bf16[16,24,128]{2,1,0:T(8,128)(2,1)S(1)} %all_to_all.36), channel_id=1, source_target_pairs={{0,1},{1,0},{2,3},{3,2},{4,5},{5,4},{6,7},{7,6},{8,9},{9,8},{10,11... | collective-permute-start | bytes 294920 | tf_op jit(solution)/shard_map/ppermute | solution.py:20
  69.2 16.1 %slice-start.2 = ((s8[7340032]{0:T(1024)(128)(4,1)}), s8[4194304]{0:T(1024)(128)(4,1)S(1)}, s32[]{:S(2)}) async-start(s8[7340032]{0:T(1024)(128)(4,1)} %bitcast.159), calls=%async_computation.9 | async-start | bytes 8388608
  81.4 1.4 %collective-permute-start.4 = (bf16[16,24,256]{2,1,0:T(8,128)(2,1)S(1)}, bf16[16,24,256]{2,1,0:T(8,128)(2,1)S(1)}, u32[]{:S(2)}, u32[]{:S(2)}) collective-permute-start(bf16[16,24,256]{2,1,0:T(8,128)(2,1)S(1)} %all_to_all.37), channel_id=1, source_target_pairs={{0,1},{1,0},{2,3},{3,2},{4,5},{5,4},{6,7},{7,6},{8,9},{9,8},{10,11... | collective-permute-start | bytes 589832 | tf_op jit(solution)/shard_map/ppermute | solution.py:20
  83.3 2.1 %slice-start.3 = ((s8[7340032]{0:T(1024)(128)(4,1)}), s8[3145728]{0:T(1024)(128)(4,1)S(1)}, s32[]{:S(2)}) async-start(s8[7340032]{0:T(1024)(128)(4,1)} %bitcast.159), calls=%async_computation.10 | async-start | bytes 6291456
  83.3 4.1 %copy-start.2 = (f32[448,448]{1,0:T(8,128)S(1)}, f32[448,448]{1,0:T(8,128)}, u32[]{:S(2)}) copy-start(f32[448,448]{1,0:T(8,128)} %constant.113.clone) | copy-start | bytes 2408452
  87.9 1.3 %collective-permute-start.5 = (f32[24,448]{1,0:T(8,128)S(1)}, f32[24,448]{1,0:T(8,128)S(1)}, u32[]{:S(2)}, u32[]{:S(2)}) collective-permute-start(f32[24,448]{1,0:T(8,128)S(1)} %fusion.58), channel_id=1, source_target_pairs={{0,1},{1,0},{2,3},{3,2},{4,5},{5,4},{6,7},{7,6},{8,9},{9,8},{10,11... | collective-permute-start | bytes 129032 | tf_op jit(solution)/shard_map/ppermute | solution.py:20
  89.2 4.8 %collective-permute-start.6 = (bf16[24,448]{1,0:T(8,128)(2,1)S(1)}, bf16[24,448]{1,0:T(8,128)(2,1)S(1)}, u32[]{:S(2)}, u32[]{:S(2)}) collective-permute-start(bf16[24,448]{1,0:T(8,128)(2,1)S(1)} %select_convert_fusion), channel_id=1, source_target_pairs={{0,16},{1,17},{2,18},{3,19},{4,20},{5,21},{6,22},{7,23},{8,24},{9,... | collective-permute-start | bytes 64520 | tf_op jit(solution)/shard_map/ppermute | solution.py:20
  94.7 9.7 %all-to-all-start.5 = ((bf16[8,24,448]{2,1,0:T(8,128)(2,1)}), bf16[8,24,448]{2,1,0:T(8,128)(2,1)S(1)}, u32[]{:S(2)}, u32[]{:S(2)}) async-start(bf16[8,24,448]{2,1,0:T(8,128)(2,1)} %broadcast_in_dim.36), calls=%async_computation.5 | async-start | bytes 393216 | tf_op jit(solution)/shard_map/all_to_all | solution.py:67
  108.8 1.5 %collective-permute-start.7 = (bf16[16,24,256]{2,1,0:T(8,128)(2,1)S(1)}, bf16[16,24,256]{2,1,0:T(8,128)(2,1)S(1)}, u32[]{:S(2)}, u32[]{:S(2)}) collective-permute-start(bf16[16,24,256]{2,1,0:T(8,128)(2,1)S(1)} %select_bitcast_fusion), channel_id=1, source_target_pairs={{0,1},{1,0},{2,3},{3,2},{4,5},{5,4},{6,7},{7,6},{8,9},{9,8},{10,11... | collective-permute-start | bytes 589832 | tf_op jit(solution)/shard_map/ppermute | solution.py:20

commit v3 on v2

v3 whole, which is shorter than its diff:
```python
import jax
import jax.numpy as jnp
import numpy as np
from jax import lax
from jax.experimental import pallas as pl
from jax.experimental.pallas import tpu as pltpu
from jax.sharding import PartitionSpec as P

D = 8192
FF = 14336
H = 32
KVH = 4
HD = 128


EPSILON = 1e-05
ROPE_BASE = 500000.0
QKV_CHUNK = 1024
DOWN_CHUNK = 1024
ROW_CHUNK = 4
ROWS_AT_ONCE = 8


def across(value, apart):
    pairs = [(source, source ^ apart) for source in range(lax.axis_size("tensor"))]
    return lax.ppermute(value, "tensor", pairs)


def same_core():
    devices = lax.axis_size("tensor")
    return [list(range(core, devices, 2)) for core in range(2)]


def scattered_sum(pieces):
    second = lax.axis_index("tensor") % 2 == 1
    halves = pieces.reshape(-1, 2, *pieces.shape[1:])
    kept = jnp.where(second, halves[:, 1], halves[:, 0])
    sent = jnp.where(second, halves[:, 0], halves[:, 1]).astype(jnp.bfloat16)
    return scattered_halves(kept, sent)


def scattered_halves(kept, sent):
    return scattered_joined(kept, across(sent, 1))


def scattered_joined(kept, arrived):
    joined = kept.astype(jnp.float32) + arrived.astype(jnp.float32)
    received = lax.all_to_all(
        joined.astype(jnp.bfloat16), "tensor", 0, 0, tiled=True, axis_index_groups=same_core()
    )
    return jnp.sum(received.astype(jnp.float32), axis=0)


def gathered(piece):
    second = lax.axis_index("tensor") % 2 == 1
    copies = jnp.broadcast_to(piece[None], (lax.axis_size("tensor") // 2, *piece.shape))
    mine = lax.all_to_all(copies, "tensor", 0, 0, tiled=True, axis_index_groups=same_core())
    theirs = across(mine, 1)
    both = jnp.stack([jnp.where(second, theirs, mine), jnp.where(second, mine, theirs)], axis=1)
    return both.reshape(-1, *piece.shape)


def signed_pair(value, apart):
    upper = lax.axis_index("tensor") // apart % 2 == 1
    partner = across(value, apart).astype(jnp.float32)
    own = value.astype(jnp.float32)
    return jnp.where(upper, partner - own, own + partner)


def signed_sum(value):
    devices = lax.axis_size("tensor")
    middle = devices // 4
    groups = [
        [top * devices // 2 + 2 * inner + core for inner in range(middle)]
        for top in range(2)
        for core in range(2)
    ]
    value = signed_pair(value, 1)
    value = signed_pair(value.astype(jnp.bfloat16), devices // 2).astype(jnp.bfloat16)
    copies = jnp.broadcast_to(value[None], (middle, *value.shape))
    received = lax.all_to_all(copies, "tensor", 0, 0, tiled=True, axis_index_groups=groups)
    received, index = lax.optimization_barrier((received, lax.axis_index("tensor")))
    common = jnp.arange(middle) & (index // 2 % middle)
    for shift in (4, 2, 1):
        common = common ^ (common >> shift)
    signs = 1.0 - 2.0 * (common & 1).astype(jnp.float32)
    return jnp.sum(received.astype(jnp.float32) * signs[:, None, None], axis=0)


def in_hbm(value):
    return pltpu.with_memory_space_constraint(value, pltpu.HBM)


def column_copies(weights_ref, held_ref, arrived, chunk):
    copies = []
    for start in range(0, weights_ref.shape[1], chunk):
        part = (slice(None), pl.ds(start, chunk))
        copies.append(
            pltpu.make_async_copy(
                weights_ref.at[part], held_ref.at[part], arrived.at[start // chunk]
            )
        )
        copies[-1].start()
    return copies


def project_kernel(
    core_ref, hidden_source, source_ref, out_ref, hidden_ref, hidden_arrived, weights_ref, arrived, stacked
):
    hidden_copy = pltpu.make_async_copy(hidden_source, hidden_ref, hidden_arrived)
    hidden_copy.start()
    copies = column_copies(source_ref, weights_ref, arrived, QKV_CHUNK)
    core = core_ref[0]
    rows = hidden_ref.shape[0]
    columns = weights_ref.shape[1]
    hidden_copy.wait()
    hidden = hidden_ref[...]
    wide = hidden.astype(jnp.float32)
    squares = jnp.sum(wide * wide, axis=1, keepdims=True)
    for start in range(0, columns, 2 * HD):
        if start % QKV_CHUNK == 0:
            copies[start // QKV_CHUNK].wait()
        part = jnp.dot(
            hidden, weights_ref[:, start : start + 2 * HD], preferred_element_type=jnp.float32
        )
        first = start // HD * rows
        stacked[first : first + rows] = part[:, :HD]
        stacked[first + rows : first + 2 * rows] = part[:, HD:]
    used = columns // HD * rows
    stacked[used : used + rows] = jnp.broadcast_to(squares, (rows, HD))
    stacked[used + rows :] = jnp.zeros((stacked.shape[0] - used - rows, HD), jnp.float32)
    held = out_ref.shape[2]
    for piece in range(stacked.shape[0] // held):
        values = stacked[piece * held : (piece + 1) * held].astype(jnp.bfloat16)
        out_ref[(piece % 2) ^ core, piece // 2] = values


def projected_pieces(core, hidden, w_qkv, devices, rows_sent):
    vmem = pl.BlockSpec(memory_space=pltpu.VMEM)
    return pl.pallas_call(
        project_kernel,
        out_shape=jax.ShapeDtypeStruct((2, devices // 2, rows_sent, HD), jnp.bfloat16),
        in_specs=[
            pl.BlockSpec(memory_space=pltpu.SMEM),
            pl.BlockSpec(memory_space=pltpu.HBM),
            pl.BlockSpec(memory_space=pltpu.HBM),
        ],
        out_specs=vmem,
        scratch_shapes=[
            pltpu.VMEM(hidden.shape, hidden.dtype),
            pltpu.SemaphoreType.DMA,
            pltpu.VMEM(w_qkv.shape, w_qkv.dtype),
            pltpu.SemaphoreType.DMA((w_qkv.shape[1] // QKV_CHUNK,)),
            pltpu.VMEM((devices * rows_sent, HD), jnp.float32),
        ],
        compiler_params=pltpu.CompilerParams(vmem_limit_bytes=8 * 2**20),
        cost_estimate=pl.CostEstimate(
            flops=2 * hidden.shape[0] * w_qkv.size, bytes_accessed=2 * w_qkv.size, transcendentals=0
        ),
    )(core, in_hbm(hidden), in_hbm(w_qkv))


def attend_kernel(
    device_ref, core_ref, lengths_ref, projected_ref, cosine_ref, sine_ref, key_source, value_source,
    out_ref, keys_ref, values_ref, keys_arrived, values_arrived, queries, fresh, sums,
):
    rows, slots = keys_ref.shape[0], keys_ref.shape[1]

    def copies(index):
        part = pl.ds(index * ROW_CHUNK, ROW_CHUNK)
        return (
            pltpu.make_async_copy(key_source.at[part], keys_ref.at[part], keys_arrived.at[index]),
            pltpu.make_async_copy(value_source.at[part], values_ref.at[part], values_arrived.at[index]),
        )

    for index in range(rows // ROW_CHUNK):
        for copy in copies(index):
            copy.start()
    device, core = device_ref[0], core_ref[0]
    group = H // KVH
    scale = HD ** (-0.5)
    cosine, sine = cosine_ref[...], sine_ref[...]
    inverse = lax.rsqrt(projected_ref[H + 2 * KVH].astype(jnp.float32) / D + EPSILON)

    def block(index):
        value = projected_ref[index].astype(jnp.float32) * inverse
        return value.astype(jnp.bfloat16).astype(jnp.float32)

    def turned(index):
        value = block(index)
        value = value * cosine + pltpu.roll(value, HD // 2, 1) * sine
        return value.astype(jnp.bfloat16).astype(jnp.float32)

    for head in range(H):
        queries[pl.ds(head, rows, stride=H), :] = turned(head)
    for head in range(KVH):
        fresh[pl.ds(head, rows, stride=2 * KVH), :] = turned(H + head)
        fresh[pl.ds(KVH + head, rows, stride=2 * KVH), :] = block(H + KVH + head)

    lane = lax.broadcasted_iota(jnp.int32, (1, slots), 1) + device * slots
    row_lane = lax.broadcasted_iota(jnp.int32, (H, HD), 1)
    pair_row = lax.broadcasted_iota(jnp.int32, (2 * group, HD), 0)
    lower = pair_row < group
    pairs = KVH // 2

    def expand(first):
        picked = [
            jnp.broadcast_to(fresh[pl.ds(first + head, 1), :], (group, HD)) for head in range(KVH)
        ]
        return jnp.concatenate(picked, axis=0)

    def some_rows(step, totals, count):
        numbers = [step * count + offset for offset in range(count)]
        scores = []
        own = []
        for offset, row in enumerate(numbers):
            if offset % ROW_CHUNK == 0:
                copies(step * (count // ROW_CHUNK) + offset // ROW_CHUNK)[0].wait()
            query = queries[pl.ds(pl.multiple_of(row * H, H), H), :]
            own_score = jnp.sum(query * expand(row * 2 * KVH), axis=1, keepdims=True) * scale
            own.append(jnp.where(device == 0, jnp.exp(own_score), 0.0))
            parts = []
            for pair in range(pairs):
                chosen = query[pair * 2 * group : (pair + 1) * 2 * group]
                spread = jnp.concatenate(
                    [jnp.where(lower, chosen, 0.0), jnp.where(lower, 0.0, chosen)], axis=1
                ).astype(jnp.bfloat16)
                parts.append(
                    lax.dot_general(
                        spread,
                        keys_ref[row, :, pair * 2 * HD : (pair + 1) * 2 * HD],
                        (((1,), (1,)), ((), ())),
                        preferred_element_type=jnp.float32,
                    )
                )
            scores.append(jnp.concatenate(parts, axis=0))
        weights = [
            jnp.where(lane < lengths_ref[pl.ds(row, 1), :1], jnp.exp(score * scale), 0.0)
            for row, score in zip(numbers, scores)
        ]
        for offset, (row, weight, own_weight) in enumerate(zip(numbers, weights, own)):
            if offset % ROW_CHUNK == 0:
                copies(step * (count // ROW_CHUNK) + offset // ROW_CHUNK)[1].wait()
            rounded = weight.astype(jnp.bfloat16)
            parts = []
            for pair in range(pairs):
                product = jnp.dot(
                    rounded[pair * 2 * group : (pair + 1) * 2 * group],
                    values_ref[row, :, pair * 2 * HD : (pair + 1) * 2 * HD],
                    preferred_element_type=jnp.float32,
                )
                parts.append(product[:group, :HD])
                parts.append(product[group:, HD:])
            total = jnp.sum(weight, axis=1, keepdims=True) + own_weight
            summed = jnp.concatenate(parts, axis=0) + own_weight * expand(row * 2 * KVH + KVH)
            sums[pl.ds(pl.multiple_of(row * H, H), H), :] = summed
            totals = jnp.where(row_lane == row, total, totals)
        return totals

    count = ROWS_AT_ONCE
    totals = lax.fori_loop(
        0,
        rows // count,
        lambda step, totals: some_rows(step, totals, count),
        jnp.zeros((H, HD), jnp.float32),
    )
    for head in range(H):
        start = head // 8 * 8
        values = jnp.concatenate(
            [sums[pl.ds(head, rows, stride=H), :], totals[start : start + 8]], axis=0
        )
        out_ref[(head % 2) ^ core, head // 2] = values.astype(jnp.bfloat16)


def attended_pieces(device, core, lengths, projected, cosine, sine, key_cache, value_cache):
    rows, slots = key_cache.shape[0], key_cache.shape[1]
    smem = pl.BlockSpec(memory_space=pltpu.SMEM)
    vmem = pl.BlockSpec(memory_space=pltpu.VMEM)
    return pl.pallas_call(
        attend_kernel,
        out_shape=jax.ShapeDtypeStruct((2, H // 2, rows + 8, HD), jnp.bfloat16),
        in_specs=[smem] * 2 + [vmem] * 4 + [pl.BlockSpec(memory_space=pltpu.HBM)] * 2,
        out_specs=vmem,
        scratch_shapes=[
            pltpu.VMEM(key_cache.shape, key_cache.dtype),
            pltpu.VMEM(value_cache.shape, value_cache.dtype),
            pltpu.SemaphoreType.DMA((rows // ROW_CHUNK,)),
            pltpu.SemaphoreType.DMA((rows // ROW_CHUNK,)),
            pltpu.VMEM((rows * H, HD), jnp.float32),
            pltpu.VMEM((rows * 2 * KVH, HD), jnp.float32),
            pltpu.VMEM((rows * H, HD), jnp.float32),
        ],
        compiler_params=pltpu.CompilerParams(vmem_limit_bytes=20 * 2**20),
        cost_estimate=pl.CostEstimate(
            flops=4 * rows * H * slots * HD,
            bytes_accessed=2 * (key_cache.size + value_cache.size),
            transcendentals=rows * H * slots,
        ),
    )(device, core, lengths, projected, cosine, sine, in_hbm(key_cache), in_hbm(value_cache))


def down_kernel(core_ref, rotated_ref, source_ref, out_ref, weights_ref, arrived):
    copies = column_copies(source_ref, weights_ref, arrived, DOWN_CHUNK)
    core = core_ref[0]
    rotated = rotated_ref[...]
    features = weights_ref.shape[1]
    width = out_ref.shape[3]
    block = max(width, min(256, features))
    for start in range(0, features, block):
        if start % DOWN_CHUNK == 0:
            copies[start // DOWN_CHUNK].wait()
        part = jnp.dot(
            rotated, weights_ref[:, start : start + block], preferred_element_type=jnp.float32
        ).astype(jnp.bfloat16)
        for offset in range(0, block, width):
            piece = (start + offset) // width
            out_ref[(piece % 2) ^ core, piece // 2] = part[:, offset : offset + width]


def down_pieces(core, rotated, w_down, devices):
    rows, features = rotated.shape[0], w_down.shape[1]
    vmem = pl.BlockSpec(memory_space=pltpu.VMEM)
    return pl.pallas_call(
        down_kernel,
        out_shape=jax.ShapeDtypeStruct((2, devices // 2, rows, features // devices), jnp.bfloat16),
        in_specs=[
            pl.BlockSpec(memory_space=pltpu.SMEM),
            vmem,
            pl.BlockSpec(memory_space=pltpu.HBM),
        ],
        out_specs=vmem,
        scratch_shapes=[
            pltpu.VMEM(w_down.shape, w_down.dtype),
            pltpu.SemaphoreType.DMA((w_down.shape[1] // DOWN_CHUNK,)),
        ],
        compiler_params=pltpu.CompilerParams(vmem_limit_bytes=12 * 2**20),
        cost_estimate=pl.CostEstimate(
            flops=2 * rows * rotated.shape[1] * features,
            bytes_accessed=w_down.size * 2,
            transcendentals=0,
        ),
    )(core, rotated, in_hbm(w_down))


def paley_table():
    prime = 13
    residues = [value * value % prime for value in range(1, prime)]
    conference = np.zeros((prime + 1, prime + 1))
    conference[0, 1:] = 1.0
    conference[1:, 0] = 1.0
    for row_number in range(prime):
        for col_number in range(prime):
            offset = (col_number - row_number) % prime
            if offset != 0:
                conference[row_number + 1, col_number + 1] = 1.0 if offset in residues else -1.0
    first_block = np.array([[1.0, -1.0], [-1.0, -1.0]])
    second_block = np.array([[1.0, 1.0], [1.0, -1.0]])
    return np.kron(conference, first_block) + np.kron(np.eye(prime + 1), second_block)


def sylvester_table(order):
    result = np.ones((1, 1))
    while result.shape[0] < order:
        result = np.kron(np.array([[1.0, 1.0], [1.0, -1.0]]), result)
    return result


def rotary_factors(positions):
    frequency = ROPE_BASE ** (-2.0 * jnp.arange(HD // 2, dtype=jnp.float32) / HD)
    angles = positions.astype(jnp.float32)[:, None] * frequency[None, :]
    cosine, sine = jnp.cos(angles), jnp.sin(angles)
    return jnp.concatenate([cosine, cosine], axis=1), jnp.concatenate([-sine, sine], axis=1)


def per_device(hidden, w_qkv, key_cache, value_cache, lengths, w_out, w_gate, w_up, w_down):
    row_count = hidden.shape[0]
    devices = lax.axis_size("tensor")
    device_index = lax.axis_index("tensor")
    query_width = H * HD
    device = device_index.astype(jnp.int32).reshape(1)
    core = device % 2
    hidden_wide = hidden.astype(jnp.float32)
    blocks = H + 2 * KVH
    rows_used = (blocks + 1) * row_count
    rows_sent = -(-rows_used // (8 * devices)) * 8
    halves = projected_pieces(core, hidden, w_qkv, devices, rows_sent)
    halves, lengths = lax.optimization_barrier((halves, lengths))
    arrived = across(halves[1], 1)
    cosine, sine = rotary_factors(lengths)
    lengths = jnp.broadcast_to(lengths[:, None], (row_count, HD))
    arrived, cosine, sine, lengths = lax.optimization_barrier((arrived, cosine, sine, lengths))
    piece = scattered_joined(halves[0], arrived).astype(jnp.bfloat16)
    projected = gathered(piece)
    projected = projected.reshape(-1, HD)[:rows_used].reshape(blocks + 1, row_count, HD)
    direct = devices == H
    halves = attended_pieces(
        device, core if direct else jnp.zeros_like(core), lengths, projected, cosine, sine, key_cache, value_cache
    )
    if direct:
        parts = scattered_halves(halves[0], halves[1])
        parts, device_index = lax.optimization_barrier((parts, device_index))
        numerators, totals = parts[:row_count], parts[row_count:]
        chosen = jnp.arange(8) == device_index % 8
        totals = jnp.sum(jnp.where(chosen[:, None], totals, 0.0), axis=0)[:row_count]
    else:
        held = H * row_count // devices
        heads = halves.transpose(1, 0, 2, 3).reshape(H, row_count + 8, HD)
        numerators = heads[:, :row_count].reshape(devices, held, HD)
        totals = heads[:, row_count:].reshape(H // 8, 8, 8, HD)
        totals = jnp.einsum("ahhl->ahl", totals).reshape(H, HD)[:, :row_count]
        totals = jnp.pad(totals.reshape(devices, 1, held), ((0, 0), (0, 0), (0, HD - held)))
        parts = scattered_sum(jnp.concatenate([numerators, totals], axis=1))
        numerators, totals = parts[:held], parts[held, :held]
    piece = (numerators / totals[:, None]).astype(jnp.bfloat16)
    attention = gathered(piece).reshape(H, row_count, HD).transpose(1, 0, 2).reshape(row_count, query_width)
    residual = (hidden_wide + jnp.dot(attention, w_out, preferred_element_type=jnp.float32)).astype(
        jnp.bfloat16
    )
    residual_full = gathered(residual).transpose(1, 0, 2).reshape(row_count, D)
    residual_wide = residual_full.astype(jnp.float32)
    normed = (
        residual_wide
        * lax.rsqrt(jnp.mean(residual_wide * residual_wide, axis=1, keepdims=True) + EPSILON)
    ).astype(jnp.bfloat16)
    gate = jnp.dot(normed, w_gate, preferred_element_type=jnp.float32)
    upward = jnp.dot(normed, w_up, preferred_element_type=jnp.float32)
    activation = jax.nn.silu(gate) * upward
    local_width = activation.shape[1]
    local_table = jnp.asarray(
        np.kron(sylvester_table(local_width // 28), paley_table()), dtype=jnp.float32
    )
    mixed = jnp.dot(activation, local_table, precision=lax.Precision.HIGHEST)
    rotated = (signed_sum(mixed) * FF ** (-0.5)).astype(jnp.bfloat16)
    halves = down_pieces(core, rotated, w_down, devices)
    down_share = scattered_halves(halves[0], halves[1])
    return (residual.astype(jnp.float32) + down_share).astype(jnp.bfloat16)


def solution(mesh):
    in_specs = (
        P("groups", "tensor"),
        P("tensor", None),
        P("groups", "tensor", None),
        P("groups", "tensor", None),
        P("groups"),
        P(None, "tensor"),
        P(None, "tensor"),
        P(None, "tensor"),
        P("tensor", None),
    )
    out_specs = P("groups", "tensor")
    return jax.shard_map(
        per_device, mesh=mesh, in_specs=in_specs, out_specs=out_specs, check_vma=False
    )
```

time: 123 us -> 119 us (0.967)
  blocking collectives: 44.7 us -> 80.4 us
  waiting for transfers between devices: 32.1 us -> 11.6 us
  starting transfers between devices: 17.2 us -> 2.03 us
  Pallas kernels: 0 us -> 12.8 us
  matrix products: 19 us -> 8.22 us
  other arithmetic: 5.56 us -> 2.42 us
  local copies, waits for them, and re-layouts: 3.47 us -> 0.96 us
    all_to_all x2 -> x4, blocking collectives: 22.4 us -> 47.3 us  [the longest x3 38.5 us: scattered_joined(): lax.all_to_all(joined.astype(jnp.bfloat16), 'tensor', 0, 0, tiled=True, a...]
    all_to_all x3 -> x0, waiting for transfers between devices: 20.3 us -> none  [the longest x1 7.78 us: scattered_sum(): lax.all_to_all(joined.astype(jnp.bfloat16), 'tensor', 0, 0, tiled=True, a...]
    all_to_all x3 -> x0, starting transfers between devices: 15.1 us -> none  [the longest x1 8.22 us: scattered_sum(): lax.all_to_all(joined.astype(jnp.bfloat16), 'tensor', 0, 0, tiled=True, a...]
    dot_general x5 -> x0, matrix products: 14 us -> none  [the longest x1 4.62 us: per_device(): jnp.einsum('kgrd,rckd->rkgc', grouped, keys_local, preferred_element_type...]
    pallas_call x0 -> x3, Pallas kernels: none -> 12.8 us  [the longest x1 6.72 us: attended_pieces(): pl.pallas_call(attend_kernel, out_shape=jax.ShapeDtypeStruct((2, H // 2,...]
    all_to_all x2 -> x3, blocking collectives: 22.3 us -> 33.1 us  [gathered(): lax.all_to_all(copies, 'tensor', 0, 0, tiled=True, axis_index_groups=same...]
    dot_general x1, matrix products: 2.01 us -> 5.24 us  [per_device(): gate = jnp.dot(normed, w_gate, preferred_element_type=jnp.float32)]
  transfers between devices with their start and end apart: 11 -> 8, of which waited for: 11 -> 8; matrix products, arithmetic and copies ran while one was open for 2% -> 1% of each run, Pallas kernels for 0% -> 0%
where the time goes in v3:
time: 119 us
  blocking collectives  80.4 us (68%)
  Pallas kernels  12.8 us (11%)
  waiting for transfers between devices  11.6 us (10%)
  matrix products  8.22 us (7%)
  other arithmetic  2.42 us (2%)
  starting transfers between devices  2.03 us (2%)
    all_to_all x3, blocking collectives, scattered_joined(): lax.all_to_all(joined.astype(jnp.bfloat16), 'tensor', 0, 0, tiled=True, a...  38.5 us
    all_to_all x3, blocking collectives, gathered(): lax.all_to_all(copies, 'tensor', 0, 0, tiled=True, axis_index_groups=same...  33.1 us
    ppermute x8, waiting for transfers between devices, across(): return lax.ppermute(value, 'tensor', pairs)  11.6 us
    all_to_all x1, blocking collectives, signed_sum(): lax.all_to_all(copies, 'tensor', 0, 0, tiled=True, axis_index_groups=groups)  8.8 us
    pallas_call x1, Pallas kernels, attended_pieces(): pl.pallas_call(attend_kernel, out_shape=jax.ShapeDtypeStruct((2, H // 2,...  6.72 us
    dot_general x1, matrix products, per_device(): gate = jnp.dot(normed, w_gate, preferred_element_type=jnp.float32)  5.24 us
    pallas_call x1, Pallas kernels, down_pieces(): pl.pallas_call(down_kernel, out_shape=jax.ShapeDtypeStruct((2, devices //...  3.48 us
    pallas_call x1, Pallas kernels, projected_pieces(): pl.pallas_call(project_kernel, out_shape=jax.ShapeDtypeStruct((2, devices...  2.63 us
  transfers between devices with their start and end apart: 8, of which 8 were waited for; matrix products, arithmetic and copies ran while one was open for 1% of the time, Pallas kernels for 0%

profile of v3, /device:TPU:0, one launch (start us, length us, event | category | flops | bytes accessed | tf_op | source)
XLA Modules:
  0.0 118.8 jit_solution(17475016100839810499)
XLA Ops:
  0.0 0.0 copy-start
  0.0 2.6 %shard_map.100 = bf16[2,16,32,128]{3,2,1,0:T(8,128)(2,1)S(1)} custom-call(s32[1]{0:T(128)S(6)} %select_n.95.core_ref, bf16[24,256]{1,0:T(8,128)(2,1)} %hidden_source.1, bf16[256,5120]{1,0:T(8,128)(2,1)} %source_ref.2), custom_call_target="tpu_custom_call" | custom-call | flops 62914560 | bytes 2621440 | tf_op jit(solution)/shard_map/pallas_call | solution.py:140
  2.7 0.5 collective-permute-start
  3.2 0.7 convert_element_type.108
  3.9 0.1 fusion.8
  4.0 0.1 pad_maximum_fusion.2
  4.1 0.1 collective-permute-done
  4.2 0.7 broadcast_in_dim.22.lengths_ref
  4.9 15.8 %all_to_all.35 = bf16[16,32,128]{2,1,0:T(8,128)(2,1)S(1)} all-to-all(bf16[16,32,128]{2,1,0:T(8,128)(2,1)S(1)} %fusion.3), channel_id=1, replica_groups={{0,2,4,6,8,10,12,14,16,18,20,22,24,26,28,30},{1,3,5,7,9,11,13,15,17,19,..., dimensions={0} | all-to-all | bytes 262144 | tf_op jit(solution)/shard_map/all_to_all | solution.py:48
  20.8 10.7 %all_to_all.36 = bf16[16,32,128]{2,1,0:T(8,128)(2,1)S(1)} all-to-all(bf16[16,32,128]{2,1,0:T(8,128)(2,1)S(1)} %broadcast_in_dim.23), channel_id=1, replica_groups={{0,2,4,6,8,10,12,14,16,18,20,22,24,26,28,30},{1,3,5,7,9,11,13,15,17,19,..., dimensions={0} | all-to-all | bytes 262144 | tf_op jit(solution)/shard_map/all_to_all | solution.py:57
  31.5 0.0 collective-permute-start.1
  31.5 1.3 %collective-permute-done.1 = bf16[16,32,128]{2,1,0:T(8,128)(2,1)S(1)} collective-permute-done((bf16[16,32,128]{2,1,0:T(8,128)(2,1)S(1)}, bf16[16,32,128]{2,1,0:T(8,128)(2,1)S(1)}, u32[]{:S(2)}, u32[]{:S(2)}) %collective-permute-start.1) | collective-permute-done | bytes 131104 | tf_op jit(solution)/shard_map/ppermute | solution.py:26
  33.0 0.0 copy-start.2
  33.0 6.7 %shard_map.101 = bf16[2,16,32,128]{3,2,1,0:T(8,128)(2,1)S(1)} custom-call(s32[1]{0:T(128)} %bitcast.device_ref, s32[1]{0:T(128)S(6)} %select_n.95.core_ref, s32[24,128]{1,0:T(8,128)S(1)} %broadcast_in_dim.22.lengths_ref, bf16[41,24,128]{2,1,0:T(8,128)(2,1)S(1)} %bitcast.58, f32[24,128]{1,0:T(8,128)S(1)} %get-tuple-element.19.cosine_ref, ...), custom_call_target="tpu_custom_call" | custom-call | flops 100663296 | bytes 12582912 | tf_op jit(solution)/shard_map/pallas_call | solution.py:279
  39.7 0.2 collective-permute-start.2
  39.9 1.2 %collective-permute-done.2 = bf16[16,32,128]{2,1,0:T(8,128)(2,1)S(1)} collective-permute-done((bf16[16,32,128]{2,1,0:T(8,128)(2,1)S(1)}, bf16[16,32,128]{2,1,0:T(8,128)(2,1)S(1)}, u32[]{:S(2)}, u32[]{:S(2)}) %collective-permute-start.2) | collective-permute-done | bytes 131104 | tf_op jit(solution)/shard_map/ppermute | solution.py:26
  41.2 10.6 %all_to_all.37 = bf16[16,32,128]{2,1,0:T(8,128)(2,1)S(1)} all-to-all(bf16[16,32,128]{2,1,0:T(8,128)(2,1)S(1)} %fusion.2), channel_id=1, replica_groups={{0,2,4,6,8,10,12,14,16,18,20,22,24,26,28,30},{1,3,5,7,9,11,13,15,17,19,..., dimensions={0} | all-to-all | bytes 262144 | tf_op jit(solution)/shard_map/all_to_all | solution.py:48
  51.8 0.1 select_reduce_fusion
  51.9 0.1 divide_convert_fusion
  52.0 10.6 %all_to_all.38 = bf16[16,24,128]{2,1,0:T(8,128)(2,1)S(1)} all-to-all(bf16[16,24,128]{2,1,0:T(8,128)(2,1)S(1)} %broadcast_in_dim.26), channel_id=1, replica_groups={{0,2,4,6,8,10,12,14,16,18,20,22,24,26,28,30},{1,3,5,7,9,11,13,15,17,19,..., dimensions={0} | all-to-all | bytes 196608 | tf_op jit(solution)/shard_map/all_to_all | solution.py:57
  62.6 0.0 collective-permute-start.3
  62.6 1.3 %collective-permute-done.3 = bf16[16,24,128]{2,1,0:T(8,128)(2,1)S(1)} collective-permute-done((bf16[16,24,128]{2,1,0:T(8,128)(2,1)S(1)}, bf16[16,24,128]{2,1,0:T(8,128)(2,1)S(1)}, u32[]{:S(2)}, u32[]{:S(2)}) %collective-permute-start.3) | collective-permute-done | bytes 98336 | tf_op jit(solution)/shard_map/ppermute | solution.py:26
  64.0 0.0 copy-done
  64.0 0.0 copy-done.2
  64.0 0.0 slice-start
  64.0 0.4 fusion
  64.4 11.8 %all_to_all.39 = bf16[16,24,256]{2,1,0:T(8,128)(2,1)S(1)} all-to-all(bf16[16,24,256]{2,1,0:T(8,128)(2,1)S(1)} %broadcast_in_dim.27), channel_id=1, replica_groups={{0,2,4,6,8,10,12,14,16,18,20,22,24,26,28,30},{1,3,5,7,9,11,13,15,17,19,..., dimensions={0} | all-to-all | bytes 393216 | tf_op jit(solution)/shard_map/all_to_all | solution.py:57
  76.2 0.0 collective-permute-start.4
  76.2 1.4 %collective-permute-done.4 = bf16[16,24,256]{2,1,0:T(8,128)(2,1)S(1)} collective-permute-done((bf16[16,24,256]{2,1,0:T(8,128)(2,1)S(1)}, bf16[16,24,256]{2,1,0:T(8,128)(2,1)S(1)}, u32[]{:S(2)}, u32[]{:S(2)}) %collective-permute-start.4) | collective-permute-done | bytes 196640 | tf_op jit(solution)/shard_map/ppermute | solution.py:26
  77.7 0.2 multiply_reduce_fusion
  77.9 0.1 maximum_convert_fusion
  78.0 0.1 copy.23
  78.0 0.0 slice-start.1
  78.1 0.0 copy-start.1
  78.1 5.2 %fusion.13 = f32[24,448]{1,0:T(8,128)S(1)} fusion(bf16[8192,448]{0,1:T(8,128)(2,1)} %param.16, f32[24,8192]{1,0:T(8,128)S(1)} %bitcast.61, f32[24]{0:T(128)S(1)} %add_rsqrt_fusion), kind=kOutput, calls=%fused_computation.54 | convolution fusion | flops 176553984 | bytes 8169568 | tf_op jit(solution)/shard_map/dot_general | solution.py:425
  83.3 0.0 slice-done
  83.3 0.0 slice-done.1
  83.3 2.0 %convolution_multiply_fusion = f32[24,448]{1,0:T(8,128)S(1)} fusion(bf16[8192,448]{0,1:T(8,128)(2,1)S(1)} %bitcast.60, f32[24,448]{1,0:T(8,128)S(1)} %fusion.13, f32[24,8192]{1,0:T(8,128)S(1)} %bitcast.62, f32[24]{0:T(128)S(1)} %add_rsqrt_fusion), kind=kOutput, calls=%fused_computation | convolution fusion | flops 176607744 | bytes 8212576 | tf_op jit(solution)/shard_map/dot_general | solution.py:426
  85.4 0.0 copy-done.1
  85.4 0.6 fusion.14
  85.9 0.2 collective-permute-start.5
  86.1 1.1 collective-permute-done.5
  87.2 1.1 collective-permute-start.6
  88.3 3.7 %collective-permute-done.6 = bf16[24,448]{1,0:T(8,128)(2,1)S(1)} collective-permute-done((bf16[24,448]{1,0:T(8,128)(2,1)S(1)}, bf16[24,448]{1,0:T(8,128)(2,1)S(1)}, u32[]{:S(2)}, u32[]{:S(2)}) %collective-permute-start.6) | collective-permute-done | bytes 21536 | tf_op jit(solution)/shard_map/ppermute | solution.py:26
  92.1 8.8 %all_to_all.40 = bf16[8,24,448]{2,1,0:T(8,128)(2,1)S(1)} all-to-all(bf16[8,24,448]{2,1,0:T(8,128)(2,1)S(1)} %broadcast_in_dim.28), channel_id=1, replica_groups={{0,2,4,6,8,10,12,14},{1,3,5,7,9,11,13,15},{16,18,20,22,24,26,28,30},{17..., dimensions={0} | all-to-all | bytes 344064 | tf_op jit(solution)/shard_map/all_to_all | solution.py:81
  100.9 0.1 multiply_reduce_fusion.1
  101.0 3.5 %shard_map.102 = bf16[2,16,24,256]{3,2,1,0:T(8,128)(2,1)S(1)} custom-call(s32[1]{0:T(128)S(6)} %select_n.95.core_ref, bf16[24,448]{1,0:T(8,128)(2,1)S(1)} %multiply_convert_fusion.1.rotated_ref, bf16[448,8192]{1,0:T(8,128)(2,1)} %source_ref.3), custom_call_target="tpu_custom_call" | custom-call | flops 176160768 | bytes 7340032 | tf_op jit(solution)/shard_map/pallas_call | solution.py:323
  104.5 0.1 collective-permute-start.7
  104.6 1.4 %collective-permute-done.7 = bf16[16,24,256]{2,1,0:T(8,128)(2,1)S(1)} collective-permute-done((bf16[16,24,256]{2,1,0:T(8,128)(2,1)S(1)}, bf16[16,24,256]{2,1,0:T(8,128)(2,1)S(1)}, u32[]{:S(2)}, u32[]{:S(2)}) %collective-permute-start.7) | collective-permute-done | bytes 196640 | tf_op jit(solution)/shard_map/ppermute | solution.py:26
  106.0 0.1 fusion.1
  106.1 12.1 %all_to_all.41 = bf16[16,24,256]{2,1,0:T(8,128)(2,1)S(1)} all-to-all(bf16[16,24,256]{2,1,0:T(8,128)(2,1)S(1)} %fusion.1), channel_id=1, replica_groups={{0,2,4,6,8,10,12,14,16,18,20,22,24,26,28,30},{1,3,5,7,9,11,13,15,17,19,..., dimensions={0} | all-to-all | bytes 393216 | tf_op jit(solution)/shard_map/all_to_all | solution.py:48
  118.2 0.6 add_convert_fusion
  (26 shorter events, 0.5 us)
Async XLA Ops:
  0.0 64.0 %copy-start = (bf16[4096,256]{1,0:T(8,128)(2,1)S(1)}, bf16[4096,256]{1,0:T(8,128)(2,1)}, u32[]{:S(2)}) copy-start(bf16[4096,256]{1,0:T(8,128)(2,1)} %param.15) | copy-start | bytes 6291460
  2.7 1.5 %collective-permute-start = (bf16[16,32,128]{2,1,0:T(8,128)(2,1)S(1)}, bf16[16,32,128]{2,1,0:T(8,128)(2,1)S(1)}, u32[]{:S(2)}, u32[]{:S(2)}) collective-permute-start(bf16[16,32,128]{2,1,0:T(8,128)(2,1)S(1)} %slice_bitcast_fusion.4), channel_id=1, source_target_pairs={{0,1},{1,0},{2,3},{3,2},{4,5},{5,4},{6,7},{7,6},{8,9},{9,8},{10,11... | collective-permute-start | bytes 393224 | tf_op jit(solution)/shard_map/ppermute | solution.py:26
  31.5 1.3 %collective-permute-start.1 = (bf16[16,32,128]{2,1,0:T(8,128)(2,1)S(1)}, bf16[16,32,128]{2,1,0:T(8,128)(2,1)S(1)}, u32[]{:S(2)}, u32[]{:S(2)}) collective-permute-start(bf16[16,32,128]{2,1,0:T(8,128)(2,1)S(1)} %all_to_all.36), channel_id=1, source_target_pairs={{0,1},{1,0},{2,3},{3,2},{4,5},{5,4},{6,7},{7,6},{8,9},{9,8},{10,11... | collective-permute-start | bytes 393224 | tf_op jit(solution)/shard_map/ppermute | solution.py:26
  33.0 31.0 %copy-start.2 = (bf16[24,256]{1,0:T(8,128)(2,1)S(1)}, bf16[24,256]{1,0:T(8,128)(2,1)}, u32[]{:S(2)}) copy-start(bf16[24,256]{1,0:T(8,128)(2,1)} %hidden_source.1) | copy-start | bytes 36868
  39.7 1.4 %collective-permute-start.2 = (bf16[16,32,128]{2,1,0:T(8,128)(2,1)S(1)}, bf16[16,32,128]{2,1,0:T(8,128)(2,1)S(1)}, u32[]{:S(2)}, u32[]{:S(2)}) collective-permute-start(bf16[16,32,128]{2,1,0:T(8,128)(2,1)S(1)} %slice_bitcast_fusion.2), channel_id=1, source_target_pairs={{0,1},{1,0},{2,3},{3,2},{4,5},{5,4},{6,7},{7,6},{8,9},{9,8},{10,11... | collective-permute-start | bytes 393224 | tf_op jit(solution)/shard_map/ppermute | solution.py:26
  62.6 1.3 %collective-permute-start.3 = (bf16[16,24,128]{2,1,0:T(8,128)(2,1)S(1)}, bf16[16,24,128]{2,1,0:T(8,128)(2,1)S(1)}, u32[]{:S(2)}, u32[]{:S(2)}) collective-permute-start(bf16[16,24,128]{2,1,0:T(8,128)(2,1)S(1)} %all_to_all.38), channel_id=1, source_target_pairs={{0,1},{1,0},{2,3},{3,2},{4,5},{5,4},{6,7},{7,6},{8,9},{9,8},{10,11... | collective-permute-start | bytes 294920 | tf_op jit(solution)/shard_map/ppermute | solution.py:26
  64.0 19.3 %slice-start = ((s8[7340032]{0:T(1024)(128)(4,1)}), s8[4194304]{0:T(1024)(128)(4,1)S(1)}, s32[]{:S(2)}) async-start(s8[7340032]{0:T(1024)(128)(4,1)} %bitcast.59), calls=%async_computation.7 | async-start | bytes 8388608
  76.2 1.4 %collective-permute-start.4 = (bf16[16,24,256]{2,1,0:T(8,128)(2,1)S(1)}, bf16[16,24,256]{2,1,0:T(8,128)(2,1)S(1)}, u32[]{:S(2)}, u32[]{:S(2)}) collective-permute-start(bf16[16,24,256]{2,1,0:T(8,128)(2,1)S(1)} %all_to_all.39), channel_id=1, source_target_pairs={{0,1},{1,0},{2,3},{3,2},{4,5},{5,4},{6,7},{7,6},{8,9},{9,8},{10,11... | collective-permute-start | bytes 589832 | tf_op jit(solution)/shard_map/ppermute | solution.py:26
  78.0 5.3 %slice-start.1 = ((s8[7340032]{0:T(1024)(128)(4,1)}), s8[3145728]{0:T(1024)(128)(4,1)S(1)}, s32[]{:S(2)}) async-start(s8[7340032]{0:T(1024)(128)(4,1)} %bitcast.59), calls=%async_computation.8 | async-start | bytes 6291456
  78.1 7.3 %copy-start.1 = (f32[448,448]{1,0:T(8,128)S(1)}, f32[448,448]{1,0:T(8,128)}, u32[]{:S(2)}) copy-start(f32[448,448]{1,0:T(8,128)} %constant.118.clone) | copy-start | bytes 2408452
  85.9 1.3 %collective-permute-start.5 = (f32[24,448]{1,0:T(8,128)S(1)}, f32[24,448]{1,0:T(8,128)S(1)}, u32[]{:S(2)}, u32[]{:S(2)}) collective-permute-start(f32[24,448]{1,0:T(8,128)S(1)} %fusion.14), channel_id=1, source_target_pairs={{0,1},{1,0},{2,3},{3,2},{4,5},{5,4},{6,7},{7,6},{8,9},{9,8},{10,11... | collective-permute-start | bytes 129032 | tf_op jit(solution)/shard_map/ppermute | solution.py:26
  87.2 4.8 %collective-permute-start.6 = (bf16[24,448]{1,0:T(8,128)(2,1)S(1)}, bf16[24,448]{1,0:T(8,128)(2,1)S(1)}, u32[]{:S(2)}, u32[]{:S(2)}) collective-permute-start(bf16[24,448]{1,0:T(8,128)(2,1)S(1)} %select_convert_fusion), channel_id=1, source_target_pairs={{0,16},{1,17},{2,18},{3,19},{4,20},{5,21},{6,22},{7,23},{8,24},{9,... | collective-permute-start | bytes 64520 | tf_op jit(solution)/shard_map/ppermute | solution.py:26
  104.5 1.5 %collective-permute-start.7 = (bf16[16,24,256]{2,1,0:T(8,128)(2,1)S(1)}, bf16[16,24,256]{2,1,0:T(8,128)(2,1)S(1)}, u32[]{:S(2)}, u32[]{:S(2)}) collective-permute-start(bf16[16,24,256]{2,1,0:T(8,128)(2,1)S(1)} %slice_bitcast_fusion), channel_id=1, source_target_pairs={{0,1},{1,0},{2,3},{3,2},{4,5},{5,4},{6,7},{7,6},{8,9},{9,8},{10,11... | collective-permute-start | bytes 589832 | tf_op jit(solution)/shard_map/ppermute | solution.py:26

commit v4 on v3

--- a/solution.py
+++ b/solution.py
@@ -15,9 +15,9 @@
 
 EPSILON = 1e-05
 ROPE_BASE = 500000.0
-QKV_CHUNK = 1024
+QKV_CHUNK = 2560
 DOWN_CHUNK = 1024
-ROW_CHUNK = 4
+ROW_CHUNK = 8
 ROWS_AT_ONCE = 8
 
 
@@ -49,6 +49,11 @@
         joined.astype(jnp.bfloat16), "tensor", 0, 0, tiled=True, axis_index_groups=same_core()
     )
     return jnp.sum(received.astype(jnp.float32), axis=0)
+
+
+def gathered_at_once(piece):
+    copies = jnp.broadcast_to(piece[None], (lax.axis_size("tensor"), *piece.shape))
+    return lax.all_to_all(copies, "tensor", 0, 0, tiled=True)
 
 
 def gathered(piece):
@@ -85,6 +90,29 @@
         common = common ^ (common >> shift)
     signs = 1.0 - 2.0 * (common & 1).astype(jnp.float32)
     return jnp.sum(received.astype(jnp.float32) * signs[:, None, None], axis=0)
+
+
+def normalize_kernel(device_ref, parts_ref, out_ref):
+    rows = out_ref.shape[0]
+    shape = (8, HD)
+    chosen = lax.broadcasted_iota(jnp.int32, shape, 0) == device_ref[0] % 8
+    totals = jnp.sum(jnp.where(chosen, parts_ref[rows : rows + 8], 0.0), axis=0, keepdims=True)
+    shape = (rows, HD)
+    own = lax.broadcasted_iota(jnp.int32, shape, 0) == lax.broadcasted_iota(jnp.int32, shape, 1)
+    column = jnp.sum(jnp.where(own, totals, 0.0), axis=1, keepdims=True)
+    out_ref[...] = (parts_ref[:rows] / column).astype(jnp.bfloat16)
+
+
+def normalized(device, parts, rows):
+    vmem = pl.BlockSpec(memory_space=pltpu.VMEM)
+    return pl.pallas_call(
+        normalize_kernel,
+        out_shape=jax.ShapeDtypeStruct((rows, HD), jnp.bfloat16),
+        in_specs=[pl.BlockSpec(memory_space=pltpu.SMEM), vmem],
+        out_specs=vmem,
+        compiler_params=pltpu.CompilerParams(vmem_limit_bytes=2**20),
+        cost_estimate=pl.CostEstimate(flops=10000, bytes_accessed=10000, transcendentals=0),
+    )(device, parts)
 
 
 def in_hbm(value):
@@ -198,6 +226,7 @@
         fresh[pl.ds(KVH + head, rows, stride=2 * KVH), :] = block(H + KVH + head)
 
     lane = lax.broadcasted_iota(jnp.int32, (1, slots), 1) + device * slots
+    lane = lane.astype(jnp.float32)
     row_lane = lax.broadcasted_iota(jnp.int32, (H, HD), 1)
     pair_row = lax.broadcasted_iota(jnp.int32, (2 * group, HD), 0)
     lower = pair_row < group
@@ -367,7 +396,7 @@
 
 def rotary_factors(positions):
     frequency = ROPE_BASE ** (-2.0 * jnp.arange(HD // 2, dtype=jnp.float32) / HD)
-    angles = positions.astype(jnp.float32)[:, None] * frequency[None, :]
+    angles = positions[:, None] * frequency[None, :]
     cosine, sine = jnp.cos(angles), jnp.sin(angles)
     return jnp.concatenate([cosine, cosine], axis=1), jnp.concatenate([-sine, sine], axis=1)
 
@@ -386,8 +415,9 @@
     halves = projected_pieces(core, hidden, w_qkv, devices, rows_sent)
     halves, lengths = lax.optimization_barrier((halves, lengths))
     arrived = across(halves[1], 1)
-    cosine, sine = rotary_factors(lengths)
-    lengths = jnp.broadcast_to(lengths[:, None], (row_count, HD))
+    positions = lax.optimization_barrier(lengths.astype(jnp.float32))
+    cosine, sine = rotary_factors(positions)
+    lengths = jnp.broadcast_to(positions[:, None], (row_count, HD))
     arrived, cosine, sine, lengths = lax.optimization_barrier((arrived, cosine, sine, lengths))
     piece = scattered_joined(halves[0], arrived).astype(jnp.bfloat16)
     projected = gathered(piece)
@@ -399,9 +429,7 @@
     if direct:
         parts = scattered_halves(halves[0], halves[1])
         parts, device_index = lax.optimization_barrier((parts, device_index))
-        numerators, totals = parts[:row_count], parts[row_count:]
-        chosen = jnp.arange(8) == device_index % 8
-        totals = jnp.sum(jnp.where(chosen[:, None], totals, 0.0), axis=0)[:row_count]
+        piece = normalized(device, parts, row_count)
     else:
         held = H * row_count // devices
         heads = halves.transpose(1, 0, 2, 3).reshape(H, row_count + 8, HD)
@@ -410,9 +438,8 @@
         totals = jnp.einsum("ahhl->ahl", totals).reshape(H, HD)[:, :row_count]
         totals = jnp.pad(totals.reshape(devices, 1, held), ((0, 0), (0, 0), (0, HD - held)))
         parts = scattered_sum(jnp.concatenate([numerators, totals], axis=1))
-        numerators, totals = parts[:held], parts[held, :held]
-    piece = (numerators / totals[:, None]).astype(jnp.bfloat16)
-    attention = gathered(piece).reshape(H, row_count, HD).transpose(1, 0, 2).reshape(row_count, query_width)
+        piece = (parts[:held] / parts[held, :held][:, None]).astype(jnp.bfloat16)
+    attention = gathered_at_once(piece).reshape(H, row_count, HD).transpose(1, 0, 2).reshape(row_count, query_width)
     residual = (hidden_wide + jnp.dot(attention, w_out, preferred_element_type=jnp.float32)).astype(
         jnp.bfloat16
     )
@@ -429,7 +456,7 @@
     local_table = jnp.asarray(
         np.kron(sylvester_table(local_width // 28), paley_table()), dtype=jnp.float32
     )
-    mixed = jnp.dot(activation, local_table, precision=lax.Precision.HIGHEST)
+    mixed = jnp.dot(activation, local_table, precision=lax.Precision.HIGH)
     rotated = (signed_sum(mixed) * FF ** (-0.5)).astype(jnp.bfloat16)
     halves = down_pieces(core, rotated, w_down, devices)
     down_share = scattered_halves(halves[0], halves[1])

time: 119 us -> 113 us (0.950)
  matrix products: 8.22 us -> 4.77 us
  waiting for transfers between devices: 11.6 us -> 10.3 us
    all_to_all x0 -> x1, blocking collectives: none -> 10.8 us  [gathered_at_once(): return lax.all_to_all(copies, 'tensor', 0, 0, tiled=True)]
    all_to_all x3 -> x2, blocking collectives: 33.1 us -> 23 us  [gathered(): lax.all_to_all(copies, 'tensor', 0, 0, tiled=True, axis_index_groups=same...]
    dot_general x1, matrix products: 5.24 us -> 2 us  [per_device(): gate = jnp.dot(normed, w_gate, preferred_element_type=jnp.float32)]
    ppermute x8 -> x7, waiting for transfers between devices: 11.6 us -> 10.3 us  [across(): return lax.ppermute(value, 'tensor', pairs)]
  transfers between devices with their start and end apart: 8 -> 7, of which waited for: 8 -> 7; matrix products, arithmetic and copies ran while one was open for 1% -> 1% of each run, Pallas kernels for 0% -> 0%
where the time goes in v4:
time: 113 us
  blocking collectives  81.1 us (72%)
  Pallas kernels  11.9 us (11%)
  waiting for transfers between devices  10.3 us (9%)
  matrix products  4.77 us (4%)
  other arithmetic  2.21 us (2%)
  starting transfers between devices  2.08 us (2%)
    all_to_all x3, blocking collectives, scattered_joined(): lax.all_to_all(joined.astype(jnp.bfloat16), 'tensor', 0, 0, tiled=True, a...  38.5 us
    all_to_all x2, blocking collectives, gathered(): lax.all_to_all(copies, 'tensor', 0, 0, tiled=True, axis_index_groups=same...  23 us
    all_to_all x1, blocking collectives, gathered_at_once(): return lax.all_to_all(copies, 'tensor', 0, 0, tiled=True)  10.8 us
    ppermute x7, waiting for transfers between devices, across(): return lax.ppermute(value, 'tensor', pairs)  10.3 us
    all_to_all x1, blocking collectives, signed_sum(): lax.all_to_all(copies, 'tensor', 0, 0, tiled=True, axis_index_groups=groups)  8.78 us
    pallas_call x1, Pallas kernels, attended_pieces(): pl.pallas_call(attend_kernel, out_shape=jax.ShapeDtypeStruct((2, H // 2,...  6.06 us
    pallas_call x1, Pallas kernels, down_pieces(): pl.pallas_call(down_kernel, out_shape=jax.ShapeDtypeStruct((2, devices //...  3.48 us
  transfers between devices with their start and end apart: 7, of which 7 were waited for; matrix products, arithmetic and copies ran while one was open for 1% of the time, Pallas kernels for 0%

profile of v4, /device:TPU:0, one launch (start us, length us, event | category | flops | bytes accessed | tf_op | source)
XLA Modules:
  0.0 112.9 jit_solution(7803118311322401056)
XLA Ops:
  0.0 0.0 copy-start
  0.0 2.2 %shard_map.100 = bf16[2,16,32,128]{3,2,1,0:T(8,128)(2,1)S(1)} custom-call(s32[1]{0:T(128)S(6)} %select_n.71.core_ref, bf16[24,256]{1,0:T(8,128)(2,1)} %hidden_source.1, bf16[256,5120]{1,0:T(8,128)(2,1)} %source_ref.2), custom_call_target="tpu_custom_call" | custom-call | flops 62914560 | bytes 2621440 | tf_op jit(solution)/shard_map/pallas_call | solution.py:168
  2.3 0.5 collective-permute-start
  2.8 0.7 convert_element_type.105
  3.5 0.1 fusion.8
  3.6 0.1 pad_maximum_fusion.1
  3.7 0.1 collective-permute-done
  3.8 0.1 broadcast_in_dim.10.lengths_ref
  3.9 15.8 %all_to_all.35 = bf16[16,32,128]{2,1,0:T(8,128)(2,1)S(1)} all-to-all(bf16[16,32,128]{2,1,0:T(8,128)(2,1)S(1)} %fusion.3), channel_id=1, replica_groups={{0,2,4,6,8,10,12,14,16,18,20,22,24,26,28,30},{1,3,5,7,9,11,13,15,17,19,..., dimensions={0} | all-to-all | bytes 262144 | tf_op jit(solution)/shard_map/all_to_all | solution.py:48
  19.8 10.7 %all_to_all.36 = bf16[16,32,128]{2,1,0:T(8,128)(2,1)S(1)} all-to-all(bf16[16,32,128]{2,1,0:T(8,128)(2,1)S(1)} %broadcast_in_dim.11), channel_id=1, replica_groups={{0,2,4,6,8,10,12,14,16,18,20,22,24,26,28,30},{1,3,5,7,9,11,13,15,17,19,..., dimensions={0} | all-to-all | bytes 262144 | tf_op jit(solution)/shard_map/all_to_all | solution.py:62
  30.5 0.0 collective-permute-start.1
  30.5 1.3 %collective-permute-done.1 = bf16[16,32,128]{2,1,0:T(8,128)(2,1)S(1)} collective-permute-done((bf16[16,32,128]{2,1,0:T(8,128)(2,1)S(1)}, bf16[16,32,128]{2,1,0:T(8,128)(2,1)S(1)}, u32[]{:S(2)}, u32[]{:S(2)}) %collective-permute-start.1) | collective-permute-done | bytes 131104 | tf_op jit(solution)/shard_map/ppermute | solution.py:26
  31.9 0.0 slice-start
  31.9 0.0 copy-start.2
  31.9 0.0 slice-start.1
  31.9 6.1 %shard_map.101 = bf16[2,16,32,128]{3,2,1,0:T(8,128)(2,1)S(1)} custom-call(s32[1]{0:T(128)} %bitcast.device_ref, s32[1]{0:T(128)S(6)} %select_n.71.core_ref, f32[24,128]{1,0:T(8,128)S(1)} %broadcast_in_dim.10.lengths_ref, bf16[41,24,128]{2,1,0:T(8,128)(2,1)S(1)} %bitcast.52, f32[24,128]{1,0:T(8,128)S(1)} %get-tuple-element.18.cosine_ref, ...), custom_call_target="tpu_custom_call" | custom-call | flops 100663296 | bytes 12582912 | tf_op jit(solution)/shard_map/pallas_call | solution.py:308
  38.0 0.2 collective-permute-start.2
  38.2 1.2 %collective-permute-done.2 = bf16[16,32,128]{2,1,0:T(8,128)(2,1)S(1)} collective-permute-done((bf16[16,32,128]{2,1,0:T(8,128)(2,1)S(1)}, bf16[16,32,128]{2,1,0:T(8,128)(2,1)S(1)}, u32[]{:S(2)}, u32[]{:S(2)}) %collective-permute-start.2) | collective-permute-done | bytes 131104 | tf_op jit(solution)/shard_map/ppermute | solution.py:26
  39.5 10.6 %all_to_all.37 = bf16[16,32,128]{2,1,0:T(8,128)(2,1)S(1)} all-to-all(bf16[16,32,128]{2,1,0:T(8,128)(2,1)S(1)} %fusion.2), channel_id=1, replica_groups={{0,2,4,6,8,10,12,14,16,18,20,22,24,26,28,30},{1,3,5,7,9,11,13,15,17,19,..., dimensions={0} | all-to-all | bytes 262144 | tf_op jit(solution)/shard_map/all_to_all | solution.py:48
  50.1 0.1 shard_map.102
  50.3 10.8 %all_to_all.38 = bf16[32,24,128]{2,1,0:T(8,128)(2,1)S(1)} all-to-all(bf16[32,24,128]{2,1,0:T(8,128)(2,1)S(1)} %broadcast_in_dim.12), channel_id=1, replica_groups=mesh['groups'=1,'tensor'=32] {'tensor'}, dimensions={0} | all-to-all | bytes 393216 | tf_op jit(solution)/shard_map/all_to_all | solution.py:56
  61.1 0.0 copy-done
  61.1 0.0 copy-done.2
  61.1 0.0 slice-start.2
  61.1 0.4 fusion
  61.5 12.3 %all_to_all.39 = bf16[16,24,256]{2,1,0:T(8,128)(2,1)S(1)} all-to-all(bf16[16,24,256]{2,1,0:T(8,128)(2,1)S(1)} %broadcast_in_dim.13), channel_id=1, replica_groups={{0,2,4,6,8,10,12,14,16,18,20,22,24,26,28,30},{1,3,5,7,9,11,13,15,17,19,..., dimensions={0} | all-to-all | bytes 393216 | tf_op jit(solution)/shard_map/all_to_all | solution.py:62
  73.7 0.0 collective-permute-start.3
  73.7 1.4 %collective-permute-done.3 = bf16[16,24,256]{2,1,0:T(8,128)(2,1)S(1)} collective-permute-done((bf16[16,24,256]{2,1,0:T(8,128)(2,1)S(1)}, bf16[16,24,256]{2,1,0:T(8,128)(2,1)S(1)}, u32[]{:S(2)}, u32[]{:S(2)}) %collective-permute-start.3) | collective-permute-done | bytes 196640 | tf_op jit(solution)/shard_map/ppermute | solution.py:26
  75.2 0.2 multiply_reduce_fusion
  75.4 0.1 maximum_convert_fusion
  75.5 0.1 copy.24
  75.6 0.0 slice-done
  75.6 0.0 slice-done.1
  75.6 0.0 slice-start.3
  75.6 0.0 copy-start.1
  75.6 2.0 %fusion.13 = f32[24,448]{1,0:T(8,128)S(1)} fusion(bf16[8192,448]{0,1:T(8,128)(2,1)S(1)} %bitcast.54, f32[24,8192]{1,0:T(8,128)S(1)} %bitcast.57, f32[24]{0:T(128)S(1)} %add_rsqrt_fusion), kind=kOutput, calls=%fused_computation.48 | convolution fusion | flops 176553984 | bytes 8169568 | tf_op jit(solution)/shard_map/dot_general | solution.py:452
  77.7 0.0 slice-done.2
  77.7 0.0 slice-done.3
  77.7 2.0 %convolution_multiply_fusion = f32[24,448]{1,0:T(8,128)S(1)} fusion(bf16[8192,448]{0,1:T(8,128)(2,1)S(1)} %bitcast.56, f32[24,448]{1,0:T(8,128)S(1)} %fusion.13, f32[24,8192]{1,0:T(8,128)S(1)} %bitcast.58, f32[24]{0:T(128)S(1)} %add_rsqrt_fusion), kind=kOutput, calls=%fused_computation | convolution fusion | flops 176607744 | bytes 8212576 | tf_op jit(solution)/shard_map/dot_general | solution.py:453
  79.7 0.0 copy-done.1
  79.7 0.3 fusion.14
  80.1 0.2 collective-permute-start.4
  80.2 1.1 collective-permute-done.4
  81.3 1.1 collective-permute-start.5
  82.4 3.7 %collective-permute-done.5 = bf16[24,448]{1,0:T(8,128)(2,1)S(1)} collective-permute-done((bf16[24,448]{1,0:T(8,128)(2,1)S(1)}, bf16[24,448]{1,0:T(8,128)(2,1)S(1)}, u32[]{:S(2)}, u32[]{:S(2)}) %collective-permute-start.5) | collective-permute-done | bytes 21536 | tf_op jit(solution)/shard_map/ppermute | solution.py:26
  86.2 8.8 %all_to_all.40 = bf16[8,24,448]{2,1,0:T(8,128)(2,1)S(1)} all-to-all(bf16[8,24,448]{2,1,0:T(8,128)(2,1)S(1)} %broadcast_in_dim.14), channel_id=1, replica_groups={{0,2,4,6,8,10,12,14},{1,3,5,7,9,11,13,15},{16,18,20,22,24,26,28,30},{17..., dimensions={0} | all-to-all | bytes 344064 | tf_op jit(solution)/shard_map/all_to_all | solution.py:86
  95.0 0.1 multiply_reduce_fusion.1
  95.1 3.5 %shard_map.103 = bf16[2,16,24,256]{3,2,1,0:T(8,128)(2,1)S(1)} custom-call(s32[1]{0:T(128)S(6)} %select_n.71.core_ref, bf16[24,448]{1,0:T(8,128)(2,1)S(1)} %multiply_convert_fusion.1.rotated_ref, bf16[448,8192]{1,0:T(8,128)(2,1)} %source_ref.3), custom_call_target="tpu_custom_call" | custom-call | flops 176160768 | bytes 7340032 | tf_op jit(solution)/shard_map/pallas_call | solution.py:352
  98.6 0.1 collective-permute-start.6
  98.7 1.4 %collective-permute-done.6 = bf16[16,24,256]{2,1,0:T(8,128)(2,1)S(1)} collective-permute-done((bf16[16,24,256]{2,1,0:T(8,128)(2,1)S(1)}, bf16[16,24,256]{2,1,0:T(8,128)(2,1)S(1)}, u32[]{:S(2)}, u32[]{:S(2)}) %collective-permute-start.6) | collective-permute-done | bytes 196640 | tf_op jit(solution)/shard_map/ppermute | solution.py:26
  100.1 0.1 fusion.1
  100.2 12.1 %all_to_all.41 = bf16[16,24,256]{2,1,0:T(8,128)(2,1)S(1)} all-to-all(bf16[16,24,256]{2,1,0:T(8,128)(2,1)S(1)} %fusion.1), channel_id=1, replica_groups={{0,2,4,6,8,10,12,14,16,18,20,22,24,26,28,30},{1,3,5,7,9,11,13,15,17,19,..., dimensions={0} | all-to-all | bytes 393216 | tf_op jit(solution)/shard_map/all_to_all | solution.py:48
  112.3 0.6 add_convert_fusion
  (24 shorter events, 0.4 us)
Async XLA Ops:
  0.0 61.1 %copy-start = (bf16[4096,256]{1,0:T(8,128)(2,1)S(1)}, bf16[4096,256]{1,0:T(8,128)(2,1)}, u32[]{:S(2)}) copy-start(bf16[4096,256]{1,0:T(8,128)(2,1)} %param.15) | copy-start | bytes 6291460
  2.3 1.5 %collective-permute-start = (bf16[16,32,128]{2,1,0:T(8,128)(2,1)S(1)}, bf16[16,32,128]{2,1,0:T(8,128)(2,1)S(1)}, u32[]{:S(2)}, u32[]{:S(2)}) collective-permute-start(bf16[16,32,128]{2,1,0:T(8,128)(2,1)S(1)} %slice_bitcast_fusion.4), channel_id=1, source_target_pairs={{0,1},{1,0},{2,3},{3,2},{4,5},{5,4},{6,7},{7,6},{8,9},{9,8},{10,11... | collective-permute-start | bytes 393224 | tf_op jit(solution)/shard_map/ppermute | solution.py:26
  30.5 1.3 %collective-permute-start.1 = (bf16[16,32,128]{2,1,0:T(8,128)(2,1)S(1)}, bf16[16,32,128]{2,1,0:T(8,128)(2,1)S(1)}, u32[]{:S(2)}, u32[]{:S(2)}) collective-permute-start(bf16[16,32,128]{2,1,0:T(8,128)(2,1)S(1)} %all_to_all.36), channel_id=1, source_target_pairs={{0,1},{1,0},{2,3},{3,2},{4,5},{5,4},{6,7},{7,6},{8,9},{9,8},{10,11... | collective-permute-start | bytes 393224 | tf_op jit(solution)/shard_map/ppermute | solution.py:26
  31.9 43.7 %slice-start = ((s8[7340032]{0:T(1024)(128)(4,1)}), s8[4194304]{0:T(1024)(128)(4,1)S(1)}, s32[]{:S(2)}) async-start(s8[7340032]{0:T(1024)(128)(4,1)} %bitcast.53), calls=%async_computation.7 | async-start | bytes 8388608
  31.9 29.1 %copy-start.2 = (bf16[24,256]{1,0:T(8,128)(2,1)S(1)}, bf16[24,256]{1,0:T(8,128)(2,1)}, u32[]{:S(2)}) copy-start(bf16[24,256]{1,0:T(8,128)(2,1)} %hidden_source.1) | copy-start | bytes 36868
  31.9 43.7 %slice-start.1 = ((s8[7340032]{0:T(1024)(128)(4,1)}), s8[3145728]{0:T(1024)(128)(4,1)S(1)}, s32[]{:S(2)}) async-start(s8[7340032]{0:T(1024)(128)(4,1)} %bitcast.53), calls=%async_computation.8 | async-start | bytes 6291456
  38.0 1.4 %collective-permute-start.2 = (bf16[16,32,128]{2,1,0:T(8,128)(2,1)S(1)}, bf16[16,32,128]{2,1,0:T(8,128)(2,1)S(1)}, u32[]{:S(2)}, u32[]{:S(2)}) collective-permute-start(bf16[16,32,128]{2,1,0:T(8,128)(2,1)S(1)} %slice_bitcast_fusion.2), channel_id=1, source_target_pairs={{0,1},{1,0},{2,3},{3,2},{4,5},{5,4},{6,7},{7,6},{8,9},{9,8},{10,11... | collective-permute-start | bytes 393224 | tf_op jit(solution)/shard_map/ppermute | solution.py:26
  61.1 16.6 %slice-start.2 = ((s8[7340032]{0:T(1024)(128)(4,1)}), s8[4194304]{0:T(1024)(128)(4,1)S(1)}, s32[]{:S(2)}) async-start(s8[7340032]{0:T(1024)(128)(4,1)} %bitcast.55), calls=%async_computation.9 | async-start | bytes 8388608
  73.7 1.4 %collective-permute-start.3 = (bf16[16,24,256]{2,1,0:T(8,128)(2,1)S(1)}, bf16[16,24,256]{2,1,0:T(8,128)(2,1)S(1)}, u32[]{:S(2)}, u32[]{:S(2)}) collective-permute-start(bf16[16,24,256]{2,1,0:T(8,128)(2,1)S(1)} %all_to_all.39), channel_id=1, source_target_pairs={{0,1},{1,0},{2,3},{3,2},{4,5},{5,4},{6,7},{7,6},{8,9},{9,8},{10,11... | collective-permute-start | bytes 589832 | tf_op jit(solution)/shard_map/ppermute | solution.py:26
  75.6 2.1 %slice-start.3 = ((s8[7340032]{0:T(1024)(128)(4,1)}), s8[3145728]{0:T(1024)(128)(4,1)S(1)}, s32[]{:S(2)}) async-start(s8[7340032]{0:T(1024)(128)(4,1)} %bitcast.55), calls=%async_computation.10 | async-start | bytes 6291456
  75.6 4.1 %copy-start.1 = (f32[448,448]{1,0:T(8,128)S(1)}, f32[448,448]{1,0:T(8,128)}, u32[]{:S(2)}) copy-start(f32[448,448]{1,0:T(8,128)} %constant.112.clone) | copy-start | bytes 2408452
  80.1 1.3 %collective-permute-start.4 = (f32[24,448]{1,0:T(8,128)S(1)}, f32[24,448]{1,0:T(8,128)S(1)}, u32[]{:S(2)}, u32[]{:S(2)}) collective-permute-start(f32[24,448]{1,0:T(8,128)S(1)} %fusion.14), channel_id=1, source_target_pairs={{0,1},{1,0},{2,3},{3,2},{4,5},{5,4},{6,7},{7,6},{8,9},{9,8},{10,11... | collective-permute-start | bytes 129032 | tf_op jit(solution)/shard_map/ppermute | solution.py:26
  81.3 4.8 %collective-permute-start.5 = (bf16[24,448]{1,0:T(8,128)(2,1)S(1)}, bf16[24,448]{1,0:T(8,128)(2,1)S(1)}, u32[]{:S(2)}, u32[]{:S(2)}) collective-permute-start(bf16[24,448]{1,0:T(8,128)(2,1)S(1)} %select_convert_fusion), channel_id=1, source_target_pairs={{0,16},{1,17},{2,18},{3,19},{4,20},{5,21},{6,22},{7,23},{8,24},{9,... | collective-permute-start | bytes 64520 | tf_op jit(solution)/shard_map/ppermute | solution.py:26
  98.6 1.5 %collective-permute-start.6 = (bf16[16,24,256]{2,1,0:T(8,128)(2,1)S(1)}, bf16[16,24,256]{2,1,0:T(8,128)(2,1)S(1)}, u32[]{:S(2)}, u32[]{:S(2)}) collective-permute-start(bf16[16,24,256]{2,1,0:T(8,128)(2,1)S(1)} %slice_bitcast_fusion), channel_id=1, source_target_pairs={{0,1},{1,0},{2,3},{3,2},{4,5},{5,4},{6,7},{7,6},{8,9},{9,8},{10,11... | collective-permute-start | bytes 589832 | tf_op jit(solution)/shard_map/ppermute | solution.py:26

commit v5 on v4

--- a/solution.py
+++ b/solution.py
@@ -18,7 +18,6 @@
 QKV_CHUNK = 2560
 DOWN_CHUNK = 1024
 ROW_CHUNK = 8
-ROWS_AT_ONCE = 8
 
 
 def across(value, apart):
@@ -56,10 +55,14 @@
     return lax.all_to_all(copies, "tensor", 0, 0, tiled=True)
 
 
+def gathered_same_core(piece):
+    copies = jnp.broadcast_to(piece[None], (lax.axis_size("tensor") // 2, *piece.shape))
+    return lax.all_to_all(copies, "tensor", 0, 0, tiled=True, axis_index_groups=same_core())
+
+
 def gathered(piece):
     second = lax.axis_index("tensor") % 2 == 1
-    copies = jnp.broadcast_to(piece[None], (lax.axis_size("tensor") // 2, *piece.shape))
-    mine = lax.all_to_all(copies, "tensor", 0, 0, tiled=True, axis_index_groups=same_core())
+    mine = gathered_same_core(piece)
     theirs = across(mine, 1)
     both = jnp.stack([jnp.where(second, theirs, mine), jnp.where(second, mine, theirs)], axis=1)
     return both.reshape(-1, *piece.shape)
@@ -95,7 +98,7 @@
 def normalize_kernel(device_ref, parts_ref, out_ref):
     rows = out_ref.shape[0]
     shape = (8, HD)
-    chosen = lax.broadcasted_iota(jnp.int32, shape, 0) == device_ref[0] % 8
+    chosen = lax.broadcasted_iota(jnp.int32, shape, 0) == device_ref[0] // 2 % 8
     totals = jnp.sum(jnp.where(chosen, parts_ref[rows : rows + 8], 0.0), axis=0, keepdims=True)
     shape = (rows, HD)
     own = lax.broadcasted_iota(jnp.int32, shape, 0) == lax.broadcasted_iota(jnp.int32, shape, 1)
@@ -145,22 +148,37 @@
     hidden = hidden_ref[...]
     wide = hidden.astype(jnp.float32)
     squares = jnp.sum(wide * wide, axis=1, keepdims=True)
+    half = stacked.shape[0] // 2
+    heads = H // 2
+    fresh = KVH // 2
+
+    def place(block):
+        if block < H:
+            return block // heads * half + block % heads * rows
+        block -= H
+        kind, head = block // KVH, block % KVH
+        return head // fresh * half + (heads + kind * fresh + head % fresh) * rows
+
     for start in range(0, columns, 2 * HD):
         if start % QKV_CHUNK == 0:
             copies[start // QKV_CHUNK].wait()
         part = jnp.dot(
             hidden, weights_ref[:, start : start + 2 * HD], preferred_element_type=jnp.float32
         )
-        first = start // HD * rows
-        stacked[first : first + rows] = part[:, :HD]
-        stacked[first + rows : first + 2 * rows] = part[:, HD:]
-    used = columns // HD * rows
-    stacked[used : used + rows] = jnp.broadcast_to(squares, (rows, HD))
-    stacked[used + rows :] = jnp.zeros((stacked.shape[0] - used - rows, HD), jnp.float32)
+        for offset in range(2):
+            first = place(start // HD + offset)
+            stacked[first : first + rows] = part[:, offset * HD : (offset + 1) * HD]
     held = out_ref.shape[2]
-    for piece in range(stacked.shape[0] // held):
-        values = stacked[piece * held : (piece + 1) * held].astype(jnp.bfloat16)
-        out_ref[(piece % 2) ^ core, piece // 2] = values
+    for pair in range(2):
+        used = pair * half + (heads + 2 * fresh) * rows
+        stacked[used : used + rows] = jnp.broadcast_to(squares, (rows, HD))
+        left = (pair + 1) * half - used - rows
+        if left:
+            stacked[used + rows : used + rows + left] = jnp.zeros((left, HD), jnp.float32)
+        for piece in range(half // held):
+            first = pair * half + piece * held
+            values = stacked[first : first + held].astype(jnp.bfloat16)
+            out_ref[pair ^ core ^ 1, piece] = values
 
 
 def projected_pieces(core, hidden, w_qkv, devices, rows_sent):
@@ -189,26 +207,32 @@
 
 
 def attend_kernel(
-    device_ref, core_ref, lengths_ref, projected_ref, cosine_ref, sine_ref, key_source, value_source,
+    device_ref, pair_ref, lengths_ref, projected_ref, cosine_ref, sine_ref, key_source, value_source,
     out_ref, keys_ref, values_ref, keys_arrived, values_arrived, queries, fresh, sums,
 ):
-    rows, slots = keys_ref.shape[0], keys_ref.shape[1]
+    rows, slots, width = keys_ref.shape
+    columns = pl.ds(pl.multiple_of(pair_ref[0] * width, width), width)
 
     def copies(index):
         part = pl.ds(index * ROW_CHUNK, ROW_CHUNK)
         return (
-            pltpu.make_async_copy(key_source.at[part], keys_ref.at[part], keys_arrived.at[index]),
-            pltpu.make_async_copy(value_source.at[part], values_ref.at[part], values_arrived.at[index]),
+            pltpu.make_async_copy(
+                key_source.at[part, :, columns], keys_ref.at[part], keys_arrived.at[index]
+            ),
+            pltpu.make_async_copy(
+                value_source.at[part, :, columns], values_ref.at[part], values_arrived.at[index]
+            ),
         )
 
     for index in range(rows // ROW_CHUNK):
         for copy in copies(index):
             copy.start()
-    device, core = device_ref[0], core_ref[0]
+    device = device_ref[0]
     group = H // KVH
+    heads = 2 * group
     scale = HD ** (-0.5)
     cosine, sine = cosine_ref[...], sine_ref[...]
-    inverse = lax.rsqrt(projected_ref[H + 2 * KVH].astype(jnp.float32) / D + EPSILON)
+    inverse = lax.rsqrt(projected_ref[heads + 4].astype(jnp.float32) / D + EPSILON)
 
     def block(index):
         value = projected_ref[index].astype(jnp.float32) * inverse
@@ -219,113 +243,94 @@
         value = value * cosine + pltpu.roll(value, HD // 2, 1) * sine
         return value.astype(jnp.bfloat16).astype(jnp.float32)
 
-    for head in range(H):
-        queries[pl.ds(head, rows, stride=H), :] = turned(head)
-    for head in range(KVH):
-        fresh[pl.ds(head, rows, stride=2 * KVH), :] = turned(H + head)
-        fresh[pl.ds(KVH + head, rows, stride=2 * KVH), :] = block(H + KVH + head)
+    for head in range(heads):
+        queries[pl.ds(head, rows, stride=heads), :] = turned(head)
+    for head in range(2):
+        fresh[pl.ds(head, rows, stride=4), :] = turned(heads + head)
+        fresh[pl.ds(2 + head, rows, stride=4), :] = block(heads + 2 + head)
 
     lane = lax.broadcasted_iota(jnp.int32, (1, slots), 1) + device * slots
     lane = lane.astype(jnp.float32)
-    row_lane = lax.broadcasted_iota(jnp.int32, (H, HD), 1)
-    pair_row = lax.broadcasted_iota(jnp.int32, (2 * group, HD), 0)
-    lower = pair_row < group
-    pairs = KVH // 2
+    row_lane = lax.broadcasted_iota(jnp.int32, (heads, HD), 1)
+    lower = lax.broadcasted_iota(jnp.int32, (heads, HD), 0) < group
 
     def expand(first):
-        picked = [
-            jnp.broadcast_to(fresh[pl.ds(first + head, 1), :], (group, HD)) for head in range(KVH)
-        ]
+        picked = [jnp.broadcast_to(fresh[pl.ds(first + head, 1), :], (group, HD)) for head in range(2)]
         return jnp.concatenate(picked, axis=0)
 
-    def some_rows(step, totals, count):
-        numbers = [step * count + offset for offset in range(count)]
+    def some_rows(step, totals):
+        numbers = [step * ROW_CHUNK + offset for offset in range(ROW_CHUNK)]
         scores = []
         own = []
-        for offset, row in enumerate(numbers):
-            if offset % ROW_CHUNK == 0:
-                copies(step * (count // ROW_CHUNK) + offset // ROW_CHUNK)[0].wait()
-            query = queries[pl.ds(pl.multiple_of(row * H, H), H), :]
-            own_score = jnp.sum(query * expand(row * 2 * KVH), axis=1, keepdims=True) * scale
+        copies(step)[0].wait()
+        for row in numbers:
+            query = queries[pl.ds(pl.multiple_of(row * heads, heads), heads), :]
+            own_score = jnp.sum(query * expand(row * 4), axis=1, keepdims=True) * scale
             own.append(jnp.where(device == 0, jnp.exp(own_score), 0.0))
-            parts = []
-            for pair in range(pairs):
-                chosen = query[pair * 2 * group : (pair + 1) * 2 * group]
-                spread = jnp.concatenate(
-                    [jnp.where(lower, chosen, 0.0), jnp.where(lower, 0.0, chosen)], axis=1
-                ).astype(jnp.bfloat16)
-                parts.append(
-                    lax.dot_general(
-                        spread,
-                        keys_ref[row, :, pair * 2 * HD : (pair + 1) * 2 * HD],
-                        (((1,), (1,)), ((), ())),
-                        preferred_element_type=jnp.float32,
-                    )
+            spread = jnp.concatenate(
+                [jnp.where(lower, query, 0.0), jnp.where(lower, 0.0, query)], axis=1
+            ).astype(jnp.bfloat16)
+            scores.append(
+                lax.dot_general(
+                    spread,
+                    keys_ref[row],
+                    (((1,), (1,)), ((), ())),
+                    preferred_element_type=jnp.float32,
                 )
-            scores.append(jnp.concatenate(parts, axis=0))
+            )
         weights = [
             jnp.where(lane < lengths_ref[pl.ds(row, 1), :1], jnp.exp(score * scale), 0.0)
             for row, score in zip(numbers, scores)
         ]
-        for offset, (row, weight, own_weight) in enumerate(zip(numbers, weights, own)):
-            if offset % ROW_CHUNK == 0:
-                copies(step * (count // ROW_CHUNK) + offset // ROW_CHUNK)[1].wait()
-            rounded = weight.astype(jnp.bfloat16)
-            parts = []
-            for pair in range(pairs):
-                product = jnp.dot(
-                    rounded[pair * 2 * group : (pair + 1) * 2 * group],
-                    values_ref[row, :, pair * 2 * HD : (pair + 1) * 2 * HD],
-                    preferred_element_type=jnp.float32,
-                )
-                parts.append(product[:group, :HD])
-                parts.append(product[group:, HD:])
+        copies(step)[1].wait()
+        for row, weight, own_weight in zip(numbers, weights, own):
+            product = jnp.dot(
+                weight.astype(jnp.bfloat16), values_ref[row], preferred_element_type=jnp.float32
+            )
+            chosen = jnp.concatenate([product[:group, :HD], product[group:, HD:]], axis=0)
             total = jnp.sum(weight, axis=1, keepdims=True) + own_weight
-            summed = jnp.concatenate(parts, axis=0) + own_weight * expand(row * 2 * KVH + KVH)
-            sums[pl.ds(pl.multiple_of(row * H, H), H), :] = summed
+            summed = chosen + own_weight * expand(row * 4 + 2)
+            sums[pl.ds(pl.multiple_of(row * heads, heads), heads), :] = summed
             totals = jnp.where(row_lane == row, total, totals)
         return totals
 
-    count = ROWS_AT_ONCE
     totals = lax.fori_loop(
-        0,
-        rows // count,
-        lambda step, totals: some_rows(step, totals, count),
-        jnp.zeros((H, HD), jnp.float32),
-    )
-    for head in range(H):
+        0, rows // ROW_CHUNK, some_rows, jnp.zeros((heads, HD), jnp.float32)
+    )
+    for head in range(heads):
         start = head // 8 * 8
         values = jnp.concatenate(
-            [sums[pl.ds(head, rows, stride=H), :], totals[start : start + 8]], axis=0
+            [sums[pl.ds(head, rows, stride=heads), :], totals[start : start + 8]], axis=0
         )
-        out_ref[(head % 2) ^ core, head // 2] = values.astype(jnp.bfloat16)
-
-
-def attended_pieces(device, core, lengths, projected, cosine, sine, key_cache, value_cache):
+        out_ref[head] = values.astype(jnp.bfloat16)
+
+
+def attended_pair(device, pair, lengths, projected, cosine, sine, key_cache, value_cache):
     rows, slots = key_cache.shape[0], key_cache.shape[1]
     smem = pl.BlockSpec(memory_space=pltpu.SMEM)
     vmem = pl.BlockSpec(memory_space=pltpu.VMEM)
+    projected = projected.reshape(-1, HD)[: (H // 2 + 5) * rows].reshape(H // 2 + 5, rows, HD)
     return pl.pallas_call(
         attend_kernel,
-        out_shape=jax.ShapeDtypeStruct((2, H // 2, rows + 8, HD), jnp.bfloat16),
+        out_shape=jax.ShapeDtypeStruct((H // 2, rows + 8, HD), jnp.bfloat16),
         in_specs=[smem] * 2 + [vmem] * 4 + [pl.BlockSpec(memory_space=pltpu.HBM)] * 2,
         out_specs=vmem,
         scratch_shapes=[
-            pltpu.VMEM(key_cache.shape, key_cache.dtype),
-            pltpu.VMEM(value_cache.shape, value_cache.dtype),
+            pltpu.VMEM((rows, slots, 2 * HD), key_cache.dtype),
+            pltpu.VMEM((rows, slots, 2 * HD), value_cache.dtype),
             pltpu.SemaphoreType.DMA((rows // ROW_CHUNK,)),
             pltpu.SemaphoreType.DMA((rows // ROW_CHUNK,)),
-            pltpu.VMEM((rows * H, HD), jnp.float32),
-            pltpu.VMEM((rows * 2 * KVH, HD), jnp.float32),
-            pltpu.VMEM((rows * H, HD), jnp.float32),
+            pltpu.VMEM((rows * H // 2, HD), jnp.float32),
+            pltpu.VMEM((rows * 4, HD), jnp.float32),
+            pltpu.VMEM((rows * H // 2, HD), jnp.float32),
         ],
-        compiler_params=pltpu.CompilerParams(vmem_limit_bytes=20 * 2**20),
+        compiler_params=pltpu.CompilerParams(vmem_limit_bytes=12 * 2**20),
         cost_estimate=pl.CostEstimate(
-            flops=4 * rows * H * slots * HD,
-            bytes_accessed=2 * (key_cache.size + value_cache.size),
-            transcendentals=rows * H * slots,
+            flops=2 * rows * H * slots * HD,
+            bytes_accessed=key_cache.size + value_cache.size,
+            transcendentals=rows * H * slots // 2,
         ),
-    )(device, core, lengths, projected, cosine, sine, in_hbm(key_cache), in_hbm(value_cache))
+    )(device, pair, lengths, projected, cosine, sine, in_hbm(key_cache), in_hbm(value_cache))
 
 
 def down_kernel(core_ref, rotated_ref, source_ref, out_ref, weights_ref, arrived):
@@ -409,37 +414,48 @@
     device = device_index.astype(jnp.int32).reshape(1)
     core = device % 2
     hidden_wide = hidden.astype(jnp.float32)
-    blocks = H + 2 * KVH
-    rows_used = (blocks + 1) * row_count
-    rows_sent = -(-rows_used // (8 * devices)) * 8
+    rows_used = (H // 2 + KVH + 1) * row_count
+    rows_sent = -(-rows_used // (4 * devices)) * 8
     halves = projected_pieces(core, hidden, w_qkv, devices, rows_sent)
     halves, lengths = lax.optimization_barrier((halves, lengths))
     arrived = across(halves[1], 1)
     positions = lax.optimization_barrier(lengths.astype(jnp.float32))
     cosine, sine = rotary_factors(positions)
     lengths = jnp.broadcast_to(positions[:, None], (row_count, HD))
-    arrived, cosine, sine, lengths = lax.optimization_barrier((arrived, cosine, sine, lengths))
+    arrived, cosine, sine, lengths, other = lax.optimization_barrier(
+        (arrived, cosine, sine, lengths, 1 - core)
+    )
     piece = scattered_joined(halves[0], arrived).astype(jnp.bfloat16)
-    projected = gathered(piece)
-    projected = projected.reshape(-1, HD)[:rows_used].reshape(blocks + 1, row_count, HD)
-    direct = devices == H
-    halves = attended_pieces(
-        device, core if direct else jnp.zeros_like(core), lengths, projected, cosine, sine, key_cache, value_cache
-    )
-    if direct:
-        parts = scattered_halves(halves[0], halves[1])
+    mine = gathered_same_core(piece)
+    theirs = across(mine, 1)
+    second = device_index % 2 == 1
+    both = lax.optimization_barrier((jnp.where(second, mine, theirs), jnp.where(second, theirs, mine)))
+    theirs = jnp.where(second, both[1], both[0])
+    shared = (lengths, cosine, sine, key_cache, value_cache)
+    attend = lambda pair, projected: attended_pair(
+        device, pair, shared[0], projected, shared[1], shared[2], shared[3], shared[4]
+    )
+    sent = attend(other, mine)
+    arrived = across(sent, 1)
+    kept = attend(core, theirs)
+    if devices == H:
+        parts = scattered_joined(kept, arrived)
         parts, device_index = lax.optimization_barrier((parts, device_index))
         piece = normalized(device, parts, row_count)
+        heads = gathered_at_once(piece).reshape(devices // 2, 2, row_count, HD)
+        attention = heads.transpose(2, 1, 0, 3).reshape(row_count, query_width)
     else:
         held = H * row_count // devices
-        heads = halves.transpose(1, 0, 2, 3).reshape(H, row_count + 8, HD)
+        first = core[0] == 0
+        heads = jnp.concatenate([jnp.where(first, kept, sent), jnp.where(first, sent, kept)])
         numerators = heads[:, :row_count].reshape(devices, held, HD)
         totals = heads[:, row_count:].reshape(H // 8, 8, 8, HD)
         totals = jnp.einsum("ahhl->ahl", totals).reshape(H, HD)[:, :row_count]
         totals = jnp.pad(totals.reshape(devices, 1, held), ((0, 0), (0, 0), (0, HD - held)))
         parts = scattered_sum(jnp.concatenate([numerators, totals], axis=1))
         piece = (parts[:held] / parts[held, :held][:, None]).astype(jnp.bfloat16)
-    attention = gathered_at_once(piece).reshape(H, row_count, HD).transpose(1, 0, 2).reshape(row_count, query_width)
+        heads = gathered_at_once(piece).reshape(H, row_count, HD)
+        attention = heads.transpose(1, 0, 2).reshape(row_count, query_width)
     residual = (hidden_wide + jnp.dot(attention, w_out, preferred_element_type=jnp.float32)).astype(
         jnp.bfloat16
     )

time: 113 us -> 112 us (level)
  waiting for transfers between devices: 10.3 us -> 7.75 us
    ppermute x7, waiting for transfers between devices: 10.3 us -> 7.75 us  [across(): return lax.ppermute(value, 'tensor', pairs)]
    pallas_call x1 -> x2, Pallas kernels: 6.06 us -> 7.06 us  [attended_pair(): pl.pallas_call(attend_kernel, out_shape=jax.ShapeDtypeStruct((H // 2, row...]
  transfers between devices with their start and end apart: 7 -> 7, of which waited for: 7 -> 5; matrix products, arithmetic and copies ran while one was open for 1% -> 1% of each run, Pallas kernels for 0% -> 6%
where the time goes in v5:
time: 112 us
  blocking collectives  81.1 us (72%)
  Pallas kernels  12.9 us (12%)
  waiting for transfers between devices  7.75 us (7%)
  matrix products  4.76 us (4%)
  starting transfers between devices  2.44 us (2%)
  other arithmetic  2.2 us (2%)
    all_to_all x3, blocking collectives, scattered_joined(): lax.all_to_all(joined.astype(jnp.bfloat16), 'tensor', 0, 0, tiled=True, a...  38.6 us
    all_to_all x2, blocking collectives, gathered_same_core(): lax.all_to_all(copies, 'tensor', 0, 0, tiled=True, axis_index_groups=same...  23 us
    all_to_all x1, blocking collectives, gathered_at_once(): return lax.all_to_all(copies, 'tensor', 0, 0, tiled=True)  10.8 us
    all_to_all x1, blocking collectives, signed_sum(): lax.all_to_all(copies, 'tensor', 0, 0, tiled=True, axis_index_groups=groups)  8.78 us
    ppermute x7, waiting for transfers between devices, across(): return lax.ppermute(value, 'tensor', pairs)  7.75 us
    pallas_call x2, Pallas kernels, attended_pair(): pl.pallas_call(attend_kernel, out_shape=jax.ShapeDtypeStruct((H // 2, row...  7.06 us
    pallas_call x1, Pallas kernels, down_pieces(): pl.pallas_call(down_kernel, out_shape=jax.ShapeDtypeStruct((2, devices //...  3.48 us
    ppermute x7, starting transfers between devices, across(): return lax.ppermute(value, 'tensor', pairs)  2.44 us
  transfers between devices with their start and end apart: 7, of which 5 were waited for; matrix products, arithmetic and copies ran while one was open for 1% of the time, Pallas kernels for 6%

profile of v5, /device:TPU:0, one launch (start us, length us, event | category | flops | bytes accessed | tf_op | source)
XLA Modules:
  0.0 111.8 jit_solution(7465691212490815073)
XLA Ops:
  0.0 0.0 copy-start
  0.0 2.2 %shard_map.100 = bf16[2,16,32,128]{3,2,1,0:T(8,128)(2,1)S(1)} custom-call(s32[1]{0:T(128)S(6)} %select_n.75.core_ref.pair_ref, bf16[24,256]{1,0:T(8,128)(2,1)} %hidden_source.1, bf16[256,5120]{1,0:T(8,128)(2,1)} %source_ref.2), custom_call_target="tpu_custom_call" | custom-call | flops 62914560 | bytes 2621440 | tf_op jit(solution)/shard_map/pallas_call | solution.py:186
  2.3 0.5 collective-permute-start
  2.8 0.7 convert_element_type.102
  3.5 0.1 fusion.7
  3.6 0.1 pad_maximum_fusion
  3.7 0.1 collective-permute-done
  3.8 0.1 broadcast_in_dim.10.lengths_ref
  3.9 15.8 %all_to_all.35 = bf16[16,32,128]{2,1,0:T(8,128)(2,1)S(1)} all-to-all(bf16[16,32,128]{2,1,0:T(8,128)(2,1)S(1)} %fusion.2), channel_id=1, replica_groups={{0,2,4,6,8,10,12,14,16,18,20,22,24,26,28,30},{1,3,5,7,9,11,13,15,17,19,..., dimensions={0} | all-to-all | bytes 262144 | tf_op jit(solution)/shard_map/all_to_all | solution.py:47
  19.8 10.7 %all_to_all.36 = bf16[16,32,128]{2,1,0:T(8,128)(2,1)S(1)} all-to-all(bf16[16,32,128]{2,1,0:T(8,128)(2,1)S(1)} %broadcast_in_dim.11), channel_id=1, replica_groups={{0,2,4,6,8,10,12,14,16,18,20,22,24,26,28,30},{1,3,5,7,9,11,13,15,17,19,..., dimensions={0} | all-to-all | bytes 262144 | tf_op jit(solution)/shard_map/all_to_all | solution.py:60
  30.5 0.0 collective-permute-start.1
  30.5 3.5 %shard_map.102 = bf16[16,32,128]{2,1,0:T(8,128)(2,1)S(1)} custom-call(s32[1]{0:T(128)} %bitcast.device_ref, s32[1]{0:T(128)S(6)} %sub.24.pair_ref, f32[24,128]{1,0:T(8,128)S(1)} %broadcast_in_dim.10.lengths_ref, bf16[21,24,128]{2,1,0:T(8,128)(2,1)S(1)} %bitcast.42, f32[24,128]{1,0:T(8,128)S(1)} %get-tuple-element.23.cosine_ref, ...), custom_call_target="tpu_custom_call" | custom-call | flops 50331648 | bytes 6291456 | tf_op jit(solution)/shard_map/pallas_call | solution.py:313
  34.0 0.6 collective-permute-start.2
  34.5 0.0 collective-permute-done.1
  34.6 0.0 slice-start
  34.6 0.0 copy-start.2
  34.6 0.0 slice-start.1
  34.6 3.6 %shard_map.101 = bf16[16,32,128]{2,1,0:T(8,128)(2,1)S(1)} custom-call(s32[1]{0:T(128)} %bitcast.device_ref, s32[1]{0:T(128)S(6)} %select_n.75.core_ref.pair_ref, f32[24,128]{1,0:T(8,128)S(1)} %broadcast_in_dim.10.lengths_ref, bf16[21,24,128]{2,1,0:T(8,128)(2,1)S(1)} %bitcast.41, f32[24,128]{1,0:T(8,128)S(1)} %get-tuple-element.23.cosine_ref, ...), custom_call_target="tpu_custom_call" | custom-call | flops 50331648 | bytes 6291456 | tf_op jit(solution)/shard_map/pallas_call | solution.py:313
  38.3 0.0 collective-permute-done.2
  38.3 10.6 %all_to_all.37 = bf16[16,32,128]{2,1,0:T(8,128)(2,1)S(1)} all-to-all(bf16[16,32,128]{2,1,0:T(8,128)(2,1)S(1)} %add_convert_fusion), channel_id=1, replica_groups={{0,2,4,6,8,10,12,14,16,18,20,22,24,26,28,30},{1,3,5,7,9,11,13,15,17,19,..., dimensions={0} | all-to-all | bytes 262144 | tf_op jit(solution)/shard_map/all_to_all | solution.py:47
  49.0 0.1 shard_map.103
  49.1 10.8 %all_to_all.38 = bf16[32,24,128]{2,1,0:T(8,128)(2,1)S(1)} all-to-all(bf16[32,24,128]{2,1,0:T(8,128)(2,1)S(1)} %broadcast_in_dim.12), channel_id=1, replica_groups=mesh['groups'=1,'tensor'=32] {'tensor'}, dimensions={0} | all-to-all | bytes 393216 | tf_op jit(solution)/shard_map/all_to_all | solution.py:55
  59.9 0.1 copy.16
  59.9 0.0 copy-done
  60.0 0.0 copy-done.2
  60.0 0.0 slice-start.2
  60.0 0.4 fusion
  60.4 12.3 %all_to_all.39 = bf16[16,24,256]{2,1,0:T(8,128)(2,1)S(1)} all-to-all(bf16[16,24,256]{2,1,0:T(8,128)(2,1)S(1)} %broadcast_in_dim.13), channel_id=1, replica_groups={{0,2,4,6,8,10,12,14,16,18,20,22,24,26,28,30},{1,3,5,7,9,11,13,15,17,19,..., dimensions={0} | all-to-all | bytes 393216 | tf_op jit(solution)/shard_map/all_to_all | solution.py:60
  72.7 0.0 collective-permute-start.3
  72.7 1.4 %collective-permute-done.3 = bf16[16,24,256]{2,1,0:T(8,128)(2,1)S(1)} collective-permute-done((bf16[16,24,256]{2,1,0:T(8,128)(2,1)S(1)}, bf16[16,24,256]{2,1,0:T(8,128)(2,1)S(1)}, u32[]{:S(2)}, u32[]{:S(2)}) %collective-permute-start.3) | collective-permute-done | bytes 196640 | tf_op jit(solution)/shard_map/ppermute | solution.py:25
  74.1 0.2 multiply_reduce_fusion
  74.4 0.1 maximum_convert_fusion
  74.4 0.1 copy.19
  74.5 0.0 slice-done
  74.5 0.0 slice-done.1
  74.5 0.0 slice-start.3
  74.6 0.0 copy-start.1
  74.6 2.0 %fusion.12 = f32[24,448]{1,0:T(8,128)S(1)} fusion(bf16[8192,448]{0,1:T(8,128)(2,1)S(1)} %bitcast.44, f32[24,8192]{1,0:T(8,128)S(1)} %bitcast.47, f32[24]{0:T(128)S(1)} %add_rsqrt_fusion), kind=kOutput, calls=%fused_computation.45 | convolution fusion | flops 176553984 | bytes 8169568 | tf_op jit(solution)/shard_map/dot_general | solution.py:468
  76.6 0.0 slice-done.2
  76.6 0.0 slice-done.3
  76.6 2.0 %convolution_multiply_fusion = f32[24,448]{1,0:T(8,128)S(1)} fusion(bf16[8192,448]{0,1:T(8,128)(2,1)S(1)} %bitcast.46, f32[24,448]{1,0:T(8,128)S(1)} %fusion.12, f32[24,8192]{1,0:T(8,128)S(1)} %bitcast.48, f32[24]{0:T(128)S(1)} %add_rsqrt_fusion), kind=kOutput, calls=%fused_computation | convolution fusion | flops 176607744 | bytes 8212576 | tf_op jit(solution)/shard_map/dot_general | solution.py:469
  78.6 0.0 copy-done.1
  78.6 0.3 fusion.13
  79.0 0.2 collective-permute-start.4
  79.1 1.1 collective-permute-done.4
  80.3 1.1 collective-permute-start.5
  81.4 3.7 %collective-permute-done.5 = bf16[24,448]{1,0:T(8,128)(2,1)S(1)} collective-permute-done((bf16[24,448]{1,0:T(8,128)(2,1)S(1)}, bf16[24,448]{1,0:T(8,128)(2,1)S(1)}, u32[]{:S(2)}, u32[]{:S(2)}) %collective-permute-start.5) | collective-permute-done | bytes 21536 | tf_op jit(solution)/shard_map/ppermute | solution.py:25
  85.1 8.8 %all_to_all.40 = bf16[8,24,448]{2,1,0:T(8,128)(2,1)S(1)} all-to-all(bf16[8,24,448]{2,1,0:T(8,128)(2,1)S(1)} %broadcast_in_dim.14), channel_id=1, replica_groups={{0,2,4,6,8,10,12,14},{1,3,5,7,9,11,13,15},{16,18,20,22,24,26,28,30},{17..., dimensions={0} | all-to-all | bytes 344064 | tf_op jit(solution)/shard_map/all_to_all | solution.py:89
  93.9 0.1 multiply_reduce_fusion.1
  94.0 3.5 %shard_map.104 = bf16[2,16,24,256]{3,2,1,0:T(8,128)(2,1)S(1)} custom-call(s32[1]{0:T(128)S(6)} %select_n.75.core_ref.pair_ref, bf16[24,448]{1,0:T(8,128)(2,1)S(1)} %multiply_convert_fusion.1.rotated_ref, bf16[448,8192]{1,0:T(8,128)(2,1)} %source_ref.3), custom_call_target="tpu_custom_call" | custom-call | flops 176160768 | bytes 7340032 | tf_op jit(solution)/shard_map/pallas_call | solution.py:357
  97.5 0.1 collective-permute-start.6
  97.6 1.4 %collective-permute-done.6 = bf16[16,24,256]{2,1,0:T(8,128)(2,1)S(1)} collective-permute-done((bf16[16,24,256]{2,1,0:T(8,128)(2,1)S(1)}, bf16[16,24,256]{2,1,0:T(8,128)(2,1)S(1)}, u32[]{:S(2)}, u32[]{:S(2)}) %collective-permute-start.6) | collective-permute-done | bytes 196640 | tf_op jit(solution)/shard_map/ppermute | solution.py:25
  99.0 0.1 fusion.1
  99.1 12.1 %all_to_all.41 = bf16[16,24,256]{2,1,0:T(8,128)(2,1)S(1)} all-to-all(bf16[16,24,256]{2,1,0:T(8,128)(2,1)S(1)} %fusion.1), channel_id=1, replica_groups={{0,2,4,6,8,10,12,14,16,18,20,22,24,26,28,30},{1,3,5,7,9,11,13,15,17,19,..., dimensions={0} | all-to-all | bytes 393216 | tf_op jit(solution)/shard_map/all_to_all | solution.py:47
  111.2 0.6 add_convert_fusion.1
  (24 shorter events, 0.4 us)
Async XLA Ops:
  0.0 59.9 %copy-start = (bf16[4096,256]{1,0:T(8,128)(2,1)S(1)}, bf16[4096,256]{1,0:T(8,128)(2,1)}, u32[]{:S(2)}) copy-start(bf16[4096,256]{1,0:T(8,128)(2,1)} %param.15) | copy-start | bytes 6291460
  2.3 1.5 %collective-permute-start = (bf16[16,32,128]{2,1,0:T(8,128)(2,1)S(1)}, bf16[16,32,128]{2,1,0:T(8,128)(2,1)S(1)}, u32[]{:S(2)}, u32[]{:S(2)}) collective-permute-start(bf16[16,32,128]{2,1,0:T(8,128)(2,1)S(1)} %slice_bitcast_fusion.2), channel_id=1, source_target_pairs={{0,1},{1,0},{2,3},{3,2},{4,5},{5,4},{6,7},{7,6},{8,9},{9,8},{10,11... | collective-permute-start | bytes 393224 | tf_op jit(solution)/shard_map/ppermute | solution.py:25
  30.5 4.1 %collective-permute-start.1 = (bf16[16,32,128]{2,1,0:T(8,128)(2,1)S(1)}, bf16[16,32,128]{2,1,0:T(8,128)(2,1)S(1)}, u32[]{:S(2)}, u32[]{:S(2)}) collective-permute-start(bf16[16,32,128]{2,1,0:T(8,128)(2,1)S(1)} %all_to_all.36), channel_id=1, source_target_pairs={{0,1},{1,0},{2,3},{3,2},{4,5},{5,4},{6,7},{7,6},{8,9},{9,8},{10,11... | collective-permute-start | bytes 393224 | tf_op jit(solution)/shard_map/ppermute | solution.py:25
  34.0 4.3 %collective-permute-start.2 = (bf16[16,32,128]{2,1,0:T(8,128)(2,1)S(1)}, bf16[16,32,128]{2,1,0:T(8,128)(2,1)S(1)}, u32[]{:S(2)}, u32[]{:S(2)}) collective-permute-start(bf16[16,32,128]{2,1,0:T(8,128)(2,1)S(1)} %shard_map.102), channel_id=1, source_target_pairs={{0,1},{1,0},{2,3},{3,2},{4,5},{5,4},{6,7},{7,6},{8,9},{9,8},{10,11... | collective-permute-start | bytes 393224 | tf_op jit(solution)/shard_map/ppermute | solution.py:25
  34.6 39.9 %slice-start = ((s8[7340032]{0:T(1024)(128)(4,1)}), s8[4194304]{0:T(1024)(128)(4,1)S(1)}, s32[]{:S(2)}) async-start(s8[7340032]{0:T(1024)(128)(4,1)} %bitcast.43), calls=%async_computation.7 | async-start | bytes 8388608
  34.6 25.3 %copy-start.2 = (bf16[24,256]{1,0:T(8,128)(2,1)S(1)}, bf16[24,256]{1,0:T(8,128)(2,1)}, u32[]{:S(2)}) copy-start(bf16[24,256]{1,0:T(8,128)(2,1)} %hidden_source.1) | copy-start | bytes 36868
  34.6 39.9 %slice-start.1 = ((s8[7340032]{0:T(1024)(128)(4,1)}), s8[3145728]{0:T(1024)(128)(4,1)S(1)}, s32[]{:S(2)}) async-start(s8[7340032]{0:T(1024)(128)(4,1)} %bitcast.43), calls=%async_computation.8 | async-start | bytes 6291456
  60.0 16.6 %slice-start.2 = ((s8[7340032]{0:T(1024)(128)(4,1)}), s8[4194304]{0:T(1024)(128)(4,1)S(1)}, s32[]{:S(2)}) async-start(s8[7340032]{0:T(1024)(128)(4,1)} %bitcast.45), calls=%async_computation.9 | async-start | bytes 8388608
  72.7 1.4 %collective-permute-start.3 = (bf16[16,24,256]{2,1,0:T(8,128)(2,1)S(1)}, bf16[16,24,256]{2,1,0:T(8,128)(2,1)S(1)}, u32[]{:S(2)}, u32[]{:S(2)}) collective-permute-start(bf16[16,24,256]{2,1,0:T(8,128)(2,1)S(1)} %all_to_all.39), channel_id=1, source_target_pairs={{0,1},{1,0},{2,3},{3,2},{4,5},{5,4},{6,7},{7,6},{8,9},{9,8},{10,11... | collective-permute-start | bytes 589832 | tf_op jit(solution)/shard_map/ppermute | solution.py:25
  74.5 2.1 %slice-start.3 = ((s8[7340032]{0:T(1024)(128)(4,1)}), s8[3145728]{0:T(1024)(128)(4,1)S(1)}, s32[]{:S(2)}) async-start(s8[7340032]{0:T(1024)(128)(4,1)} %bitcast.45), calls=%async_computation.10 | async-start | bytes 6291456
  74.6 4.1 %copy-start.1 = (f32[448,448]{1,0:T(8,128)S(1)}, f32[448,448]{1,0:T(8,128)}, u32[]{:S(2)}) copy-start(f32[448,448]{1,0:T(8,128)} %constant.113.clone) | copy-start | bytes 2408452
  79.0 1.3 %collective-permute-start.4 = (f32[24,448]{1,0:T(8,128)S(1)}, f32[24,448]{1,0:T(8,128)S(1)}, u32[]{:S(2)}, u32[]{:S(2)}) collective-permute-start(f32[24,448]{1,0:T(8,128)S(1)} %fusion.13), channel_id=1, source_target_pairs={{0,1},{1,0},{2,3},{3,2},{4,5},{5,4},{6,7},{7,6},{8,9},{9,8},{10,11... | collective-permute-start | bytes 129032 | tf_op jit(solution)/shard_map/ppermute | solution.py:25
  80.3 4.8 %collective-permute-start.5 = (bf16[24,448]{1,0:T(8,128)(2,1)S(1)}, bf16[24,448]{1,0:T(8,128)(2,1)S(1)}, u32[]{:S(2)}, u32[]{:S(2)}) collective-permute-start(bf16[24,448]{1,0:T(8,128)(2,1)S(1)} %select_convert_fusion), channel_id=1, source_target_pairs={{0,16},{1,17},{2,18},{3,19},{4,20},{5,21},{6,22},{7,23},{8,24},{9,... | collective-permute-start | bytes 64520 | tf_op jit(solution)/shard_map/ppermute | solution.py:25
  97.5 1.5 %collective-permute-start.6 = (bf16[16,24,256]{2,1,0:T(8,128)(2,1)S(1)}, bf16[16,24,256]{2,1,0:T(8,128)(2,1)S(1)}, u32[]{:S(2)}, u32[]{:S(2)}) collective-permute-start(bf16[16,24,256]{2,1,0:T(8,128)(2,1)S(1)} %slice_bitcast_fusion), channel_id=1, source_target_pairs={{0,1},{1,0},{2,3},{3,2},{4,5},{5,4},{6,7},{7,6},{8,9},{9,8},{10,11... | collective-permute-start | bytes 589832 | tf_op jit(solution)/shard_map/ppermute | solution.py:25

commit v6 on v5

--- a/solution.py
+++ b/solution.py
@@ -16,7 +16,6 @@
 EPSILON = 1e-05
 ROPE_BASE = 500000.0
 QKV_CHUNK = 2560
-DOWN_CHUNK = 1024
 ROW_CHUNK = 8
 
 
@@ -30,8 +29,7 @@
     return [list(range(core, devices, 2)) for core in range(2)]
 
 
-def scattered_sum(pieces):
-    second = lax.axis_index("tensor") % 2 == 1
+def scattered_sum(pieces, second):
     halves = pieces.reshape(-1, 2, *pieces.shape[1:])
     kept = jnp.where(second, halves[:, 1], halves[:, 0])
     sent = jnp.where(second, halves[:, 0], halves[:, 1]).astype(jnp.bfloat16)
@@ -60,22 +58,26 @@
     return lax.all_to_all(copies, "tensor", 0, 0, tiled=True, axis_index_groups=same_core())
 
 
-def gathered(piece):
-    second = lax.axis_index("tensor") % 2 == 1
+def gathered(piece, second):
     mine = gathered_same_core(piece)
     theirs = across(mine, 1)
     both = jnp.stack([jnp.where(second, theirs, mine), jnp.where(second, mine, theirs)], axis=1)
     return both.reshape(-1, *piece.shape)
 
 
-def signed_pair(value, apart):
-    upper = lax.axis_index("tensor") // apart % 2 == 1
-    partner = across(value, apart).astype(jnp.float32)
-    own = value.astype(jnp.float32)
+def signed_join(value, partner, upper):
+    own, partner = value.astype(jnp.float32), partner.astype(jnp.float32)
     return jnp.where(upper, partner - own, own + partner)
 
 
-def signed_sum(value):
+def middle_signs(index, middle):
+    common = jnp.arange(middle) & (index // 2 % middle)
+    for shift in (4, 2, 1):
+        common = common ^ (common >> shift)
+    return 1.0 - 2.0 * (common & 1).astype(jnp.float32)
+
+
+def signed_sum(value, second, upper, signs):
     devices = lax.axis_size("tensor")
     middle = devices // 4
     groups = [
@@ -83,15 +85,11 @@
         for top in range(2)
         for core in range(2)
     ]
-    value = signed_pair(value, 1)
-    value = signed_pair(value.astype(jnp.bfloat16), devices // 2).astype(jnp.bfloat16)
+    value = signed_join(value, across(value, 1), second)
+    value = value.astype(jnp.bfloat16)
+    value = signed_join(value, across(value, devices // 2), upper).astype(jnp.bfloat16)
     copies = jnp.broadcast_to(value[None], (middle, *value.shape))
     received = lax.all_to_all(copies, "tensor", 0, 0, tiled=True, axis_index_groups=groups)
-    received, index = lax.optimization_barrier((received, lax.axis_index("tensor")))
-    common = jnp.arange(middle) & (index // 2 % middle)
-    for shift in (4, 2, 1):
-        common = common ^ (common >> shift)
-    signs = 1.0 - 2.0 * (common & 1).astype(jnp.float32)
     return jnp.sum(received.astype(jnp.float32) * signs[:, None, None], axis=0)
 
 
@@ -333,16 +331,13 @@
     )(device, pair, lengths, projected, cosine, sine, in_hbm(key_cache), in_hbm(value_cache))
 
 
-def down_kernel(core_ref, rotated_ref, source_ref, out_ref, weights_ref, arrived):
-    copies = column_copies(source_ref, weights_ref, arrived, DOWN_CHUNK)
+def down_kernel(core_ref, rotated_ref, weights_ref, out_ref):
     core = core_ref[0]
     rotated = rotated_ref[...]
     features = weights_ref.shape[1]
     width = out_ref.shape[3]
     block = max(width, min(256, features))
     for start in range(0, features, block):
-        if start % DOWN_CHUNK == 0:
-            copies[start // DOWN_CHUNK].wait()
         part = jnp.dot(
             rotated, weights_ref[:, start : start + block], preferred_element_type=jnp.float32
         ).astype(jnp.bfloat16)
@@ -357,23 +352,15 @@
     return pl.pallas_call(
         down_kernel,
         out_shape=jax.ShapeDtypeStruct((2, devices // 2, rows, features // devices), jnp.bfloat16),
-        in_specs=[
-            pl.BlockSpec(memory_space=pltpu.SMEM),
-            vmem,
-            pl.BlockSpec(memory_space=pltpu.HBM),
-        ],
+        in_specs=[pl.BlockSpec(memory_space=pltpu.SMEM), vmem, vmem],
         out_specs=vmem,
-        scratch_shapes=[
-            pltpu.VMEM(w_down.shape, w_down.dtype),
-            pltpu.SemaphoreType.DMA((w_down.shape[1] // DOWN_CHUNK,)),
-        ],
         compiler_params=pltpu.CompilerParams(vmem_limit_bytes=12 * 2**20),
         cost_estimate=pl.CostEstimate(
             flops=2 * rows * rotated.shape[1] * features,
             bytes_accessed=w_down.size * 2,
             transcendentals=0,
         ),
-    )(core, rotated, in_hbm(w_down))
+    )(core, rotated, w_down)
 
 
 def paley_table():
@@ -422,15 +409,15 @@
     positions = lax.optimization_barrier(lengths.astype(jnp.float32))
     cosine, sine = rotary_factors(positions)
     lengths = jnp.broadcast_to(positions[:, None], (row_count, HD))
-    arrived, cosine, sine, lengths, other = lax.optimization_barrier(
-        (arrived, cosine, sine, lengths, 1 - core)
+    second = device_index % 2 == 1
+    upper = device_index // (devices // 2) == 1
+    signs = middle_signs(device_index, devices // 4)
+    arrived, cosine, sine, lengths, other, second, upper, signs = lax.optimization_barrier(
+        (arrived, cosine, sine, lengths, 1 - core, second, upper, signs)
     )
     piece = scattered_joined(halves[0], arrived).astype(jnp.bfloat16)
     mine = gathered_same_core(piece)
     theirs = across(mine, 1)
-    second = device_index % 2 == 1
-    both = lax.optimization_barrier((jnp.where(second, mine, theirs), jnp.where(second, theirs, mine)))
-    theirs = jnp.where(second, both[1], both[0])
     shared = (lengths, cosine, sine, key_cache, value_cache)
     attend = lambda pair, projected: attended_pair(
         device, pair, shared[0], projected, shared[1], shared[2], shared[3], shared[4]
@@ -440,7 +427,6 @@
     kept = attend(core, theirs)
     if devices == H:
         parts = scattered_joined(kept, arrived)
-        parts, device_index = lax.optimization_barrier((parts, device_index))
         piece = normalized(device, parts, row_count)
         heads = gathered_at_once(piece).reshape(devices // 2, 2, row_count, HD)
         attention = heads.transpose(2, 1, 0, 3).reshape(row_count, query_width)
@@ -452,14 +438,14 @@
         totals = heads[:, row_count:].reshape(H // 8, 8, 8, HD)
         totals = jnp.einsum("ahhl->ahl", totals).reshape(H, HD)[:, :row_count]
         totals = jnp.pad(totals.reshape(devices, 1, held), ((0, 0), (0, 0), (0, HD - held)))
-        parts = scattered_sum(jnp.concatenate([numerators, totals], axis=1))
+        parts = scattered_sum(jnp.concatenate([numerators, totals], axis=1), second)
         piece = (parts[:held] / parts[held, :held][:, None]).astype(jnp.bfloat16)
         heads = gathered_at_once(piece).reshape(H, row_count, HD)
         attention = heads.transpose(1, 0, 2).reshape(row_count, query_width)
     residual = (hidden_wide + jnp.dot(attention, w_out, preferred_element_type=jnp.float32)).astype(
         jnp.bfloat16
     )
-    residual_full = gathered(residual).transpose(1, 0, 2).reshape(row_count, D)
+    residual_full = gathered(residual, second).transpose(1, 0, 2).reshape(row_count, D)
     residual_wide = residual_full.astype(jnp.float32)
     normed = (
         residual_wide
@@ -473,7 +459,8 @@
         np.kron(sylvester_table(local_width // 28), paley_table()), dtype=jnp.float32
     )
     mixed = jnp.dot(activation, local_table, precision=lax.Precision.HIGH)
-    rotated = (signed_sum(mixed) * FF ** (-0.5)).astype(jnp.bfloat16)
+    rotated = signed_sum(mixed, second, upper, signs)
+    rotated = (rotated * FF ** (-0.5)).astype(jnp.bfloat16)
     halves = down_pieces(core, rotated, w_down, devices)
     down_share = scattered_halves(halves[0], halves[1])
     return (residual.astype(jnp.float32) + down_share).astype(jnp.bfloat16)

time: 112 us -> 110 us (0.982)
  Pallas kernels: 12.9 us -> 10.8 us
    pallas_call x1, Pallas kernels: 3.48 us -> 1.42 us  [down_pieces(): pl.pallas_call(down_kernel, out_shape=jax.ShapeDtypeStruct((2, devices //...]
where the time goes in v6:
time: 110 us
  blocking collectives  81 us (74%)
  Pallas kernels  10.8 us (10%)
  waiting for transfers between devices  7.71 us (7%)
  matrix products  4.76 us (4%)
  starting transfers between devices  2.49 us (2%)
  other arithmetic  2.16 us (2%)
    all_to_all x3, blocking collectives, scattered_joined(): lax.all_to_all(joined.astype(jnp.bfloat16), 'tensor', 0, 0, tiled=True, a...  38.7 us
    all_to_all x2, blocking collectives, gathered_same_core(): lax.all_to_all(copies, 'tensor', 0, 0, tiled=True, axis_index_groups=same...  22.7 us
    all_to_all x1, blocking collectives, gathered_at_once(): return lax.all_to_all(copies, 'tensor', 0, 0, tiled=True)  10.8 us
    all_to_all x1, blocking collectives, signed_sum(): lax.all_to_all(copies, 'tensor', 0, 0, tiled=True, axis_index_groups=groups)  8.78 us
    ppermute x7, waiting for transfers between devices, across(): return lax.ppermute(value, 'tensor', pairs)  7.71 us
    pallas_call x2, Pallas kernels, attended_pair(): pl.pallas_call(attend_kernel, out_shape=jax.ShapeDtypeStruct((H // 2, row...  7.06 us
    ppermute x7, starting transfers between devices, across(): return lax.ppermute(value, 'tensor', pairs)  2.49 us
    pallas_call x1, Pallas kernels, projected_pieces(): pl.pallas_call(project_kernel, out_shape=jax.ShapeDtypeStruct((2, devices...  2.24 us
  transfers between devices with their start and end apart: 7, of which 5 were waited for; matrix products, arithmetic and copies ran while one was open for 1% of the time, Pallas kernels for 6%

profile of v6, /device:TPU:0, one launch (start us, length us, event | category | flops | bytes accessed | tf_op | source)
XLA Modules:
  0.0 109.7 jit_solution(9098070325233499117)
XLA Ops:
  0.0 0.0 copy-start
  0.0 2.2 %shard_map.100 = bf16[2,16,32,128]{3,2,1,0:T(8,128)(2,1)S(1)} custom-call(s32[1]{0:T(128)S(6)} %select_n.50.core_ref.pair_ref, bf16[24,256]{1,0:T(8,128)(2,1)} %hidden_source.1, bf16[256,5120]{1,0:T(8,128)(2,1)} %source_ref.1), custom_call_target="tpu_custom_call" | custom-call | flops 62914560 | bytes 2621440 | tf_op jit(solution)/shard_map/pallas_call | solution.py:184
  2.3 0.5 collective-permute-start
  2.8 0.7 convert_element_type.98
  3.5 0.1 fusion.7
  3.6 0.1 pad_maximum_fusion
  3.7 0.1 collective-permute-done
  3.8 0.1 broadcast_in_dim.10.lengths_ref
  3.9 15.8 %all_to_all.35 = bf16[16,32,128]{2,1,0:T(8,128)(2,1)S(1)} all-to-all(bf16[16,32,128]{2,1,0:T(8,128)(2,1)S(1)} %fusion.2), channel_id=1, replica_groups={{0,2,4,6,8,10,12,14,16,18,20,22,24,26,28,30},{1,3,5,7,9,11,13,15,17,19,..., dimensions={0} | all-to-all | bytes 262144 | tf_op jit(solution)/shard_map/all_to_all | solution.py:45
  19.8 10.7 %all_to_all.36 = bf16[16,32,128]{2,1,0:T(8,128)(2,1)S(1)} all-to-all(bf16[16,32,128]{2,1,0:T(8,128)(2,1)S(1)} %broadcast_in_dim.11), channel_id=1, replica_groups={{0,2,4,6,8,10,12,14,16,18,20,22,24,26,28,30},{1,3,5,7,9,11,13,15,17,19,..., dimensions={0} | all-to-all | bytes 262144 | tf_op jit(solution)/shard_map/all_to_all | solution.py:58
  30.5 0.1 collective-permute-start.1
  30.6 3.5 %shard_map.102 = bf16[16,32,128]{2,1,0:T(8,128)(2,1)S(1)} custom-call(s32[1]{0:T(128)} %bitcast.device_ref, s32[1]{0:T(128)S(6)} %sub.19.pair_ref, f32[24,128]{1,0:T(8,128)S(1)} %broadcast_in_dim.10.lengths_ref, bf16[21,24,128]{2,1,0:T(8,128)(2,1)S(1)} %bitcast.43, f32[24,128]{1,0:T(8,128)S(1)} %get-tuple-element.19.cosine_ref, ...), custom_call_target="tpu_custom_call" | custom-call | flops 50331648 | bytes 6291456 | tf_op jit(solution)/shard_map/pallas_call | solution.py:311
  34.0 0.6 collective-permute-start.2
  34.6 0.0 collective-permute-done.1
  34.6 0.0 slice-start.2
  34.6 0.0 copy-start.2
  34.6 0.0 slice-start.3
  34.6 3.6 %shard_map.101 = bf16[16,32,128]{2,1,0:T(8,128)(2,1)S(1)} custom-call(s32[1]{0:T(128)} %bitcast.device_ref, s32[1]{0:T(128)S(6)} %select_n.50.core_ref.pair_ref, f32[24,128]{1,0:T(8,128)S(1)} %broadcast_in_dim.10.lengths_ref, bf16[21,24,128]{2,1,0:T(8,128)(2,1)S(1)} %bitcast.44, f32[24,128]{1,0:T(8,128)S(1)} %get-tuple-element.19.cosine_ref, ...), custom_call_target="tpu_custom_call" | custom-call | flops 50331648 | bytes 6291456 | tf_op jit(solution)/shard_map/pallas_call | solution.py:311
  38.3 0.0 collective-permute-done.2
  38.3 0.0 slice-start.4
  38.3 10.8 %all_to_all.37 = bf16[16,32,128]{2,1,0:T(8,128)(2,1)S(1)} all-to-all(bf16[16,32,128]{2,1,0:T(8,128)(2,1)S(1)} %add_convert_fusion), channel_id=1, replica_groups={{0,2,4,6,8,10,12,14,16,18,20,22,24,26,28,30},{1,3,5,7,9,11,13,15,17,19,..., dimensions={0} | all-to-all | bytes 262144 | tf_op jit(solution)/shard_map/all_to_all | solution.py:45
  49.1 0.1 shard_map.103
  49.3 10.8 %all_to_all.38 = bf16[32,24,128]{2,1,0:T(8,128)(2,1)S(1)} all-to-all(bf16[32,24,128]{2,1,0:T(8,128)(2,1)S(1)} %broadcast_in_dim.12), channel_id=1, replica_groups=mesh['groups'=1,'tensor'=32] {'tensor'}, dimensions={0} | all-to-all | bytes 393216 | tf_op jit(solution)/shard_map/all_to_all | solution.py:53
  60.0 0.1 copy.16
  60.1 0.0 copy-done
  60.1 0.0 copy-done.2
  60.1 0.4 fusion
  60.5 12.0 %all_to_all.39 = bf16[16,24,256]{2,1,0:T(8,128)(2,1)S(1)} all-to-all(bf16[16,24,256]{2,1,0:T(8,128)(2,1)S(1)} %broadcast_in_dim.13), channel_id=1, replica_groups={{0,2,4,6,8,10,12,14,16,18,20,22,24,26,28,30},{1,3,5,7,9,11,13,15,17,19,..., dimensions={0} | all-to-all | bytes 393216 | tf_op jit(solution)/shard_map/all_to_all | solution.py:58
  72.5 0.0 collective-permute-start.3
  72.5 1.4 %collective-permute-done.3 = bf16[16,24,256]{2,1,0:T(8,128)(2,1)S(1)} collective-permute-done((bf16[16,24,256]{2,1,0:T(8,128)(2,1)S(1)}, bf16[16,24,256]{2,1,0:T(8,128)(2,1)S(1)}, u32[]{:S(2)}, u32[]{:S(2)}) %collective-permute-start.3) | collective-permute-done | bytes 196640 | tf_op jit(solution)/shard_map/ppermute | solution.py:24
  74.0 0.2 multiply_reduce_fusion
  74.2 0.1 maximum_convert_fusion
  74.3 0.0 slice-start.5
  74.3 0.1 copy.19
  74.4 0.0 slice-done.2
  74.4 0.0 slice-done.3
  74.4 0.0 copy-start.1
  74.4 0.0 slice-start
  74.4 2.0 %fusion.12 = f32[24,448]{1,0:T(8,128)S(1)} fusion(bf16[8192,448]{0,1:T(8,128)(2,1)S(1)} %bitcast.46, f32[24,8192]{1,0:T(8,128)S(1)} %bitcast.49, f32[24]{0:T(128)S(1)} %add_rsqrt_fusion), kind=kOutput, calls=%fused_computation.42 | convolution fusion | flops 176553984 | bytes 8169568 | tf_op jit(solution)/shard_map/dot_general | solution.py:454
  76.5 0.0 slice-done.4
  76.5 0.0 slice-done.5
  76.5 0.0 slice-start.1
  76.5 2.0 %convolution_multiply_fusion = f32[24,448]{1,0:T(8,128)S(1)} fusion(bf16[8192,448]{0,1:T(8,128)(2,1)S(1)} %bitcast.48, f32[24,448]{1,0:T(8,128)S(1)} %fusion.12, f32[24,8192]{1,0:T(8,128)S(1)} %bitcast.50, f32[24]{0:T(128)S(1)} %add_rsqrt_fusion), kind=kOutput, calls=%fused_computation | convolution fusion | flops 176607744 | bytes 8212576 | tf_op jit(solution)/shard_map/dot_general | solution.py:455
  78.5 0.0 copy-done.1
  78.5 0.3 fusion.13
  78.9 0.2 collective-permute-start.4
  79.0 1.1 collective-permute-done.4
  80.1 1.1 %collective-permute-start.5 = (bf16[24,448]{1,0:T(8,128)(2,1)S(1)}, bf16[24,448]{1,0:T(8,128)(2,1)S(1)}, u32[]{:S(2)}, u32[]{:S(2)}) collective-permute-start(bf16[24,448]{1,0:T(8,128)(2,1)S(1)} %select_convert_fusion), channel_id=1, source_target_pairs={{0,16},{1,17},{2,18},{3,19},{4,20},{5,21},{6,22},{7,23},{8,24},{9,... | collective-permute-start | bytes 64520 | tf_op jit(solution)/shard_map/ppermute | solution.py:24
  81.3 3.7 %collective-permute-done.5 = bf16[24,448]{1,0:T(8,128)(2,1)S(1)} collective-permute-done((bf16[24,448]{1,0:T(8,128)(2,1)S(1)}, bf16[24,448]{1,0:T(8,128)(2,1)S(1)}, u32[]{:S(2)}, u32[]{:S(2)}) %collective-permute-start.5) | collective-permute-done | bytes 21536 | tf_op jit(solution)/shard_map/ppermute | solution.py:24
  85.0 8.8 %all_to_all.40 = bf16[8,24,448]{2,1,0:T(8,128)(2,1)S(1)} all-to-all(bf16[8,24,448]{2,1,0:T(8,128)(2,1)S(1)} %broadcast_in_dim.14), channel_id=1, replica_groups={{0,2,4,6,8,10,12,14},{1,3,5,7,9,11,13,15},{16,18,20,22,24,26,28,30},{17..., dimensions={0} | all-to-all | bytes 344064 | tf_op jit(solution)/shard_map/all_to_all | solution.py:92
  93.8 0.1 multiply_reduce_fusion.1
  93.9 0.0 slice-done
  93.9 0.0 slice-done.1
  93.9 1.4 %shard_map.104 = bf16[2,16,24,256]{3,2,1,0:T(8,128)(2,1)S(1)} custom-call(s32[1]{0:T(128)S(6)} %select_n.50.core_ref.pair_ref, bf16[24,448]{1,0:T(8,128)(2,1)S(1)} %multiply_convert_fusion.1.rotated_ref, bf16[448,8192]{1,0:T(8,128)(2,1)S(1)} %bitcast.42), custom_call_target="tpu_custom_call" | custom-call | flops 176160768 | bytes 7340032 | tf_op jit(solution)/shard_map/pallas_call | solution.py:352
  95.4 0.1 collective-permute-start.6
  95.5 1.4 %collective-permute-done.6 = bf16[16,24,256]{2,1,0:T(8,128)(2,1)S(1)} collective-permute-done((bf16[16,24,256]{2,1,0:T(8,128)(2,1)S(1)}, bf16[16,24,256]{2,1,0:T(8,128)(2,1)S(1)}, u32[]{:S(2)}, u32[]{:S(2)}) %collective-permute-start.6) | collective-permute-done | bytes 196640 | tf_op jit(solution)/shard_map/ppermute | solution.py:24
  96.9 0.1 fusion.1
  96.9 12.1 %all_to_all.41 = bf16[16,24,256]{2,1,0:T(8,128)(2,1)S(1)} all-to-all(bf16[16,24,256]{2,1,0:T(8,128)(2,1)S(1)} %fusion.1), channel_id=1, replica_groups={{0,2,4,6,8,10,12,14,16,18,20,22,24,26,28,30},{1,3,5,7,9,11,13,15,17,19,..., dimensions={0} | all-to-all | bytes 393216 | tf_op jit(solution)/shard_map/all_to_all | solution.py:45
  109.1 0.6 add_convert_fusion.1
  (23 shorter events, 0.4 us)
Async XLA Ops:
  0.0 60.1 %copy-start = (bf16[4096,256]{1,0:T(8,128)(2,1)S(1)}, bf16[4096,256]{1,0:T(8,128)(2,1)}, u32[]{:S(2)}) copy-start(bf16[4096,256]{1,0:T(8,128)(2,1)} %param.15) | copy-start | bytes 6291460
  2.3 1.5 %collective-permute-start = (bf16[16,32,128]{2,1,0:T(8,128)(2,1)S(1)}, bf16[16,32,128]{2,1,0:T(8,128)(2,1)S(1)}, u32[]{:S(2)}, u32[]{:S(2)}) collective-permute-start(bf16[16,32,128]{2,1,0:T(8,128)(2,1)S(1)} %slice_bitcast_fusion.2), channel_id=1, source_target_pairs={{0,1},{1,0},{2,3},{3,2},{4,5},{5,4},{6,7},{7,6},{8,9},{9,8},{10,11... | collective-permute-start | bytes 393224 | tf_op jit(solution)/shard_map/ppermute | solution.py:24
  30.5 4.1 %collective-permute-start.1 = (bf16[16,32,128]{2,1,0:T(8,128)(2,1)S(1)}, bf16[16,32,128]{2,1,0:T(8,128)(2,1)S(1)}, u32[]{:S(2)}, u32[]{:S(2)}) collective-permute-start(bf16[16,32,128]{2,1,0:T(8,128)(2,1)S(1)} %all_to_all.36), channel_id=1, source_target_pairs={{0,1},{1,0},{2,3},{3,2},{4,5},{5,4},{6,7},{7,6},{8,9},{9,8},{10,11... | collective-permute-start | bytes 393224 | tf_op jit(solution)/shard_map/ppermute | solution.py:24
  34.0 4.2 %collective-permute-start.2 = (bf16[16,32,128]{2,1,0:T(8,128)(2,1)S(1)}, bf16[16,32,128]{2,1,0:T(8,128)(2,1)S(1)}, u32[]{:S(2)}, u32[]{:S(2)}) collective-permute-start(bf16[16,32,128]{2,1,0:T(8,128)(2,1)S(1)} %shard_map.102), channel_id=1, source_target_pairs={{0,1},{1,0},{2,3},{3,2},{4,5},{5,4},{6,7},{7,6},{8,9},{9,8},{10,11... | collective-permute-start | bytes 393224 | tf_op jit(solution)/shard_map/ppermute | solution.py:24
  34.6 39.8 %slice-start.2 = ((s8[7340032]{0:T(1024)(128)(4,1)}), s8[4194304]{0:T(1024)(128)(4,1)S(1)}, s32[]{:S(2)}) async-start(s8[7340032]{0:T(1024)(128)(4,1)} %bitcast.45), calls=%async_computation.9 | async-start | bytes 8388608
  34.6 25.5 %copy-start.2 = (bf16[24,256]{1,0:T(8,128)(2,1)S(1)}, bf16[24,256]{1,0:T(8,128)(2,1)}, u32[]{:S(2)}) copy-start(bf16[24,256]{1,0:T(8,128)(2,1)} %hidden_source.1) | copy-start | bytes 36868
  34.6 39.8 %slice-start.3 = ((s8[7340032]{0:T(1024)(128)(4,1)}), s8[3145728]{0:T(1024)(128)(4,1)S(1)}, s32[]{:S(2)}) async-start(s8[7340032]{0:T(1024)(128)(4,1)} %bitcast.45), calls=%async_computation.10 | async-start | bytes 6291456
  38.3 38.1 %slice-start.4 = ((s8[7340032]{0:T(1024)(128)(4,1)}), s8[4194304]{0:T(1024)(128)(4,1)S(1)}, s32[]{:S(2)}) async-start(s8[7340032]{0:T(1024)(128)(4,1)} %bitcast.47), calls=%async_computation.11 | async-start | bytes 8388608
  72.5 1.4 %collective-permute-start.3 = (bf16[16,24,256]{2,1,0:T(8,128)(2,1)S(1)}, bf16[16,24,256]{2,1,0:T(8,128)(2,1)S(1)}, u32[]{:S(2)}, u32[]{:S(2)}) collective-permute-start(bf16[16,24,256]{2,1,0:T(8,128)(2,1)S(1)} %all_to_all.39), channel_id=1, source_target_pairs={{0,1},{1,0},{2,3},{3,2},{4,5},{5,4},{6,7},{7,6},{8,9},{9,8},{10,11... | collective-permute-start | bytes 589832 | tf_op jit(solution)/shard_map/ppermute | solution.py:24
  74.3 2.2 %slice-start.5 = ((s8[7340032]{0:T(1024)(128)(4,1)}), s8[3145728]{0:T(1024)(128)(4,1)S(1)}, s32[]{:S(2)}) async-start(s8[7340032]{0:T(1024)(128)(4,1)} %bitcast.47), calls=%async_computation.12 | async-start | bytes 6291456
  74.4 4.1 %copy-start.1 = (f32[448,448]{1,0:T(8,128)S(1)}, f32[448,448]{1,0:T(8,128)}, u32[]{:S(2)}) copy-start(f32[448,448]{1,0:T(8,128)} %constant.95.clone) | copy-start | bytes 2408452
  74.4 19.5 %slice-start = ((s8[7340032]{0:T(1024)(128)(4,1)}), s8[4194304]{0:T(1024)(128)(4,1)S(1)}, s32[]{:S(2)}) async-start(s8[7340032]{0:T(1024)(128)(4,1)} %bitcast.41), calls=%async_computation.7 | async-start | bytes 8388608
  76.5 17.4 %slice-start.1 = ((s8[7340032]{0:T(1024)(128)(4,1)}), s8[3145728]{0:T(1024)(128)(4,1)S(1)}, s32[]{:S(2)}) async-start(s8[7340032]{0:T(1024)(128)(4,1)} %bitcast.41), calls=%async_computation.8 | async-start | bytes 6291456
  78.9 1.3 %collective-permute-start.4 = (f32[24,448]{1,0:T(8,128)S(1)}, f32[24,448]{1,0:T(8,128)S(1)}, u32[]{:S(2)}, u32[]{:S(2)}) collective-permute-start(f32[24,448]{1,0:T(8,128)S(1)} %fusion.13), channel_id=1, source_target_pairs={{0,1},{1,0},{2,3},{3,2},{4,5},{5,4},{6,7},{7,6},{8,9},{9,8},{10,11... | collective-permute-start | bytes 129032 | tf_op jit(solution)/shard_map/ppermute | solution.py:24
  80.1 4.8 %collective-permute-start.5 = (bf16[24,448]{1,0:T(8,128)(2,1)S(1)}, bf16[24,448]{1,0:T(8,128)(2,1)S(1)}, u32[]{:S(2)}, u32[]{:S(2)}) collective-permute-start(bf16[24,448]{1,0:T(8,128)(2,1)S(1)} %select_convert_fusion), channel_id=1, source_target_pairs={{0,16},{1,17},{2,18},{3,19},{4,20},{5,21},{6,22},{7,23},{8,24},{9,... | collective-permute-start | bytes 64520 | tf_op jit(solution)/shard_map/ppermute | solution.py:24
  95.4 1.5 %collective-permute-start.6 = (bf16[16,24,256]{2,1,0:T(8,128)(2,1)S(1)}, bf16[16,24,256]{2,1,0:T(8,128)(2,1)S(1)}, u32[]{:S(2)}, u32[]{:S(2)}) collective-permute-start(bf16[16,24,256]{2,1,0:T(8,128)(2,1)S(1)} %slice_bitcast_fusion), channel_id=1, source_target_pairs={{0,1},{1,0},{2,3},{3,2},{4,5},{5,4},{6,7},{7,6},{8,9},{9,8},{10,11... | collective-permute-start | bytes 589832 | tf_op jit(solution)/shard_map/ppermute | solution.py:24

commit v7 on v6

--- a/solution.py
+++ b/solution.py
@@ -40,11 +40,32 @@
     return scattered_joined(kept, across(sent, 1))
 
 
-def scattered_joined(kept, arrived):
+def sum_kernel(parts_ref, out_ref):
+    total = parts_ref[0].astype(jnp.float32)
+    for index in range(1, parts_ref.shape[0]):
+        total = total + parts_ref[index].astype(jnp.float32)
+    out_ref[...] = total.astype(out_ref.dtype)
+
+
+def summed(parts):
+    vmem = pl.BlockSpec(memory_space=pltpu.VMEM)
+    return pl.pallas_call(
+        sum_kernel,
+        out_shape=jax.ShapeDtypeStruct(parts.shape[1:], parts.dtype),
+        in_specs=[vmem],
+        out_specs=vmem,
+        compiler_params=pltpu.CompilerParams(vmem_limit_bytes=2**20),
+        cost_estimate=pl.CostEstimate(flops=4000000000, bytes_accessed=16000000, transcendentals=0),
+    )(parts)
+
+
+def scattered_joined(kept, arrived, short=False):
     joined = kept.astype(jnp.float32) + arrived.astype(jnp.float32)
     received = lax.all_to_all(
         joined.astype(jnp.bfloat16), "tensor", 0, 0, tiled=True, axis_index_groups=same_core()
     )
+    if short:
+        return summed(received)
     return jnp.sum(received.astype(jnp.float32), axis=0)
 
 
@@ -205,26 +226,11 @@
 
 
 def attend_kernel(
-    device_ref, pair_ref, lengths_ref, projected_ref, cosine_ref, sine_ref, key_source, value_source,
-    out_ref, keys_ref, values_ref, keys_arrived, values_arrived, queries, fresh, sums,
+    device_ref, pair_ref, lengths_ref, projected_ref, cosine_ref, sine_ref, keys_ref, values_ref,
+    out_ref, queries, fresh, sums,
 ):
-    rows, slots, width = keys_ref.shape
-    columns = pl.ds(pl.multiple_of(pair_ref[0] * width, width), width)
-
-    def copies(index):
-        part = pl.ds(index * ROW_CHUNK, ROW_CHUNK)
-        return (
-            pltpu.make_async_copy(
-                key_source.at[part, :, columns], keys_ref.at[part], keys_arrived.at[index]
-            ),
-            pltpu.make_async_copy(
-                value_source.at[part, :, columns], values_ref.at[part], values_arrived.at[index]
-            ),
-        )
-
-    for index in range(rows // ROW_CHUNK):
-        for copy in copies(index):
-            copy.start()
+    rows, slots = keys_ref.shape[:2]
+    columns = pl.ds(pl.multiple_of(pair_ref[0] * 2 * HD, 2 * HD), 2 * HD)
     device = device_ref[0]
     group = H // KVH
     heads = 2 * group
@@ -260,7 +266,6 @@
         numbers = [step * ROW_CHUNK + offset for offset in range(ROW_CHUNK)]
         scores = []
         own = []
-        copies(step)[0].wait()
         for row in numbers:
             query = queries[pl.ds(pl.multiple_of(row * heads, heads), heads), :]
             own_score = jnp.sum(query * expand(row * 4), axis=1, keepdims=True) * scale
@@ -271,7 +276,7 @@
             scores.append(
                 lax.dot_general(
                     spread,
-                    keys_ref[row],
+                    keys_ref[row, :, columns],
                     (((1,), (1,)), ((), ())),
                     preferred_element_type=jnp.float32,
                 )
@@ -280,10 +285,9 @@
             jnp.where(lane < lengths_ref[pl.ds(row, 1), :1], jnp.exp(score * scale), 0.0)
             for row, score in zip(numbers, scores)
         ]
-        copies(step)[1].wait()
         for row, weight, own_weight in zip(numbers, weights, own):
             product = jnp.dot(
-                weight.astype(jnp.bfloat16), values_ref[row], preferred_element_type=jnp.float32
+                weight.astype(jnp.bfloat16), values_ref[row, :, columns], preferred_element_type=jnp.float32
             )
             chosen = jnp.concatenate([product[:group, :HD], product[group:, HD:]], axis=0)
             total = jnp.sum(weight, axis=1, keepdims=True) + own_weight
@@ -311,56 +315,47 @@
     return pl.pallas_call(
         attend_kernel,
         out_shape=jax.ShapeDtypeStruct((H // 2, rows + 8, HD), jnp.bfloat16),
-        in_specs=[smem] * 2 + [vmem] * 4 + [pl.BlockSpec(memory_space=pltpu.HBM)] * 2,
+        in_specs=[smem] * 2 + [vmem] * 6,
         out_specs=vmem,
         scratch_shapes=[
-            pltpu.VMEM((rows, slots, 2 * HD), key_cache.dtype),
-            pltpu.VMEM((rows, slots, 2 * HD), value_cache.dtype),
-            pltpu.SemaphoreType.DMA((rows // ROW_CHUNK,)),
-            pltpu.SemaphoreType.DMA((rows // ROW_CHUNK,)),
             pltpu.VMEM((rows * H // 2, HD), jnp.float32),
             pltpu.VMEM((rows * 4, HD), jnp.float32),
             pltpu.VMEM((rows * H // 2, HD), jnp.float32),
         ],
-        compiler_params=pltpu.CompilerParams(vmem_limit_bytes=12 * 2**20),
+        compiler_params=pltpu.CompilerParams(vmem_limit_bytes=20 * 2**20),
         cost_estimate=pl.CostEstimate(
             flops=2 * rows * H * slots * HD,
             bytes_accessed=key_cache.size + value_cache.size,
             transcendentals=rows * H * slots // 2,
         ),
-    )(device, pair, lengths, projected, cosine, sine, in_hbm(key_cache), in_hbm(value_cache))
-
-
-def down_kernel(core_ref, rotated_ref, weights_ref, out_ref):
-    core = core_ref[0]
+    )(device, pair, lengths, projected, cosine, sine, key_cache, value_cache)
+
+
+def down_kernel(part_ref, rotated_ref, weights_ref, out_ref):
+    part = part_ref[0]
     rotated = rotated_ref[...]
-    features = weights_ref.shape[1]
-    width = out_ref.shape[3]
-    block = max(width, min(256, features))
-    for start in range(0, features, block):
-        part = jnp.dot(
-            rotated, weights_ref[:, start : start + block], preferred_element_type=jnp.float32
+    pieces, _, width = out_ref.shape
+    for piece in range(pieces):
+        first = pl.multiple_of((2 * piece + part) * width, width)
+        out_ref[piece] = jnp.dot(
+            rotated, weights_ref[:, pl.ds(first, width)], preferred_element_type=jnp.float32
         ).astype(jnp.bfloat16)
-        for offset in range(0, block, width):
-            piece = (start + offset) // width
-            out_ref[(piece % 2) ^ core, piece // 2] = part[:, offset : offset + width]
-
-
-def down_pieces(core, rotated, w_down, devices):
-    rows, features = rotated.shape[0], w_down.shape[1]
+
+
+def down_pieces(part, rotated, w_down, devices):
+    rows = rotated.shape[0]
+    width = w_down.shape[1] // devices
     vmem = pl.BlockSpec(memory_space=pltpu.VMEM)
     return pl.pallas_call(
         down_kernel,
-        out_shape=jax.ShapeDtypeStruct((2, devices // 2, rows, features // devices), jnp.bfloat16),
+        out_shape=jax.ShapeDtypeStruct((devices // 2, rows, width), jnp.bfloat16),
         in_specs=[pl.BlockSpec(memory_space=pltpu.SMEM), vmem, vmem],
         out_specs=vmem,
         compiler_params=pltpu.CompilerParams(vmem_limit_bytes=12 * 2**20),
         cost_estimate=pl.CostEstimate(
-            flops=2 * rows * rotated.shape[1] * features,
-            bytes_accessed=w_down.size * 2,
-            transcendentals=0,
+            flops=rows * w_down.size, bytes_accessed=w_down.size, transcendentals=0
         ),
-    )(core, rotated, w_down)
+    )(part, rotated, w_down)
 
 
 def paley_table():
@@ -415,7 +410,7 @@
     arrived, cosine, sine, lengths, other, second, upper, signs = lax.optimization_barrier(
         (arrived, cosine, sine, lengths, 1 - core, second, upper, signs)
     )
-    piece = scattered_joined(halves[0], arrived).astype(jnp.bfloat16)
+    piece = scattered_joined(halves[0], arrived, True)
     mine = gathered_same_core(piece)
     theirs = across(mine, 1)
     shared = (lengths, cosine, sine, key_cache, value_cache)
@@ -461,8 +456,13 @@
     mixed = jnp.dot(activation, local_table, precision=lax.Precision.HIGH)
     rotated = signed_sum(mixed, second, upper, signs)
     rotated = (rotated * FF ** (-0.5)).astype(jnp.bfloat16)
-    halves = down_pieces(core, rotated, w_down, devices)
-    down_share = scattered_halves(halves[0], halves[1])
+    if D // devices % HD == 0:
+        sent = down_pieces(other, rotated, w_down, devices)
+        arrived = across(sent, 1)
+        down_share = scattered_joined(down_pieces(core, rotated, w_down, devices), arrived)
+    else:
+        down = jnp.dot(rotated, w_down, preferred_element_type=jnp.float32)
+        down_share = scattered_sum(down.reshape(row_count, devices, -1).transpose(1, 0, 2), second)
     return (residual.astype(jnp.float32) + down_share).astype(jnp.bfloat16)
 
 

time: 110 us -> 106 us (0.964)
  Pallas kernels: 10.8 us -> 7.52 us
    pallas_call x2, Pallas kernels: 7.06 us -> 3.6 us  [attended_pair(): pl.pallas_call(attend_kernel, out_shape=jax.ShapeDtypeStruct((H // 2, row...]
  transfers between devices with their start and end apart: 7 -> 7, of which waited for: 5 -> 5; matrix products, arithmetic and copies ran while one was open for 1% -> 1% of each run, Pallas kernels for 6% -> 4%
where the time goes in v7:
time: 106 us
  blocking collectives  81.5 us (77%)
  Pallas kernels  7.52 us (7%)
  waiting for transfers between devices  6.94 us (7%)
  matrix products  4.76 us (4%)
  starting transfers between devices  2.41 us (2%)
  other arithmetic  2.13 us (2%)
    all_to_all x3, blocking collectives, scattered_joined(): lax.all_to_all(joined.astype(jnp.bfloat16), 'tensor', 0, 0, tiled=True, a...  39 us
    all_to_all x2, blocking collectives, gathered_same_core(): lax.all_to_all(copies, 'tensor', 0, 0, tiled=True, axis_index_groups=same...  23 us
    all_to_all x1, blocking collectives, gathered_at_once(): return lax.all_to_all(copies, 'tensor', 0, 0, tiled=True)  10.8 us
    all_to_all x1, blocking collectives, signed_sum(): lax.all_to_all(copies, 'tensor', 0, 0, tiled=True, axis_index_groups=groups)  8.78 us
    ppermute x7, waiting for transfers between devices, across(): return lax.ppermute(value, 'tensor', pairs)  6.94 us
    pallas_call x2, Pallas kernels, attended_pair(): pl.pallas_call(attend_kernel, out_shape=jax.ShapeDtypeStruct((H // 2, row...  3.6 us
    ppermute x7, starting transfers between devices, across(): return lax.ppermute(value, 'tensor', pairs)  2.41 us
    pallas_call x1, Pallas kernels, projected_pieces(): pl.pallas_call(project_kernel, out_shape=jax.ShapeDtypeStruct((2, devices...  2.24 us
  transfers between devices with their start and end apart: 7, of which 5 were waited for; matrix products, arithmetic and copies ran while one was open for 1% of the time, Pallas kernels for 4%

profile of v7, /device:TPU:0, one launch (start us, length us, event | category | flops | bytes accessed | tf_op | source)
XLA Modules:
  0.0 106.1 jit_solution(9003455571165986649)
XLA Ops:
  0.0 0.0 copy-start
  0.0 2.2 %shard_map.100 = bf16[2,16,32,128]{3,2,1,0:T(8,128)(2,1)S(1)} custom-call(s32[1]{0:T(128)S(6)} %select_n.50.core_ref.pair_ref.part_ref, bf16[24,256]{1,0:T(8,128)(2,1)} %hidden_source.1, bf16[256,5120]{1,0:T(8,128)(2,1)} %source_ref.1), custom_call_target="tpu_custom_call" | custom-call | flops 62914560 | bytes 2621440 | tf_op jit(solution)/shard_map/pallas_call | solution.py:205
  2.3 0.5 collective-permute-start
  2.8 0.7 convert_element_type.93
  3.5 0.1 fusion.6
  3.6 0.1 pad_maximum_fusion
  3.7 0.1 collective-permute-done
  3.8 0.1 broadcast_in_dim.10.lengths_ref
  3.9 0.0 slice-start.2
  3.9 16.1 %all_to_all.35.parts_ref = bf16[16,32,128]{2,1,0:T(8,128)(2,1)S(1)} all-to-all(bf16[16,32,128]{2,1,0:T(8,128)(2,1)S(1)} %fusion.1), channel_id=1, replica_groups={{0,2,4,6,8,10,12,14,16,18,20,22,24,26,28,30},{1,3,5,7,9,11,13,15,17,19,..., dimensions={0} | all-to-all | bytes 262144 | tf_op jit(solution)/shard_map/all_to_all | solution.py:64
  20.0 11.0 %all_to_all.36 = bf16[16,32,128]{2,1,0:T(8,128)(2,1)S(1)} all-to-all(bf16[16,32,128]{2,1,0:T(8,128)(2,1)S(1)} %broadcast_in_dim.11), channel_id=1, replica_groups={{0,2,4,6,8,10,12,14,16,18,20,22,24,26,28,30},{1,3,5,7,9,11,13,15,17,19,..., dimensions={0} | all-to-all | bytes 262144 | tf_op jit(solution)/shard_map/all_to_all | solution.py:79
  31.0 0.1 collective-permute-start.1
  31.1 0.0 slice-done.2
  31.1 0.0 slice-done.3
  31.1 0.0 copy-done.1
  31.2 1.8 %shard_map.103 = bf16[16,32,128]{2,1,0:T(8,128)(2,1)S(1)} custom-call(s32[1]{0:T(128)} %bitcast.device_ref, s32[1]{0:T(128)S(6)} %sub.19.pair_ref.part_ref, f32[24,128]{1,0:T(8,128)S(1)} %broadcast_in_dim.10.lengths_ref, bf16[21,24,128]{2,1,0:T(8,128)(2,1)S(1)} %bitcast.38, f32[24,128]{1,0:T(8,128)S(1)} %get-tuple-element.19.cosine_ref, ...), custom_call_target="tpu_custom_call" | custom-call | flops 50331648 | bytes 6291456 | tf_op jit(solution)/shard_map/pallas_call | solution.py:315
  33.0 0.5 collective-permute-start.2
  33.5 0.0 collective-permute-done.1
  33.5 0.0 slice-start.4
  33.5 0.0 copy-start.3
  33.5 0.0 slice-start.5
  33.5 1.8 %shard_map.102 = bf16[16,32,128]{2,1,0:T(8,128)(2,1)S(1)} custom-call(s32[1]{0:T(128)} %bitcast.device_ref, s32[1]{0:T(128)S(6)} %select_n.50.core_ref.pair_ref.part_ref, f32[24,128]{1,0:T(8,128)S(1)} %broadcast_in_dim.10.lengths_ref, bf16[21,24,128]{2,1,0:T(8,128)(2,1)S(1)} %bitcast.39, f32[24,128]{1,0:T(8,128)S(1)} %get-tuple-element.19.cosine_ref, ...), custom_call_target="tpu_custom_call" | custom-call | flops 50331648 | bytes 6291456 | tf_op jit(solution)/shard_map/pallas_call | solution.py:315
  35.4 0.0 collective-permute-done.2
  35.4 0.0 slice-start.6
  35.4 10.8 %all_to_all.37 = bf16[16,32,128]{2,1,0:T(8,128)(2,1)S(1)} all-to-all(bf16[16,32,128]{2,1,0:T(8,128)(2,1)S(1)} %add_convert_fusion.1), channel_id=1, replica_groups={{0,2,4,6,8,10,12,14,16,18,20,22,24,26,28,30},{1,3,5,7,9,11,13,15,17,19,..., dimensions={0} | all-to-all | bytes 262144 | tf_op jit(solution)/shard_map/all_to_all | solution.py:64
  46.2 0.1 shard_map.104
  46.4 10.8 %all_to_all.38 = bf16[32,24,128]{2,1,0:T(8,128)(2,1)S(1)} all-to-all(bf16[32,24,128]{2,1,0:T(8,128)(2,1)S(1)} %broadcast_in_dim.12), channel_id=1, replica_groups=mesh['groups'=1,'tensor'=32] {'tensor'}, dimensions={0} | all-to-all | bytes 393216 | tf_op jit(solution)/shard_map/all_to_all | solution.py:74
  57.1 0.1 copy.16
  57.2 0.0 copy-done
  57.2 0.0 copy-done.3
  57.2 0.4 fusion
  57.7 12.0 %all_to_all.39 = bf16[16,24,256]{2,1,0:T(8,128)(2,1)S(1)} all-to-all(bf16[16,24,256]{2,1,0:T(8,128)(2,1)S(1)} %broadcast_in_dim.13), channel_id=1, replica_groups={{0,2,4,6,8,10,12,14,16,18,20,22,24,26,28,30},{1,3,5,7,9,11,13,15,17,19,..., dimensions={0} | all-to-all | bytes 393216 | tf_op jit(solution)/shard_map/all_to_all | solution.py:79
  69.6 0.0 collective-permute-start.3
  69.6 1.4 %collective-permute-done.3 = bf16[16,24,256]{2,1,0:T(8,128)(2,1)S(1)} collective-permute-done((bf16[16,24,256]{2,1,0:T(8,128)(2,1)S(1)}, bf16[16,24,256]{2,1,0:T(8,128)(2,1)S(1)}, u32[]{:S(2)}, u32[]{:S(2)}) %collective-permute-start.3) | collective-permute-done | bytes 196640 | tf_op jit(solution)/shard_map/ppermute | solution.py:24
  71.1 0.2 multiply_reduce_fusion
  71.3 0.1 maximum_convert_fusion
  71.4 0.0 slice-start.7
  71.4 0.1 copy.19
  71.5 0.0 slice-done.4
  71.5 0.0 slice-done.5
  71.5 0.0 copy-start.2
  71.5 0.0 slice-start
  71.6 2.0 %fusion.11 = f32[24,448]{1,0:T(8,128)S(1)} fusion(bf16[8192,448]{0,1:T(8,128)(2,1)S(1)} %bitcast.41, f32[24,8192]{1,0:T(8,128)S(1)} %bitcast.44, f32[24]{0:T(128)S(1)} %add_rsqrt_fusion), kind=kOutput, calls=%fused_computation.39 | convolution fusion | flops 176553984 | bytes 8169568 | tf_op jit(solution)/shard_map/dot_general | solution.py:449
  73.6 0.0 slice-done.6
  73.6 0.0 slice-done.7
  73.6 0.0 slice-start.1
  73.6 2.0 %convolution_multiply_fusion = f32[24,448]{1,0:T(8,128)S(1)} fusion(bf16[8192,448]{0,1:T(8,128)(2,1)S(1)} %bitcast.43, f32[24,448]{1,0:T(8,128)S(1)} %fusion.11, f32[24,8192]{1,0:T(8,128)S(1)} %bitcast.45, f32[24]{0:T(128)S(1)} %add_rsqrt_fusion), kind=kOutput, calls=%fused_computation | convolution fusion | flops 176607744 | bytes 8212576 | tf_op jit(solution)/shard_map/dot_general | solution.py:450
  75.6 0.0 copy-done.2
  75.6 0.3 fusion.12
  76.0 0.2 collective-permute-start.4
  76.2 1.1 %collective-permute-done.4 = f32[24,448]{1,0:T(8,128)S(1)} collective-permute-done((f32[24,448]{1,0:T(8,128)S(1)}, f32[24,448]{1,0:T(8,128)S(1)}, u32[]{:S(2)}, u32[]{:S(2)}) %collective-permute-start.4) | collective-permute-done | bytes 43040 | tf_op jit(solution)/shard_map/ppermute | solution.py:24
  77.3 1.1 %collective-permute-start.5 = (bf16[24,448]{1,0:T(8,128)(2,1)S(1)}, bf16[24,448]{1,0:T(8,128)(2,1)S(1)}, u32[]{:S(2)}, u32[]{:S(2)}) collective-permute-start(bf16[24,448]{1,0:T(8,128)(2,1)S(1)} %select_convert_fusion), channel_id=1, source_target_pairs={{0,16},{1,17},{2,18},{3,19},{4,20},{5,21},{6,22},{7,23},{8,24},{9,... | collective-permute-start | bytes 64520 | tf_op jit(solution)/shard_map/ppermute | solution.py:24
  78.4 3.7 %collective-permute-done.5 = bf16[24,448]{1,0:T(8,128)(2,1)S(1)} collective-permute-done((bf16[24,448]{1,0:T(8,128)(2,1)S(1)}, bf16[24,448]{1,0:T(8,128)(2,1)S(1)}, u32[]{:S(2)}, u32[]{:S(2)}) %collective-permute-start.5) | collective-permute-done | bytes 21536 | tf_op jit(solution)/shard_map/ppermute | solution.py:24
  82.1 8.8 %all_to_all.40 = bf16[8,24,448]{2,1,0:T(8,128)(2,1)S(1)} all-to-all(bf16[8,24,448]{2,1,0:T(8,128)(2,1)S(1)} %broadcast_in_dim.14), channel_id=1, replica_groups={{0,2,4,6,8,10,12,14},{1,3,5,7,9,11,13,15},{16,18,20,22,24,26,28,30},{17..., dimensions={0} | all-to-all | bytes 344064 | tf_op jit(solution)/shard_map/all_to_all | solution.py:113
  90.9 0.1 multiply_reduce_fusion.1
  91.0 0.0 slice-done
  91.0 0.0 slice-done.1
  91.0 0.8 shard_map.106
  91.8 0.0 collective-permute-start.6
  91.8 0.8 shard_map.105
  92.6 0.7 collective-permute-done.6
  93.3 0.1 add_convert_fusion
  93.3 12.1 %all_to_all.41 = bf16[16,24,256]{2,1,0:T(8,128)(2,1)S(1)} all-to-all(bf16[16,24,256]{2,1,0:T(8,128)(2,1)S(1)} %add_convert_fusion), channel_id=1, replica_groups={{0,2,4,6,8,10,12,14,16,18,20,22,24,26,28,30},{1,3,5,7,9,11,13,15,17,19,..., dimensions={0} | all-to-all | bytes 393216 | tf_op jit(solution)/shard_map/all_to_all | solution.py:64
  105.5 0.6 add_convert_fusion.2
  (25 shorter events, 0.4 us)
Async XLA Ops:
  0.0 57.2 %copy-start = (bf16[4096,256]{1,0:T(8,128)(2,1)S(1)}, bf16[4096,256]{1,0:T(8,128)(2,1)}, u32[]{:S(2)}) copy-start(bf16[4096,256]{1,0:T(8,128)(2,1)} %param.15) | copy-start | bytes 6291460
  2.3 1.5 %collective-permute-start = (bf16[16,32,128]{2,1,0:T(8,128)(2,1)S(1)}, bf16[16,32,128]{2,1,0:T(8,128)(2,1)S(1)}, u32[]{:S(2)}, u32[]{:S(2)}) collective-permute-start(bf16[16,32,128]{2,1,0:T(8,128)(2,1)S(1)} %slice_bitcast_fusion), channel_id=1, source_target_pairs={{0,1},{1,0},{2,3},{3,2},{4,5},{5,4},{6,7},{7,6},{8,9},{9,8},{10,11... | collective-permute-start | bytes 393224 | tf_op jit(solution)/shard_map/ppermute | solution.py:24
  3.9 27.2 %slice-start.2 = ((s8[6291456]{0:T(1024)(128)(4,1)}), s8[4194304]{0:T(1024)(128)(4,1)S(1)}, s32[]{:S(2)}) async-start(s8[6291456]{0:T(1024)(128)(4,1)} %bitcast.36), calls=%async_computation.9 | async-start | bytes 8388608
  20.0 11.1 %slice-start.3 = ((s8[6291456]{0:T(1024)(128)(4,1)}), s8[2097152]{0:T(1024)(128)(4,1)S(1)}, s32[]{:S(2)}) async-start(s8[6291456]{0:T(1024)(128)(4,1)} %bitcast.36), calls=%async_computation.10 | async-start | bytes 4194304
  20.0 11.1 %copy-start.1 = (bf16[24,256,512]{2,1,0:T(8,128)(2,1)S(1)}, bf16[24,256,512]{2,1,0:T(8,128)(2,1)}, u32[]{:S(2)}) copy-start(bf16[24,256,512]{2,1,0:T(8,128)(2,1)} %values_ref.3) | copy-start | bytes 18874372
  31.0 2.5 %collective-permute-start.1 = (bf16[16,32,128]{2,1,0:T(8,128)(2,1)S(1)}, bf16[16,32,128]{2,1,0:T(8,128)(2,1)S(1)}, u32[]{:S(2)}, u32[]{:S(2)}) collective-permute-start(bf16[16,32,128]{2,1,0:T(8,128)(2,1)S(1)} %all_to_all.36), channel_id=1, source_target_pairs={{0,1},{1,0},{2,3},{3,2},{4,5},{5,4},{6,7},{7,6},{8,9},{9,8},{10,11... | collective-permute-start | bytes 393224 | tf_op jit(solution)/shard_map/ppermute | solution.py:24
  33.0 2.4 %collective-permute-start.2 = (bf16[16,32,128]{2,1,0:T(8,128)(2,1)S(1)}, bf16[16,32,128]{2,1,0:T(8,128)(2,1)S(1)}, u32[]{:S(2)}, u32[]{:S(2)}) collective-permute-start(bf16[16,32,128]{2,1,0:T(8,128)(2,1)S(1)} %shard_map.103), channel_id=1, source_target_pairs={{0,1},{1,0},{2,3},{3,2},{4,5},{5,4},{6,7},{7,6},{8,9},{9,8},{10,11... | collective-permute-start | bytes 393224 | tf_op jit(solution)/shard_map/ppermute | solution.py:24
  33.5 38.0 %slice-start.4 = ((s8[7340032]{0:T(1024)(128)(4,1)}), s8[4194304]{0:T(1024)(128)(4,1)S(1)}, s32[]{:S(2)}) async-start(s8[7340032]{0:T(1024)(128)(4,1)} %bitcast.40), calls=%async_computation.11 | async-start | bytes 8388608
  33.5 23.7 %copy-start.3 = (bf16[24,256]{1,0:T(8,128)(2,1)S(1)}, bf16[24,256]{1,0:T(8,128)(2,1)}, u32[]{:S(2)}) copy-start(bf16[24,256]{1,0:T(8,128)(2,1)} %hidden_source.1) | copy-start | bytes 36868
  33.5 38.0 %slice-start.5 = ((s8[7340032]{0:T(1024)(128)(4,1)}), s8[3145728]{0:T(1024)(128)(4,1)S(1)}, s32[]{:S(2)}) async-start(s8[7340032]{0:T(1024)(128)(4,1)} %bitcast.40), calls=%async_computation.12 | async-start | bytes 6291456
  35.4 38.1 %slice-start.6 = ((s8[7340032]{0:T(1024)(128)(4,1)}), s8[4194304]{0:T(1024)(128)(4,1)S(1)}, s32[]{:S(2)}) async-start(s8[7340032]{0:T(1024)(128)(4,1)} %bitcast.42), calls=%async_computation.13 | async-start | bytes 8388608
  69.6 1.4 %collective-permute-start.3 = (bf16[16,24,256]{2,1,0:T(8,128)(2,1)S(1)}, bf16[16,24,256]{2,1,0:T(8,128)(2,1)S(1)}, u32[]{:S(2)}, u32[]{:S(2)}) collective-permute-start(bf16[16,24,256]{2,1,0:T(8,128)(2,1)S(1)} %all_to_all.39), channel_id=1, source_target_pairs={{0,1},{1,0},{2,3},{3,2},{4,5},{5,4},{6,7},{7,6},{8,9},{9,8},{10,11... | collective-permute-start | bytes 589832 | tf_op jit(solution)/shard_map/ppermute | solution.py:24
  71.4 2.2 %slice-start.7 = ((s8[7340032]{0:T(1024)(128)(4,1)}), s8[3145728]{0:T(1024)(128)(4,1)S(1)}, s32[]{:S(2)}) async-start(s8[7340032]{0:T(1024)(128)(4,1)} %bitcast.42), calls=%async_computation.14 | async-start | bytes 6291456
  71.5 4.1 %copy-start.2 = (f32[448,448]{1,0:T(8,128)S(1)}, f32[448,448]{1,0:T(8,128)}, u32[]{:S(2)}) copy-start(f32[448,448]{1,0:T(8,128)} %constant.93.clone) | copy-start | bytes 2408452
  71.5 19.5 %slice-start = ((s8[7340032]{0:T(1024)(128)(4,1)}), s8[4194304]{0:T(1024)(128)(4,1)S(1)}, s32[]{:S(2)}) async-start(s8[7340032]{0:T(1024)(128)(4,1)} %bitcast.34), calls=%async_computation.7 | async-start | bytes 8388608
  73.6 17.4 %slice-start.1 = ((s8[7340032]{0:T(1024)(128)(4,1)}), s8[3145728]{0:T(1024)(128)(4,1)S(1)}, s32[]{:S(2)}) async-start(s8[7340032]{0:T(1024)(128)(4,1)} %bitcast.34), calls=%async_computation.8 | async-start | bytes 6291456
  76.0 1.3 %collective-permute-start.4 = (f32[24,448]{1,0:T(8,128)S(1)}, f32[24,448]{1,0:T(8,128)S(1)}, u32[]{:S(2)}, u32[]{:S(2)}) collective-permute-start(f32[24,448]{1,0:T(8,128)S(1)} %fusion.12), channel_id=1, source_target_pairs={{0,1},{1,0},{2,3},{3,2},{4,5},{5,4},{6,7},{7,6},{8,9},{9,8},{10,11... | collective-permute-start | bytes 129032 | tf_op jit(solution)/shard_map/ppermute | solution.py:24
  77.3 4.8 %collective-permute-start.5 = (bf16[24,448]{1,0:T(8,128)(2,1)S(1)}, bf16[24,448]{1,0:T(8,128)(2,1)S(1)}, u32[]{:S(2)}, u32[]{:S(2)}) collective-permute-start(bf16[24,448]{1,0:T(8,128)(2,1)S(1)} %select_convert_fusion), channel_id=1, source_target_pairs={{0,16},{1,17},{2,18},{3,19},{4,20},{5,21},{6,22},{7,23},{8,24},{9,... | collective-permute-start | bytes 64520 | tf_op jit(solution)/shard_map/ppermute | solution.py:24
  91.8 1.5 %collective-permute-start.6 = (bf16[16,24,256]{2,1,0:T(8,128)(2,1)S(1)}, bf16[16,24,256]{2,1,0:T(8,128)(2,1)S(1)}, u32[]{:S(2)}, u32[]{:S(2)}) collective-permute-start(bf16[16,24,256]{2,1,0:T(8,128)(2,1)S(1)} %shard_map.106), channel_id=1, source_target_pairs={{0,1},{1,0},{2,3},{3,2},{4,5},{5,4},{6,7},{7,6},{8,9},{9,8},{10,11... | collective-permute-start | bytes 589832 | tf_op jit(solution)/shard_map/ppermute | solution.py:24

commit v8 on v7

--- a/solution.py
+++ b/solution.py
@@ -16,7 +16,7 @@
 EPSILON = 1e-05
 ROPE_BASE = 500000.0
 QKV_CHUNK = 2560
-ROW_CHUNK = 8
+ROW_CHUNK = 24
 
 
 def across(value, apart):

time: 106 us -> 106 us (level)
  transfers between devices with their start and end apart: 7 -> 7, of which waited for: 5 -> 5; matrix products, arithmetic and copies ran while one was open for 1% -> 1% of each run, Pallas kernels for 4% -> 3%
where the time goes in v8:
time: 106 us; the launch traced here: 105 us
  blocking collectives  81.6 us (77%)
  waiting for transfers between devices  6.94 us (7%)
  Pallas kernels  6.81 us (6%)
  matrix products  4.76 us (4%)
  starting transfers between devices  2.43 us (2%)
  other arithmetic  2.13 us (2%)
    all_to_all x3, blocking collectives, scattered_joined(): lax.all_to_all(joined.astype(jnp.bfloat16), 'tensor', 0, 0, tiled=True, a...  39.1 us
    all_to_all x2, blocking collectives, gathered_same_core(): lax.all_to_all(copies, 'tensor', 0, 0, tiled=True, axis_index_groups=same...  23 us
    all_to_all x1, blocking collectives, gathered_at_once(): return lax.all_to_all(copies, 'tensor', 0, 0, tiled=True)  10.8 us
    all_to_all x1, blocking collectives, signed_sum(): lax.all_to_all(copies, 'tensor', 0, 0, tiled=True, axis_index_groups=groups)  8.78 us
    ppermute x7, waiting for transfers between devices, across(): return lax.ppermute(value, 'tensor', pairs)  6.94 us
    pallas_call x2, Pallas kernels, attended_pair(): pl.pallas_call(attend_kernel, out_shape=jax.ShapeDtypeStruct((H // 2, row...  2.9 us
    ppermute x7, starting transfers between devices, across(): return lax.ppermute(value, 'tensor', pairs)  2.43 us
    pallas_call x1, Pallas kernels, projected_pieces(): pl.pallas_call(project_kernel, out_shape=jax.ShapeDtypeStruct((2, devices...  2.24 us
  transfers between devices with their start and end apart: 7, of which 5 were waited for; matrix products, arithmetic and copies ran while one was open for 1% of the time, Pallas kernels for 3%

profile of v8, /device:TPU:0, one launch (start us, length us, event | category | flops | bytes accessed | tf_op | source)
XLA Modules:
  0.0 105.5 jit_solution(6262011869582062614)
XLA Ops:
  0.0 0.0 copy-start
  0.0 2.2 %shard_map.100 = bf16[2,16,32,128]{3,2,1,0:T(8,128)(2,1)S(1)} custom-call(s32[1]{0:T(128)S(6)} %select_n.50.core_ref.pair_ref.part_ref, bf16[24,256]{1,0:T(8,128)(2,1)} %hidden_source.1, bf16[256,5120]{1,0:T(8,128)(2,1)} %source_ref.1), custom_call_target="tpu_custom_call" | custom-call | flops 62914560 | bytes 2621440 | tf_op jit(solution)/shard_map/pallas_call | solution.py:205
  2.3 0.5 collective-permute-start
  2.8 0.7 convert_element_type.93
  3.5 0.1 fusion.6
  3.6 0.1 pad_maximum_fusion
  3.7 0.1 collective-permute-done
  3.8 0.1 broadcast_in_dim.10.lengths_ref
  3.9 0.0 slice-start.2
  3.9 16.1 %all_to_all.35.parts_ref = bf16[16,32,128]{2,1,0:T(8,128)(2,1)S(1)} all-to-all(bf16[16,32,128]{2,1,0:T(8,128)(2,1)S(1)} %fusion.1), channel_id=1, replica_groups={{0,2,4,6,8,10,12,14,16,18,20,22,24,26,28,30},{1,3,5,7,9,11,13,15,17,19,..., dimensions={0} | all-to-all | bytes 262144 | tf_op jit(solution)/shard_map/all_to_all | solution.py:64
  20.0 11.0 %all_to_all.36 = bf16[16,32,128]{2,1,0:T(8,128)(2,1)S(1)} all-to-all(bf16[16,32,128]{2,1,0:T(8,128)(2,1)S(1)} %broadcast_in_dim.11), channel_id=1, replica_groups={{0,2,4,6,8,10,12,14,16,18,20,22,24,26,28,30},{1,3,5,7,9,11,13,15,17,19,..., dimensions={0} | all-to-all | bytes 262144 | tf_op jit(solution)/shard_map/all_to_all | solution.py:79
  31.0 0.1 collective-permute-start.1
  31.1 0.0 slice-done.2
  31.1 0.0 slice-done.3
  31.1 0.0 copy-done.1
  31.2 1.4 %shard_map.103 = bf16[16,32,128]{2,1,0:T(8,128)(2,1)S(1)} custom-call(s32[1]{0:T(128)} %bitcast.device_ref, s32[1]{0:T(128)S(6)} %sub.19.pair_ref.part_ref, f32[24,128]{1,0:T(8,128)S(1)} %broadcast_in_dim.10.lengths_ref, bf16[21,24,128]{2,1,0:T(8,128)(2,1)S(1)} %bitcast.38, f32[24,128]{1,0:T(8,128)S(1)} %get-tuple-element.19.cosine_ref, ...), custom_call_target="tpu_custom_call" | custom-call | flops 50331648 | bytes 6291456 | tf_op jit(solution)/shard_map/pallas_call | solution.py:315
  32.6 0.6 collective-permute-start.2
  33.2 0.0 collective-permute-done.1
  33.2 0.0 slice-start.4
  33.2 0.0 copy-start.3
  33.2 0.0 slice-start.5
  33.2 1.5 %shard_map.102 = bf16[16,32,128]{2,1,0:T(8,128)(2,1)S(1)} custom-call(s32[1]{0:T(128)} %bitcast.device_ref, s32[1]{0:T(128)S(6)} %select_n.50.core_ref.pair_ref.part_ref, f32[24,128]{1,0:T(8,128)S(1)} %broadcast_in_dim.10.lengths_ref, bf16[21,24,128]{2,1,0:T(8,128)(2,1)S(1)} %bitcast.39, f32[24,128]{1,0:T(8,128)S(1)} %get-tuple-element.19.cosine_ref, ...), custom_call_target="tpu_custom_call" | custom-call | flops 50331648 | bytes 6291456 | tf_op jit(solution)/shard_map/pallas_call | solution.py:315
  34.7 0.0 collective-permute-done.2
  34.7 0.0 slice-start.6
  34.7 10.9 %all_to_all.37 = bf16[16,32,128]{2,1,0:T(8,128)(2,1)S(1)} all-to-all(bf16[16,32,128]{2,1,0:T(8,128)(2,1)S(1)} %add_convert_fusion.1), channel_id=1, replica_groups={{0,2,4,6,8,10,12,14,16,18,20,22,24,26,28,30},{1,3,5,7,9,11,13,15,17,19,..., dimensions={0} | all-to-all | bytes 262144 | tf_op jit(solution)/shard_map/all_to_all | solution.py:64
  45.6 0.1 shard_map.104
  45.8 10.8 %all_to_all.38 = bf16[32,24,128]{2,1,0:T(8,128)(2,1)S(1)} all-to-all(bf16[32,24,128]{2,1,0:T(8,128)(2,1)S(1)} %broadcast_in_dim.12), channel_id=1, replica_groups=mesh['groups'=1,'tensor'=32] {'tensor'}, dimensions={0} | all-to-all | bytes 393216 | tf_op jit(solution)/shard_map/all_to_all | solution.py:74
  56.6 0.1 copy.16
  56.6 0.0 copy-done
  56.6 0.0 copy-done.3
  56.6 0.4 fusion
  57.1 12.0 %all_to_all.39 = bf16[16,24,256]{2,1,0:T(8,128)(2,1)S(1)} all-to-all(bf16[16,24,256]{2,1,0:T(8,128)(2,1)S(1)} %broadcast_in_dim.13), channel_id=1, replica_groups={{0,2,4,6,8,10,12,14,16,18,20,22,24,26,28,30},{1,3,5,7,9,11,13,15,17,19,..., dimensions={0} | all-to-all | bytes 393216 | tf_op jit(solution)/shard_map/all_to_all | solution.py:79
  69.1 0.0 collective-permute-start.3
  69.1 1.4 %collective-permute-done.3 = bf16[16,24,256]{2,1,0:T(8,128)(2,1)S(1)} collective-permute-done((bf16[16,24,256]{2,1,0:T(8,128)(2,1)S(1)}, bf16[16,24,256]{2,1,0:T(8,128)(2,1)S(1)}, u32[]{:S(2)}, u32[]{:S(2)}) %collective-permute-start.3) | collective-permute-done | bytes 196640 | tf_op jit(solution)/shard_map/ppermute | solution.py:24
  70.5 0.2 multiply_reduce_fusion
  70.8 0.1 maximum_convert_fusion
  70.8 0.0 slice-start.7
  70.8 0.1 copy.19
  70.9 0.0 slice-done.4
  70.9 0.0 slice-done.5
  70.9 0.0 copy-start.2
  71.0 0.0 slice-start
  71.0 2.0 %fusion.11 = f32[24,448]{1,0:T(8,128)S(1)} fusion(bf16[8192,448]{0,1:T(8,128)(2,1)S(1)} %bitcast.41, f32[24,8192]{1,0:T(8,128)S(1)} %bitcast.44, f32[24]{0:T(128)S(1)} %add_rsqrt_fusion), kind=kOutput, calls=%fused_computation.39 | convolution fusion | flops 176553984 | bytes 8169568 | tf_op jit(solution)/shard_map/dot_general | solution.py:449
  73.0 0.0 slice-done.6
  73.0 0.0 slice-done.7
  73.0 0.0 slice-start.1
  73.0 2.0 %convolution_multiply_fusion = f32[24,448]{1,0:T(8,128)S(1)} fusion(bf16[8192,448]{0,1:T(8,128)(2,1)S(1)} %bitcast.43, f32[24,448]{1,0:T(8,128)S(1)} %fusion.11, f32[24,8192]{1,0:T(8,128)S(1)} %bitcast.45, f32[24]{0:T(128)S(1)} %add_rsqrt_fusion), kind=kOutput, calls=%fused_computation | convolution fusion | flops 176607744 | bytes 8212576 | tf_op jit(solution)/shard_map/dot_general | solution.py:450
  75.0 0.0 copy-done.2
  75.1 0.3 fusion.12
  75.4 0.2 collective-permute-start.4
  75.6 1.1 %collective-permute-done.4 = f32[24,448]{1,0:T(8,128)S(1)} collective-permute-done((f32[24,448]{1,0:T(8,128)S(1)}, f32[24,448]{1,0:T(8,128)S(1)}, u32[]{:S(2)}, u32[]{:S(2)}) %collective-permute-start.4) | collective-permute-done | bytes 43040 | tf_op jit(solution)/shard_map/ppermute | solution.py:24
  76.7 1.1 %collective-permute-start.5 = (bf16[24,448]{1,0:T(8,128)(2,1)S(1)}, bf16[24,448]{1,0:T(8,128)(2,1)S(1)}, u32[]{:S(2)}, u32[]{:S(2)}) collective-permute-start(bf16[24,448]{1,0:T(8,128)(2,1)S(1)} %select_convert_fusion), channel_id=1, source_target_pairs={{0,16},{1,17},{2,18},{3,19},{4,20},{5,21},{6,22},{7,23},{8,24},{9,... | collective-permute-start | bytes 64520 | tf_op jit(solution)/shard_map/ppermute | solution.py:24
  77.8 3.7 %collective-permute-done.5 = bf16[24,448]{1,0:T(8,128)(2,1)S(1)} collective-permute-done((bf16[24,448]{1,0:T(8,128)(2,1)S(1)}, bf16[24,448]{1,0:T(8,128)(2,1)S(1)}, u32[]{:S(2)}, u32[]{:S(2)}) %collective-permute-start.5) | collective-permute-done | bytes 21536 | tf_op jit(solution)/shard_map/ppermute | solution.py:24
  81.5 8.8 %all_to_all.40 = bf16[8,24,448]{2,1,0:T(8,128)(2,1)S(1)} all-to-all(bf16[8,24,448]{2,1,0:T(8,128)(2,1)S(1)} %broadcast_in_dim.14), channel_id=1, replica_groups={{0,2,4,6,8,10,12,14},{1,3,5,7,9,11,13,15},{16,18,20,22,24,26,28,30},{17..., dimensions={0} | all-to-all | bytes 344064 | tf_op jit(solution)/shard_map/all_to_all | solution.py:113
  90.3 0.1 multiply_reduce_fusion.1
  90.4 0.0 slice-done
  90.4 0.0 slice-done.1
  90.4 0.8 shard_map.106
  91.2 0.0 collective-permute-start.6
  91.2 0.8 shard_map.105
  92.0 0.7 collective-permute-done.6
  92.7 0.1 add_convert_fusion
  92.7 12.1 %all_to_all.41 = bf16[16,24,256]{2,1,0:T(8,128)(2,1)S(1)} all-to-all(bf16[16,24,256]{2,1,0:T(8,128)(2,1)S(1)} %add_convert_fusion), channel_id=1, replica_groups={{0,2,4,6,8,10,12,14,16,18,20,22,24,26,28,30},{1,3,5,7,9,11,13,15,17,19,..., dimensions={0} | all-to-all | bytes 393216 | tf_op jit(solution)/shard_map/all_to_all | solution.py:64
  104.9 0.6 add_convert_fusion.2
  (25 shorter events, 0.4 us)
Async XLA Ops:
  0.0 56.6 %copy-start = (bf16[4096,256]{1,0:T(8,128)(2,1)S(1)}, bf16[4096,256]{1,0:T(8,128)(2,1)}, u32[]{:S(2)}) copy-start(bf16[4096,256]{1,0:T(8,128)(2,1)} %param.15) | copy-start | bytes 6291460
  2.3 1.5 %collective-permute-start = (bf16[16,32,128]{2,1,0:T(8,128)(2,1)S(1)}, bf16[16,32,128]{2,1,0:T(8,128)(2,1)S(1)}, u32[]{:S(2)}, u32[]{:S(2)}) collective-permute-start(bf16[16,32,128]{2,1,0:T(8,128)(2,1)S(1)} %slice_bitcast_fusion), channel_id=1, source_target_pairs={{0,1},{1,0},{2,3},{3,2},{4,5},{5,4},{6,7},{7,6},{8,9},{9,8},{10,11... | collective-permute-start | bytes 393224 | tf_op jit(solution)/shard_map/ppermute | solution.py:24
  3.9 27.2 %slice-start.2 = ((s8[6291456]{0:T(1024)(128)(4,1)}), s8[4194304]{0:T(1024)(128)(4,1)S(1)}, s32[]{:S(2)}) async-start(s8[6291456]{0:T(1024)(128)(4,1)} %bitcast.36), calls=%async_computation.9 | async-start | bytes 8388608
  20.0 11.1 %slice-start.3 = ((s8[6291456]{0:T(1024)(128)(4,1)}), s8[2097152]{0:T(1024)(128)(4,1)S(1)}, s32[]{:S(2)}) async-start(s8[6291456]{0:T(1024)(128)(4,1)} %bitcast.36), calls=%async_computation.10 | async-start | bytes 4194304
  20.0 11.1 %copy-start.1 = (bf16[24,256,512]{2,1,0:T(8,128)(2,1)S(1)}, bf16[24,256,512]{2,1,0:T(8,128)(2,1)}, u32[]{:S(2)}) copy-start(bf16[24,256,512]{2,1,0:T(8,128)(2,1)} %values_ref.3) | copy-start | bytes 18874372
  31.0 2.1 %collective-permute-start.1 = (bf16[16,32,128]{2,1,0:T(8,128)(2,1)S(1)}, bf16[16,32,128]{2,1,0:T(8,128)(2,1)S(1)}, u32[]{:S(2)}, u32[]{:S(2)}) collective-permute-start(bf16[16,32,128]{2,1,0:T(8,128)(2,1)S(1)} %all_to_all.36), channel_id=1, source_target_pairs={{0,1},{1,0},{2,3},{3,2},{4,5},{5,4},{6,7},{7,6},{8,9},{9,8},{10,11... | collective-permute-start | bytes 393224 | tf_op jit(solution)/shard_map/ppermute | solution.py:24
  32.6 2.1 %collective-permute-start.2 = (bf16[16,32,128]{2,1,0:T(8,128)(2,1)S(1)}, bf16[16,32,128]{2,1,0:T(8,128)(2,1)S(1)}, u32[]{:S(2)}, u32[]{:S(2)}) collective-permute-start(bf16[16,32,128]{2,1,0:T(8,128)(2,1)S(1)} %shard_map.103), channel_id=1, source_target_pairs={{0,1},{1,0},{2,3},{3,2},{4,5},{5,4},{6,7},{7,6},{8,9},{9,8},{10,11... | collective-permute-start | bytes 393224 | tf_op jit(solution)/shard_map/ppermute | solution.py:24
  33.2 37.7 %slice-start.4 = ((s8[7340032]{0:T(1024)(128)(4,1)}), s8[4194304]{0:T(1024)(128)(4,1)S(1)}, s32[]{:S(2)}) async-start(s8[7340032]{0:T(1024)(128)(4,1)} %bitcast.40), calls=%async_computation.11 | async-start | bytes 8388608
  33.2 23.4 %copy-start.3 = (bf16[24,256]{1,0:T(8,128)(2,1)S(1)}, bf16[24,256]{1,0:T(8,128)(2,1)}, u32[]{:S(2)}) copy-start(bf16[24,256]{1,0:T(8,128)(2,1)} %hidden_source.1) | copy-start | bytes 36868
  33.2 37.7 %slice-start.5 = ((s8[7340032]{0:T(1024)(128)(4,1)}), s8[3145728]{0:T(1024)(128)(4,1)S(1)}, s32[]{:S(2)}) async-start(s8[7340032]{0:T(1024)(128)(4,1)} %bitcast.40), calls=%async_computation.12 | async-start | bytes 6291456
  34.7 38.2 %slice-start.6 = ((s8[7340032]{0:T(1024)(128)(4,1)}), s8[4194304]{0:T(1024)(128)(4,1)S(1)}, s32[]{:S(2)}) async-start(s8[7340032]{0:T(1024)(128)(4,1)} %bitcast.42), calls=%async_computation.13 | async-start | bytes 8388608
  69.1 1.4 %collective-permute-start.3 = (bf16[16,24,256]{2,1,0:T(8,128)(2,1)S(1)}, bf16[16,24,256]{2,1,0:T(8,128)(2,1)S(1)}, u32[]{:S(2)}, u32[]{:S(2)}) collective-permute-start(bf16[16,24,256]{2,1,0:T(8,128)(2,1)S(1)} %all_to_all.39), channel_id=1, source_target_pairs={{0,1},{1,0},{2,3},{3,2},{4,5},{5,4},{6,7},{7,6},{8,9},{9,8},{10,11... | collective-permute-start | bytes 589832 | tf_op jit(solution)/shard_map/ppermute | solution.py:24
  70.8 2.2 %slice-start.7 = ((s8[7340032]{0:T(1024)(128)(4,1)}), s8[3145728]{0:T(1024)(128)(4,1)S(1)}, s32[]{:S(2)}) async-start(s8[7340032]{0:T(1024)(128)(4,1)} %bitcast.42), calls=%async_computation.14 | async-start | bytes 6291456
  70.9 4.1 %copy-start.2 = (f32[448,448]{1,0:T(8,128)S(1)}, f32[448,448]{1,0:T(8,128)}, u32[]{:S(2)}) copy-start(f32[448,448]{1,0:T(8,128)} %constant.93.clone) | copy-start | bytes 2408452
  71.0 19.5 %slice-start = ((s8[7340032]{0:T(1024)(128)(4,1)}), s8[4194304]{0:T(1024)(128)(4,1)S(1)}, s32[]{:S(2)}) async-start(s8[7340032]{0:T(1024)(128)(4,1)} %bitcast.34), calls=%async_computation.7 | async-start | bytes 8388608
  73.0 17.4 %slice-start.1 = ((s8[7340032]{0:T(1024)(128)(4,1)}), s8[3145728]{0:T(1024)(128)(4,1)S(1)}, s32[]{:S(2)}) async-start(s8[7340032]{0:T(1024)(128)(4,1)} %bitcast.34), calls=%async_computation.8 | async-start | bytes 6291456
  75.4 1.3 %collective-permute-start.4 = (f32[24,448]{1,0:T(8,128)S(1)}, f32[24,448]{1,0:T(8,128)S(1)}, u32[]{:S(2)}, u32[]{:S(2)}) collective-permute-start(f32[24,448]{1,0:T(8,128)S(1)} %fusion.12), channel_id=1, source_target_pairs={{0,1},{1,0},{2,3},{3,2},{4,5},{5,4},{6,7},{7,6},{8,9},{9,8},{10,11... | collective-permute-start | bytes 129032 | tf_op jit(solution)/shard_map/ppermute | solution.py:24
  76.7 4.8 %collective-permute-start.5 = (bf16[24,448]{1,0:T(8,128)(2,1)S(1)}, bf16[24,448]{1,0:T(8,128)(2,1)S(1)}, u32[]{:S(2)}, u32[]{:S(2)}) collective-permute-start(bf16[24,448]{1,0:T(8,128)(2,1)S(1)} %select_convert_fusion), channel_id=1, source_target_pairs={{0,16},{1,17},{2,18},{3,19},{4,20},{5,21},{6,22},{7,23},{8,24},{9,... | collective-permute-start | bytes 64520 | tf_op jit(solution)/shard_map/ppermute | solution.py:24
  91.2 1.5 %collective-permute-start.6 = (bf16[16,24,256]{2,1,0:T(8,128)(2,1)S(1)}, bf16[16,24,256]{2,1,0:T(8,128)(2,1)S(1)}, u32[]{:S(2)}, u32[]{:S(2)}) collective-permute-start(bf16[16,24,256]{2,1,0:T(8,128)(2,1)S(1)} %shard_map.106), channel_id=1, source_target_pairs={{0,1},{1,0},{2,3},{3,2},{4,5},{5,4},{6,7},{7,6},{8,9},{9,8},{10,11... | collective-permute-start | bytes 589832 | tf_op jit(solution)/shard_map/ppermute | solution.py:24

commit v9 on v8

--- a/solution.py
+++ b/solution.py
@@ -106,7 +106,7 @@
         for top in range(2)
         for core in range(2)
     ]
-    value = signed_join(value, across(value, 1), second)
+    value = signed_join(value, across(value.astype(jnp.bfloat16), 1), second)
     value = value.astype(jnp.bfloat16)
     value = signed_join(value, across(value, devices // 2), upper).astype(jnp.bfloat16)
     copies = jnp.broadcast_to(value[None], (middle, *value.shape))

time: 106 us -> 106 us (level)
  no operation moved by 1% of the time
where the time goes in v9:
time: 106 us; the launch traced here: 105 us
  blocking collectives  81.6 us (77%)
  waiting for transfers between devices  6.9 us (7%)
  Pallas kernels  6.81 us (6%)
  matrix products  4.76 us (4%)
  starting transfers between devices  2.46 us (2%)
  other arithmetic  2.13 us (2%)
    all_to_all x3, blocking collectives, scattered_joined(): lax.all_to_all(joined.astype(jnp.bfloat16), 'tensor', 0, 0, tiled=True, a...  39.1 us
    all_to_all x2, blocking collectives, gathered_same_core(): lax.all_to_all(copies, 'tensor', 0, 0, tiled=True, axis_index_groups=same...  23 us
    all_to_all x1, blocking collectives, gathered_at_once(): return lax.all_to_all(copies, 'tensor', 0, 0, tiled=True)  10.8 us
    all_to_all x1, blocking collectives, signed_sum(): lax.all_to_all(copies, 'tensor', 0, 0, tiled=True, axis_index_groups=groups)  8.78 us
    ppermute x7, waiting for transfers between devices, across(): return lax.ppermute(value, 'tensor', pairs)  6.9 us
    pallas_call x2, Pallas kernels, attended_pair(): pl.pallas_call(attend_kernel, out_shape=jax.ShapeDtypeStruct((H // 2, row...  2.9 us
    ppermute x7, starting transfers between devices, across(): return lax.ppermute(value, 'tensor', pairs)  2.46 us
    pallas_call x1, Pallas kernels, projected_pieces(): pl.pallas_call(project_kernel, out_shape=jax.ShapeDtypeStruct((2, devices...  2.24 us
  transfers between devices with their start and end apart: 7, of which 5 were waited for; matrix products, arithmetic and copies ran while one was open for 1% of the time, Pallas kernels for 3%

profile of v9, /device:TPU:0, one launch (start us, length us, event | category | flops | bytes accessed | tf_op | source)
XLA Modules:
  0.0 105.5 jit_solution(1233927301870480751)
XLA Ops:
  0.0 0.0 copy-start
  0.0 2.2 %shard_map.100 = bf16[2,16,32,128]{3,2,1,0:T(8,128)(2,1)S(1)} custom-call(s32[1]{0:T(128)S(6)} %select_n.50.core_ref.pair_ref.part_ref, bf16[24,256]{1,0:T(8,128)(2,1)} %hidden_source.1, bf16[256,5120]{1,0:T(8,128)(2,1)} %source_ref.1), custom_call_target="tpu_custom_call" | custom-call | flops 62914560 | bytes 2621440 | tf_op jit(solution)/shard_map/pallas_call | solution.py:205
  2.3 0.5 collective-permute-start
  2.8 0.7 convert_element_type.99
  3.5 0.1 fusion.8
  3.6 0.1 pad_maximum_fusion
  3.7 0.1 collective-permute-done
  3.8 0.1 broadcast_in_dim.10.lengths_ref
  3.9 0.0 slice-start.2
  3.9 16.1 %all_to_all.35.parts_ref = bf16[16,32,128]{2,1,0:T(8,128)(2,1)S(1)} all-to-all(bf16[16,32,128]{2,1,0:T(8,128)(2,1)S(1)} %fusion.1), channel_id=1, replica_groups={{0,2,4,6,8,10,12,14,16,18,20,22,24,26,28,30},{1,3,5,7,9,11,13,15,17,19,..., dimensions={0} | all-to-all | bytes 262144 | tf_op jit(solution)/shard_map/all_to_all | solution.py:64
  20.0 11.0 %all_to_all.36 = bf16[16,32,128]{2,1,0:T(8,128)(2,1)S(1)} all-to-all(bf16[16,32,128]{2,1,0:T(8,128)(2,1)S(1)} %broadcast_in_dim.11), channel_id=1, replica_groups={{0,2,4,6,8,10,12,14,16,18,20,22,24,26,28,30},{1,3,5,7,9,11,13,15,17,19,..., dimensions={0} | all-to-all | bytes 262144 | tf_op jit(solution)/shard_map/all_to_all | solution.py:79
  31.0 0.1 collective-permute-start.1
  31.1 0.0 slice-done.2
  31.1 0.0 slice-done.3
  31.1 0.0 copy-done.1
  31.2 1.4 %shard_map.103 = bf16[16,32,128]{2,1,0:T(8,128)(2,1)S(1)} custom-call(s32[1]{0:T(128)} %bitcast.device_ref, s32[1]{0:T(128)S(6)} %sub.19.pair_ref.part_ref, f32[24,128]{1,0:T(8,128)S(1)} %broadcast_in_dim.10.lengths_ref, bf16[21,24,128]{2,1,0:T(8,128)(2,1)S(1)} %bitcast.38, f32[24,128]{1,0:T(8,128)S(1)} %get-tuple-element.19.cosine_ref, ...), custom_call_target="tpu_custom_call" | custom-call | flops 50331648 | bytes 6291456 | tf_op jit(solution)/shard_map/pallas_call | solution.py:315
  32.6 0.6 collective-permute-start.2
  33.2 0.0 collective-permute-done.1
  33.2 0.0 slice-start.4
  33.2 0.0 copy-start.3
  33.2 0.0 slice-start.5
  33.2 1.5 %shard_map.102 = bf16[16,32,128]{2,1,0:T(8,128)(2,1)S(1)} custom-call(s32[1]{0:T(128)} %bitcast.device_ref, s32[1]{0:T(128)S(6)} %select_n.50.core_ref.pair_ref.part_ref, f32[24,128]{1,0:T(8,128)S(1)} %broadcast_in_dim.10.lengths_ref, bf16[21,24,128]{2,1,0:T(8,128)(2,1)S(1)} %bitcast.39, f32[24,128]{1,0:T(8,128)S(1)} %get-tuple-element.19.cosine_ref, ...), custom_call_target="tpu_custom_call" | custom-call | flops 50331648 | bytes 6291456 | tf_op jit(solution)/shard_map/pallas_call | solution.py:315
  34.7 0.0 collective-permute-done.2
  34.7 0.0 slice-start.6
  34.7 10.9 %all_to_all.37 = bf16[16,32,128]{2,1,0:T(8,128)(2,1)S(1)} all-to-all(bf16[16,32,128]{2,1,0:T(8,128)(2,1)S(1)} %add_convert_fusion.1), channel_id=1, replica_groups={{0,2,4,6,8,10,12,14,16,18,20,22,24,26,28,30},{1,3,5,7,9,11,13,15,17,19,..., dimensions={0} | all-to-all | bytes 262144 | tf_op jit(solution)/shard_map/all_to_all | solution.py:64
  45.6 0.1 shard_map.104
  45.8 10.8 %all_to_all.38 = bf16[32,24,128]{2,1,0:T(8,128)(2,1)S(1)} all-to-all(bf16[32,24,128]{2,1,0:T(8,128)(2,1)S(1)} %broadcast_in_dim.12), channel_id=1, replica_groups=mesh['groups'=1,'tensor'=32] {'tensor'}, dimensions={0} | all-to-all | bytes 393216 | tf_op jit(solution)/shard_map/all_to_all | solution.py:74
  56.6 0.1 copy.16
  56.6 0.0 copy-done
  56.6 0.0 copy-done.3
  56.6 0.4 fusion
  57.1 12.0 %all_to_all.39 = bf16[16,24,256]{2,1,0:T(8,128)(2,1)S(1)} all-to-all(bf16[16,24,256]{2,1,0:T(8,128)(2,1)S(1)} %broadcast_in_dim.13), channel_id=1, replica_groups={{0,2,4,6,8,10,12,14,16,18,20,22,24,26,28,30},{1,3,5,7,9,11,13,15,17,19,..., dimensions={0} | all-to-all | bytes 393216 | tf_op jit(solution)/shard_map/all_to_all | solution.py:79
  69.1 0.0 collective-permute-start.3
  69.1 1.4 %collective-permute-done.3 = bf16[16,24,256]{2,1,0:T(8,128)(2,1)S(1)} collective-permute-done((bf16[16,24,256]{2,1,0:T(8,128)(2,1)S(1)}, bf16[16,24,256]{2,1,0:T(8,128)(2,1)S(1)}, u32[]{:S(2)}, u32[]{:S(2)}) %collective-permute-start.3) | collective-permute-done | bytes 196640 | tf_op jit(solution)/shard_map/ppermute | solution.py:24
  70.5 0.2 multiply_reduce_fusion
  70.8 0.1 maximum_convert_fusion
  70.8 0.0 slice-start.7
  70.8 0.1 copy.19
  70.9 0.0 slice-done.4
  70.9 0.0 slice-done.5
  70.9 0.0 copy-start.2
  71.0 0.0 slice-start
  71.0 2.0 %fusion.13 = f32[24,448]{1,0:T(8,128)S(1)} fusion(bf16[8192,448]{0,1:T(8,128)(2,1)S(1)} %bitcast.41, f32[24,8192]{1,0:T(8,128)S(1)} %bitcast.44, f32[24]{0:T(128)S(1)} %add_rsqrt_fusion), kind=kOutput, calls=%fused_computation.42 | convolution fusion | flops 176553984 | bytes 8169568 | tf_op jit(solution)/shard_map/dot_general | solution.py:449
  73.0 0.0 slice-done.6
  73.0 0.0 slice-done.7
  73.0 0.0 slice-start.1
  73.0 2.0 %convolution_multiply_fusion = f32[24,448]{1,0:T(8,128)S(1)} fusion(bf16[8192,448]{0,1:T(8,128)(2,1)S(1)} %bitcast.43, f32[24,448]{1,0:T(8,128)S(1)} %fusion.13, f32[24,8192]{1,0:T(8,128)S(1)} %bitcast.45, f32[24]{0:T(128)S(1)} %add_rsqrt_fusion), kind=kOutput, calls=%fused_computation | convolution fusion | flops 176607744 | bytes 8212576 | tf_op jit(solution)/shard_map/dot_general | solution.py:450
  75.0 0.0 copy-done.2
  75.1 0.3 fusion.14
  75.4 0.2 collective-permute-start.4
  75.6 1.1 %collective-permute-done.4 = bf16[24,448]{1,0:T(8,128)(2,1)S(1)} collective-permute-done((bf16[24,448]{1,0:T(8,128)(2,1)S(1)}, bf16[24,448]{1,0:T(8,128)(2,1)S(1)}, u32[]{:S(2)}, u32[]{:S(2)}) %collective-permute-start.4) | collective-permute-done | bytes 21536 | tf_op jit(solution)/shard_map/ppermute | solution.py:24
  76.7 1.1 %collective-permute-start.5 = (bf16[24,448]{1,0:T(8,128)(2,1)S(1)}, bf16[24,448]{1,0:T(8,128)(2,1)S(1)}, u32[]{:S(2)}, u32[]{:S(2)}) collective-permute-start(bf16[24,448]{1,0:T(8,128)(2,1)S(1)} %fusion.5), channel_id=1, source_target_pairs={{0,16},{1,17},{2,18},{3,19},{4,20},{5,21},{6,22},{7,23},{8,24},{9,... | collective-permute-start | bytes 64520 | tf_op jit(solution)/shard_map/ppermute | solution.py:24
  77.8 3.7 %collective-permute-done.5 = bf16[24,448]{1,0:T(8,128)(2,1)S(1)} collective-permute-done((bf16[24,448]{1,0:T(8,128)(2,1)S(1)}, bf16[24,448]{1,0:T(8,128)(2,1)S(1)}, u32[]{:S(2)}, u32[]{:S(2)}) %collective-permute-start.5) | collective-permute-done | bytes 21536 | tf_op jit(solution)/shard_map/ppermute | solution.py:24
  81.5 8.8 %all_to_all.40 = bf16[8,24,448]{2,1,0:T(8,128)(2,1)S(1)} all-to-all(bf16[8,24,448]{2,1,0:T(8,128)(2,1)S(1)} %broadcast_in_dim.14), channel_id=1, replica_groups={{0,2,4,6,8,10,12,14},{1,3,5,7,9,11,13,15},{16,18,20,22,24,26,28,30},{17..., dimensions={0} | all-to-all | bytes 344064 | tf_op jit(solution)/shard_map/all_to_all | solution.py:113
  90.3 0.1 multiply_reduce_fusion.1
  90.4 0.0 slice-done
  90.4 0.0 slice-done.1
  90.4 0.8 shard_map.106
  91.2 0.0 collective-permute-start.6
  91.2 0.8 shard_map.105
  92.0 0.7 collective-permute-done.6
  92.7 0.1 add_convert_fusion
  92.7 12.1 %all_to_all.41 = bf16[16,24,256]{2,1,0:T(8,128)(2,1)S(1)} all-to-all(bf16[16,24,256]{2,1,0:T(8,128)(2,1)S(1)} %add_convert_fusion), channel_id=1, replica_groups={{0,2,4,6,8,10,12,14,16,18,20,22,24,26,28,30},{1,3,5,7,9,11,13,15,17,19,..., dimensions={0} | all-to-all | bytes 393216 | tf_op jit(solution)/shard_map/all_to_all | solution.py:64
  104.9 0.6 add_convert_fusion.2
  (25 shorter events, 0.4 us)
Async XLA Ops:
  0.0 56.6 %copy-start = (bf16[4096,256]{1,0:T(8,128)(2,1)S(1)}, bf16[4096,256]{1,0:T(8,128)(2,1)}, u32[]{:S(2)}) copy-start(bf16[4096,256]{1,0:T(8,128)(2,1)} %param.15) | copy-start | bytes 6291460
  2.3 1.5 %collective-permute-start = (bf16[16,32,128]{2,1,0:T(8,128)(2,1)S(1)}, bf16[16,32,128]{2,1,0:T(8,128)(2,1)S(1)}, u32[]{:S(2)}, u32[]{:S(2)}) collective-permute-start(bf16[16,32,128]{2,1,0:T(8,128)(2,1)S(1)} %slice_bitcast_fusion), channel_id=1, source_target_pairs={{0,1},{1,0},{2,3},{3,2},{4,5},{5,4},{6,7},{7,6},{8,9},{9,8},{10,11... | collective-permute-start | bytes 393224 | tf_op jit(solution)/shard_map/ppermute | solution.py:24
  3.9 27.2 %slice-start.2 = ((s8[6291456]{0:T(1024)(128)(4,1)}), s8[4194304]{0:T(1024)(128)(4,1)S(1)}, s32[]{:S(2)}) async-start(s8[6291456]{0:T(1024)(128)(4,1)} %bitcast.36), calls=%async_computation.9 | async-start | bytes 8388608
  20.0 11.1 %slice-start.3 = ((s8[6291456]{0:T(1024)(128)(4,1)}), s8[2097152]{0:T(1024)(128)(4,1)S(1)}, s32[]{:S(2)}) async-start(s8[6291456]{0:T(1024)(128)(4,1)} %bitcast.36), calls=%async_computation.10 | async-start | bytes 4194304
  20.0 11.1 %copy-start.1 = (bf16[24,256,512]{2,1,0:T(8,128)(2,1)S(1)}, bf16[24,256,512]{2,1,0:T(8,128)(2,1)}, u32[]{:S(2)}) copy-start(bf16[24,256,512]{2,1,0:T(8,128)(2,1)} %values_ref.3) | copy-start | bytes 18874372
  31.0 2.1 %collective-permute-start.1 = (bf16[16,32,128]{2,1,0:T(8,128)(2,1)S(1)}, bf16[16,32,128]{2,1,0:T(8,128)(2,1)S(1)}, u32[]{:S(2)}, u32[]{:S(2)}) collective-permute-start(bf16[16,32,128]{2,1,0:T(8,128)(2,1)S(1)} %all_to_all.36), channel_id=1, source_target_pairs={{0,1},{1,0},{2,3},{3,2},{4,5},{5,4},{6,7},{7,6},{8,9},{9,8},{10,11... | collective-permute-start | bytes 393224 | tf_op jit(solution)/shard_map/ppermute | solution.py:24
  32.6 2.1 %collective-permute-start.2 = (bf16[16,32,128]{2,1,0:T(8,128)(2,1)S(1)}, bf16[16,32,128]{2,1,0:T(8,128)(2,1)S(1)}, u32[]{:S(2)}, u32[]{:S(2)}) collective-permute-start(bf16[16,32,128]{2,1,0:T(8,128)(2,1)S(1)} %shard_map.103), channel_id=1, source_target_pairs={{0,1},{1,0},{2,3},{3,2},{4,5},{5,4},{6,7},{7,6},{8,9},{9,8},{10,11... | collective-permute-start | bytes 393224 | tf_op jit(solution)/shard_map/ppermute | solution.py:24
  33.2 37.7 %slice-start.4 = ((s8[7340032]{0:T(1024)(128)(4,1)}), s8[4194304]{0:T(1024)(128)(4,1)S(1)}, s32[]{:S(2)}) async-start(s8[7340032]{0:T(1024)(128)(4,1)} %bitcast.40), calls=%async_computation.11 | async-start | bytes 8388608
  33.2 23.4 %copy-start.3 = (bf16[24,256]{1,0:T(8,128)(2,1)S(1)}, bf16[24,256]{1,0:T(8,128)(2,1)}, u32[]{:S(2)}) copy-start(bf16[24,256]{1,0:T(8,128)(2,1)} %hidden_source.1) | copy-start | bytes 36868
  33.2 37.7 %slice-start.5 = ((s8[7340032]{0:T(1024)(128)(4,1)}), s8[3145728]{0:T(1024)(128)(4,1)S(1)}, s32[]{:S(2)}) async-start(s8[7340032]{0:T(1024)(128)(4,1)} %bitcast.40), calls=%async_computation.12 | async-start | bytes 6291456
  34.7 38.2 %slice-start.6 = ((s8[7340032]{0:T(1024)(128)(4,1)}), s8[4194304]{0:T(1024)(128)(4,1)S(1)}, s32[]{:S(2)}) async-start(s8[7340032]{0:T(1024)(128)(4,1)} %bitcast.42), calls=%async_computation.13 | async-start | bytes 8388608
  69.1 1.4 %collective-permute-start.3 = (bf16[16,24,256]{2,1,0:T(8,128)(2,1)S(1)}, bf16[16,24,256]{2,1,0:T(8,128)(2,1)S(1)}, u32[]{:S(2)}, u32[]{:S(2)}) collective-permute-start(bf16[16,24,256]{2,1,0:T(8,128)(2,1)S(1)} %all_to_all.39), channel_id=1, source_target_pairs={{0,1},{1,0},{2,3},{3,2},{4,5},{5,4},{6,7},{7,6},{8,9},{9,8},{10,11... | collective-permute-start | bytes 589832 | tf_op jit(solution)/shard_map/ppermute | solution.py:24
  70.8 2.2 %slice-start.7 = ((s8[7340032]{0:T(1024)(128)(4,1)}), s8[3145728]{0:T(1024)(128)(4,1)S(1)}, s32[]{:S(2)}) async-start(s8[7340032]{0:T(1024)(128)(4,1)} %bitcast.42), calls=%async_computation.14 | async-start | bytes 6291456
  70.9 4.1 %copy-start.2 = (f32[448,448]{1,0:T(8,128)S(1)}, f32[448,448]{1,0:T(8,128)}, u32[]{:S(2)}) copy-start(f32[448,448]{1,0:T(8,128)} %constant.93.clone) | copy-start | bytes 2408452
  71.0 19.4 %slice-start = ((s8[7340032]{0:T(1024)(128)(4,1)}), s8[4194304]{0:T(1024)(128)(4,1)S(1)}, s32[]{:S(2)}) async-start(s8[7340032]{0:T(1024)(128)(4,1)} %bitcast.34), calls=%async_computation.7 | async-start | bytes 8388608
  73.0 17.4 %slice-start.1 = ((s8[7340032]{0:T(1024)(128)(4,1)}), s8[3145728]{0:T(1024)(128)(4,1)S(1)}, s32[]{:S(2)}) async-start(s8[7340032]{0:T(1024)(128)(4,1)} %bitcast.34), calls=%async_computation.8 | async-start | bytes 6291456
  75.4 1.2 %collective-permute-start.4 = (bf16[24,448]{1,0:T(8,128)(2,1)S(1)}, bf16[24,448]{1,0:T(8,128)(2,1)S(1)}, u32[]{:S(2)}, u32[]{:S(2)}) collective-permute-start(bf16[24,448]{1,0:T(8,128)(2,1)S(1)} %get-tuple-element.30), channel_id=1, source_target_pairs={{0,1},{1,0},{2,3},{3,2},{4,5},{5,4},{6,7},{7,6},{8,9},{9,8},{10,11... | collective-permute-start | bytes 64520 | tf_op jit(solution)/shard_map/ppermute | solution.py:24
  76.7 4.8 %collective-permute-start.5 = (bf16[24,448]{1,0:T(8,128)(2,1)S(1)}, bf16[24,448]{1,0:T(8,128)(2,1)S(1)}, u32[]{:S(2)}, u32[]{:S(2)}) collective-permute-start(bf16[24,448]{1,0:T(8,128)(2,1)S(1)} %fusion.5), channel_id=1, source_target_pairs={{0,16},{1,17},{2,18},{3,19},{4,20},{5,21},{6,22},{7,23},{8,24},{9,... | collective-permute-start | bytes 64520 | tf_op jit(solution)/shard_map/ppermute | solution.py:24
  91.2 1.5 %collective-permute-start.6 = (bf16[16,24,256]{2,1,0:T(8,128)(2,1)S(1)}, bf16[16,24,256]{2,1,0:T(8,128)(2,1)S(1)}, u32[]{:S(2)}, u32[]{:S(2)}) collective-permute-start(bf16[16,24,256]{2,1,0:T(8,128)(2,1)S(1)} %shard_map.106), channel_id=1, source_target_pairs={{0,1},{1,0},{2,3},{3,2},{4,5},{5,4},{6,7},{7,6},{8,9},{9,8},{10,11... | collective-permute-start | bytes 589832 | tf_op jit(solution)/shard_map/ppermute | solution.py:24
